TPU v7x, 128 devices: a whole 4x4x4 slice. The times are simulated.
128 devices in a mesh: oy: 8 (over x, core), ox: 16 (over y, z).
Axes of the slice: x: 4, y: 4, z: 4, core: 2. Of those that a mesh axis runs over, the one named last changes fastest.
Arguments:
- atm_flux: bfloat16 [8192, 4, 128], P(('oy', 'ox')), may hold values from -6 to 6
- remap_weights: bfloat16 [49152, 128, 128], P(('oy', 'ox')), may hold values from -0.5 to 0.5
- link_source: int32 [49152], P(('oy', 'ox')), may hold values from 0 to 63
- link_owner: int32 [49152, 1], P(('oy', 'ox')), may hold values from 0 to 127; in each aligned block of 384 rows (0 to 383, 384 to 767, ...) at most 6 rows name the same one
- link_block: int32 [49152], P(('oy', 'ox')), may hold values from 0 to 63
- ocean_mask: int32 [256, 4096], P('oy', 'ox'), may hold values 0 or 1
- level_count: int32 [256, 4096], P('oy', 'ox'), may hold values from 1 to 20
- tracers: float32 [4, 20, 256, 4096], P(None, None, 'oy', 'ox'), may hold values from -6 to 6
- diffusivity: float32 [20, 256, 4096], P(None, 'oy', 'ox'), may hold values from 0.05 to 5
- viscosity: float32 [20, 256, 4096], P(None, 'oy', 'ox'), may hold values from 0.003 to 0.025
Outputs:
- tracers_out: float32 [4, 20, 256, 4096], P(None, None, 'oy', 'ox')
- ocean_flux: float32 [4, 256, 4096], P(None, 'oy', 'ox')
Inputs may be any that keep to these rules, and one draw needn't show every extreme that they name: `link_owner`: among the 384 links of one device no tile is named more than 6 times, a bound that some block reaches.
All inputs are finite; a program needn't handle non-finite values. No bound on the sum of `ocean_mask` on one device may be relied on, other than what follows from the above.
Results may differ from a plain program's by a relative error of at most 0.0003.
Values sent between devices are 32-bit elements; how exact they have to be, the bound alone decides.
No kernel may reach another device: no remote copies, remote signals or barrier semaphores. Data moves between devices by JAX's collectives and lax.ppermute only.
A program may use at most 128 MiB of HBM per device.

v0:
```python
import jax
import jax.numpy as jnp
from jax import lax
from jax.sharding import PartitionSpec as P

SUBSTEPS = 2


def with_halo(array, sides, width, wrap):
    for axis, dim in sides:
        devices, length = (lax.axis_size(axis), array.shape[dim])
        up = [(i, (i + 1) % devices) for i in range(devices if wrap else devices - 1)]
        down = [(j, i) for i, j in up]
        last = lax.slice_in_dim(array, length - width, length, axis=dim)
        initial = lax.slice_in_dim(array, 0, width, axis=dim)
        before = lax.ppermute(last, axis, up)
        after = lax.ppermute(initial, axis, down)
        array = jnp.concatenate([before, array, after], axis=dim)
    return array


def laplace(padded):
    return (
        padded[..., :-2, 1:-1]
        + padded[..., 2:, 1:-1]
        + padded[..., 1:-1, :-2]
        + padded[..., 1:-1, 2:]
        - 4.0 * padded[..., 1:-1, 1:-1]
    )


def mix_columns(forced, diffusivity, levels):
    count = forced.shape[1]
    nothing = jnp.zeros(levels.shape, jnp.float32)
    couplings = [
        jnp.where(level + 1 < levels, diffusivity[level], nothing) for level in range(count - 1)
    ]
    couplings = couplings + [nothing]
    sweep_ratio = nothing
    sweep_value = jnp.zeros(forced[:, 0].shape, jnp.float32)
    ratio_list = []
    value_list = []
    for level in range(count):
        upper_link = couplings[level - 1] if level > 0 else nothing
        lower_link = couplings[level]
        pivot_value = 1.0 + upper_link + lower_link - -upper_link * sweep_ratio
        sweep_ratio = -lower_link / pivot_value
        sweep_value = (forced[:, level] + upper_link * sweep_value) / pivot_value
        ratio_list.append(sweep_ratio)
        value_list.append(sweep_value)
    result_list = [value_list[count - 1]]
    for level in range(count - 2, -1, -1):
        result_list.append(value_list[level] - ratio_list[level] * result_list[-1])
    result_list = result_list[::-1]
    return jnp.stack(result_list, axis=1)


def narrow_extend(field):
    widened = with_halo(field, (("ox", 3),), 1, True)
    return with_halo(widened, (("oy", 2),), 1, False)


def body(
    atm_flux,
    remap_weights,
    link_source,
    link_owner,
    link_block,
    ocean_mask,
    level_count,
    tracers,
    diffusivity,
    viscosity,
):
    count_oy = lax.axis_size("oy")
    count_ox = lax.axis_size("ox")
    devices = count_oy * count_ox
    link_dev = link_source.shape[0]
    fields = atm_flux.shape[1]
    block_len = atm_flux.shape[2]
    capacity = 2 * ((link_dev + devices - 1) // devices)
    lat_cells, lon_cells = ocean_mask.shape
    ocean_blocks = lat_cells * lon_cells // block_len
    picked = atm_flux[link_source]
    contrib = lax.dot_general(
        picked, remap_weights, (((2,), (1,)), ((0,), (0,))), preferred_element_type=jnp.float32
    ).reshape(link_dev, fields * block_len)
    owner_tile = link_owner[:, 0]
    owner_onehot = (owner_tile[:, None] == jnp.arange(devices, dtype=jnp.int32)[None, :]).astype(
        jnp.int32
    )
    slot_rank = jnp.sum(owner_onehot * (jnp.cumsum(owner_onehot, axis=0) - 1), axis=1)
    slot_index = owner_tile * capacity + slot_rank
    payload = (
        jnp.zeros((devices * capacity, fields * block_len), jnp.float32).at[slot_index].set(contrib)
    )
    targets = jnp.full((devices * capacity,), -1, jnp.int32).at[slot_index].set(link_block)
    arrived, arrived_ids = (
        lax.all_to_all(
            payload.reshape(devices, capacity, fields * block_len),
            ("oy", "ox"),
            split_axis=0,
            concat_axis=0,
            tiled=True,
        ),
        lax.all_to_all(
            targets.reshape(devices, capacity),
            ("oy", "ox"),
            split_axis=0,
            concat_axis=0,
            tiled=True,
        ),
    )
    arrived = arrived.reshape(devices * capacity, fields * block_len)
    arrived_ids = arrived_ids.reshape(devices * capacity)
    block_onehot = (
        jnp.arange(ocean_blocks, dtype=jnp.int32)[:, None] == arrived_ids[None, :]
    ).astype(jnp.float32)
    summed = jnp.dot(
        block_onehot, arrived, precision=lax.Precision.HIGHEST, preferred_element_type=jnp.float32
    ).reshape(ocean_blocks, fields, block_len)
    surface = jnp.transpose(summed, (1, 0, 2)).reshape(fields, lat_cells, lon_cells)
    ocean_flux = surface * ocean_mask.astype(jnp.float32)[None]
    count_levels = tracers.shape[1]
    levels = level_count * ocean_mask
    active = jnp.where(
        jnp.arange(count_levels, dtype=jnp.int32)[:, None, None] < levels[None], 1.0, 0.0
    ).astype(jnp.float32)
    forced = tracers.at[:, 0].add(ocean_flux)
    current = mix_columns(forced, diffusivity, levels)
    weight = viscosity * active
    for substep in range(SUBSTEPS):
        first_pass = laplace(narrow_extend(current))
        second = laplace(narrow_extend(weight[None] * first_pass))
        current = current - active[None] * second
    return (current, ocean_flux)


def solution(mesh):
    placed = (
        P(("oy", "ox"), None, None),
        P(("oy", "ox"), None, None),
        P(("oy", "ox")),
        P(("oy", "ox"), None),
        P(("oy", "ox")),
        P("oy", "ox"),
        P("oy", "ox"),
        P(None, None, "oy", "ox"),
        P(None, "oy", "ox"),
        P(None, "oy", "ox"),
    )
    return jax.shard_map(
        body,
        mesh=mesh,
        in_specs=placed,
        out_specs=(P(None, None, "oy", "ox"), P(None, "oy", "ox")),
        check_vma=False,
    )
```

profile of v0, /device:TPU:1, one launch (start us, length us, event | category | flops | bytes accessed | tf_op | source)
XLA Modules:
  0.0 227.9 jit_solution(16354020898226829908)
XLA Ops:
  2.8 3.1 %scatter_custom_fusion = s32[768]{0:T(1024)S(1)} fusion(s32[384]{0:T(512)S(1)} %fusion.39, s32[384]{0:T(512)} %param.16, s32[]{:T(128)} %constant.29.clone.1), kind=kCustom, calls=%fused_computation.211 | custom fusion | bytes 3584 | tf_op jit(solution)/shard_map/scatter | solution.py:97
  6.6 12.0 %all-to-all-start = ((s32[128,1,6]{2,1,0:T(1,128)}), s32[128,1,6]{2,1,0:T(1,128)}, u32[]{:S(2)}, u32[]{:S(2)}) async-start(s32[128,1,6]{2,1,0:T(1,128)} %bitcast.3), calls=%async_computation | async-start | bytes 131072 | tf_op jit(solution)/shard_map/all_to_all | solution.py:106
  30.8 2.0 gather_fusion
  32.8 6.3 %fusion.44 = f32[384,4,128]{2,1,0:T(4,128)S(1)} fusion(bf16[384,4,128]{2,1,0:T(4,128)(2,1)S(1)} %gather_fusion, bf16[384,128,128]{2,1,0:T(8,128)(2,1)} %param.13), kind=kOutput, calls=%fused_computation.218 | convolution fusion | flops 50331648 | bytes 13762560 | tf_op jit(solution)/shard_map/dot_general | solution.py:85
  40.0 2.3 scatter_custom_fusion.1
  43.9 9.8 %all-to-all-start.1 = ((f32[128,6,512]{2,1,0:T(8,128)}), f32[128,6,512]{2,1,0:T(8,128)S(1)}, u32[]{:S(2)}, u32[]{:S(2)}) async-start(f32[128,6,512]{2,1,0:T(8,128)} %reshape.155), calls=%async_computation.1 | async-start | bytes 4194304 | tf_op jit(solution)/shard_map/all_to_all | solution.py:99
  60.6 22.5 %all-to-all-done.1 = f32[128,6,512]{2,1,0:T(8,128)S(1)} async-done(((f32[128,6,512]{2,1,0:T(8,128)}), f32[128,6,512]{2,1,0:T(8,128)S(1)}, u32[]{:S(2)}, u32[]{:S(2)}) %all-to-all-start.1) | async-done | bytes 1572896 | tf_op jit(solution)/shard_map/all_to_all | solution.py:99
  84.7 2.0 copy.253
  88.0 2.5 %subtract_dynamic-update-slice_fusion = (f32[4,20,32,256]{3,2,1,0:T(8,128)S(1)}, f32[4,1,32,256]{3,2,1,0:T(8,128)S(1)}, f32[4,1,32,256]{3,2,1,0:T(8,128)S(1)}, f...) fusion(f32[32,256]{1,0:T(8,128)S(1)} %copy-done.56, ...), kind=kLoop, calls=%fused_computation.89 | loop fusion | flops 3211263 | bytes 7176192
  97.5 4.1 %collective-permute-start.1 = (f32[4,20,32,1]{2,1,3,0:T(8,128)}, f32[4,20,32,1]{2,1,3,0:T(8,128)S(1)}, u32[]{:S(2)}, u32[]{:S(2)}) collective-permute-start(f32[4,20,32,1]{2,1,3,0:T(8,128)} %copy.288), channel_id=1, source_target_pairs={{1,0},{2,1},{3,2},{4,3},{5,4},{6,5},{7,6},{8,7},{9,8},{10,9},{11,1... | collective-permute-start | bytes 30728 | tf_op jit(solution)/shard_map/ppermute | solution.py:17
  101.6 3.3 %copy.273 = f32[4,20,32,256]{3,1,2,0:T(8,128)S(1)} copy(f32[4,20,32,256]{3,2,1,0:T(8,128)} %copy-done.7) | data formatting | bytes 5242880 | tf_op jit(solution)/shard_map/stack | solution.py:55
  104.9 2.1 copy.259
  107.0 1.8 copy.261
  110.1 4.5 %collective-permute-start.2 = (f32[4,20,1,258]{3,1,2,0:T(8,128)S(1)}, f32[4,20,1,258]{3,1,2,0:T(8,128)S(1)}, u32[]{:S(2)}, u32[]{:S(2)}) collective-permute-start(f32[4,20,1,258]{3,1,2,0:T(8,128)S(1)} %get-tuple-element.92), channel_id=1, source_target_pairs={{0,16},{16,32},{32,48},{48,64},{64,80},{80,96},{96,112},{1,17},{17... | collective-permute-start | bytes 247688 | tf_op jit(solution)/shard_map/ppermute | solution.py:16
  114.6 1.9 collective-permute-start.3
  118.0 3.1 %collective-permute-done.3 = f32[4,20,1,258]{3,1,2,0:T(8,128)S(1)} collective-permute-done((f32[4,20,1,258]{3,1,2,0:T(8,128)S(1)}, f32[4,20,1,258]{3,1,2,0:T(8,128)S(1)}, u32[]{:S(2)}, u32[]{:S(2)}) %collective-permute-start.3) | collective-permute-done | bytes 82592 | tf_op jit(solution)/shard_map/ppermute | solution.py:17
  121.1 4.0 %fusion.19 = f32[4,20,32,256]{3,1,2,0:T(8,128)S(1)} fusion(f32[4,20,32,1]{3,1,2,0:T(8,128)S(1)} %copy-done.11, f32[4,20,32,256]{3,1,2,0:T(8,128)S(1)} %copy-done.6, f32[4,20,32,1]{3,1,2,0:T(8,128)S(1)} %copy-done.9, f32[4,20,1,258]{3,1,2,0:T(8,128)S(1)} %collective-permute-done.3, f32[4,20,1,258]{3,1,2,0:T(8,128)S(1)} %collective-permute-done.2, ...), kind=kLoop, calls=%fused_computation.47 | loop fusion | flops 9175040 | bytes 6083840 | tf_op jit(solution)/shard_map/mul | solution.py:134
  125.1 2.5 %fusion.42 = (f32[4,20,32,1]{3,1,2,0:T(8,128)}, f32[4,20,32,1]{3,1,2,0:T(8,128)}) fusion(f32[4,20,32,256]{3,1,2,0:T(8,128)S(1)} %fusion.19), kind=kLoop, calls=%fused_computation.216 | loop fusion | bytes 40960 | tf_op jit(solution)/shard_map/slice | solution.py:14
  127.6 2.0 copy.267
  129.7 2.0 copy.268
  131.7 4.8 %collective-permute-start.5 = (f32[4,20,32,1]{2,1,3,0:T(8,128)S(1)}, f32[4,20,32,1]{2,1,3,0:T(8,128)}, u32[]{:S(2)}, u32[]{:S(2)}) collective-permute-start(f32[4,20,32,1]{2,1,3,0:T(8,128)S(1)} %copy.268), channel_id=1, source_target_pairs={{1,0},{2,1},{3,2},{4,3},{5,4},{6,5},{7,6},{8,7},{9,8},{10,9},{11,1... | collective-permute-start | bytes 30728 | tf_op jit(solution)/shard_map/ppermute | solution.py:17
  136.5 1.8 copy.269
  138.4 2.6 %copy.270 = f32[4,20,32,1]{3,1,2,0:T(8,128)} copy(f32[4,20,32,1]{2,1,3,0:T(8,128)} %collective-permute-done.5) | data formatting | bytes 20480 | tf_op jit(solution)/shard_map/ppermute | solution.py:17
  142.2 2.6 %collective-permute-start.6 = (f32[4,20,1,258]{3,1,2,0:T(8,128)S(1)}, f32[4,20,1,258]{3,1,2,0:T(8,128)S(1)}, u32[]{:S(2)}, u32[]{:S(2)}) collective-permute-start(f32[4,20,1,258]{3,1,2,0:T(8,128)S(1)} %get-tuple-element.90), channel_id=1, source_target_pairs={{0,16},{16,32},{32,48},{48,64},{64,80},{80,96},{96,112},{1,17},{17... | collective-permute-start | bytes 247688 | tf_op jit(solution)/shard_map/ppermute | solution.py:16
  144.8 2.0 collective-permute-start.7
  147.3 4.0 %collective-permute-done.7 = f32[4,20,1,258]{3,1,2,0:T(8,128)S(1)} collective-permute-done((f32[4,20,1,258]{3,1,2,0:T(8,128)S(1)}, f32[4,20,1,258]{3,1,2,0:T(8,128)S(1)}, u32[]{:S(2)}, u32[]{:S(2)}) %collective-permute-start.7) | collective-permute-done | bytes 82592 | tf_op jit(solution)/shard_map/ppermute | solution.py:17
  151.3 11.0 %fusion.14 = f32[4,20,32,256]{3,1,2,0:T(8,128)S(1)} fusion(f32[4,20,32,1]{3,1,2,0:T(8,128)S(1)} %copy-done.13, f32[4,20,32,256]{3,1,2,0:T(8,128)} %copy-done.2, f32[4,20,32,1]{3,1,2,0:T(8,128)S(1)} %copy-done.10, f32[4,20,1,258]{3,1,2,0:T(8,128)S(1)} %collective-permute-done.7, f32[4,20,1,258]{3,1,2,0:T(8,128)S(1)} %collective-permute-done.6, ...), kind=kLoop, calls=%fused_computation.34 | loop fusion | flops 9830400 | bytes 8705280 | tf_op jit(solution)/shard_map/sub | solution.py:135
  162.3 2.2 fusion.41
  164.5 2.0 copy.274
  166.8 2.0 copy.275
  168.8 5.4 %collective-permute-start.9 = (f32[4,20,32,1]{2,1,3,0:T(8,128)S(1)}, f32[4,20,32,1]{2,1,3,0:T(8,128)}, u32[]{:S(2)}, u32[]{:S(2)}) collective-permute-start(f32[4,20,32,1]{2,1,3,0:T(8,128)S(1)} %copy.275), channel_id=1, source_target_pairs={{1,0},{2,1},{3,2},{4,3},{5,4},{6,5},{7,6},{8,7},{9,8},{10,9},{11,1... | collective-permute-start | bytes 30728 | tf_op jit(solution)/shard_map/ppermute | solution.py:17
  174.3 1.8 copy.276
  176.1 2.6 %copy.277 = f32[4,20,32,1]{3,1,2,0:T(8,128)} copy(f32[4,20,32,1]{2,1,3,0:T(8,128)} %collective-permute-done.9) | data formatting | bytes 20480 | tf_op jit(solution)/shard_map/ppermute | solution.py:17
  179.8 2.4 %collective-permute-start.10 = (f32[4,20,1,258]{3,1,2,0:T(8,128)S(1)}, f32[4,20,1,258]{3,1,2,0:T(8,128)S(1)}, u32[]{:S(2)}, u32[]{:S(2)}) collective-permute-start(f32[4,20,1,258]{3,1,2,0:T(8,128)S(1)} %get-tuple-element.88), channel_id=1, source_target_pairs={{0,16},{16,32},{32,48},{48,64},{64,80},{80,96},{96,112},{1,17},{17... | collective-permute-start | bytes 247688 | tf_op jit(solution)/shard_map/ppermute | solution.py:16
  182.2 2.1 collective-permute-start.11
  184.3 4.4 %collective-permute-done.11 = f32[4,20,1,258]{3,1,2,0:T(8,128)S(1)} collective-permute-done((f32[4,20,1,258]{3,1,2,0:T(8,128)S(1)}, f32[4,20,1,258]{3,1,2,0:T(8,128)S(1)}, u32[]{:S(2)}, u32[]{:S(2)}) %collective-permute-start.11) | collective-permute-done | bytes 82592 | tf_op jit(solution)/shard_map/ppermute | solution.py:17
  188.7 4.0 %fusion.8 = f32[4,20,32,256]{3,1,2,0:T(8,128)S(1)} fusion(f32[4,20,32,1]{3,1,2,0:T(8,128)S(1)} %copy-done.14, f32[4,20,32,256]{3,1,2,0:T(8,128)S(1)} %fusion.14, f32[4,20,32,1]{3,1,2,0:T(8,128)S(1)} %copy-done.12, f32[4,20,1,258]{3,1,2,0:T(8,128)S(1)} %collective-permute-done.11, f32[4,20,1,258]{3,1,2,0:T(8,128)S(1)} %collective-permute-done.10, ...), kind=kLoop, calls=%fused_computation.20 | loop fusion | flops 9175040 | bytes 6083840 | tf_op jit(solution)/shard_map/mul | solution.py:134
  192.7 2.5 %fusion.40 = (f32[4,20,32,1]{3,1,2,0:T(8,128)}, f32[4,20,32,1]{3,1,2,0:T(8,128)}) fusion(f32[4,20,32,256]{3,1,2,0:T(8,128)S(1)} %fusion.8), kind=kLoop, calls=%fused_computation.214 | loop fusion | bytes 40960 | tf_op jit(solution)/shard_map/slice | solution.py:14
  195.3 2.0 copy.280
  197.4 2.7 %copy.281 = f32[4,20,32,1]{2,1,3,0:T(8,128)} copy(f32[4,20,32,1]{3,1,2,0:T(8,128)} %get-tuple-element.95) | data formatting | bytes 20480 | tf_op jit(solution)/shard_map/slice | solution.py:15
  200.1 5.2 %collective-permute-start.13 = (f32[4,20,32,1]{2,1,3,0:T(8,128)}, f32[4,20,32,1]{2,1,3,0:T(8,128)}, u32[]{:S(2)}, u32[]{:S(2)}) collective-permute-start(f32[4,20,32,1]{2,1,3,0:T(8,128)} %copy.281), channel_id=1, source_target_pairs={{1,0},{2,1},{3,2},{4,3},{5,4},{6,5},{7,6},{8,7},{9,8},{10,9},{11,1... | collective-permute-start | bytes 30728 | tf_op jit(solution)/shard_map/ppermute | solution.py:17
  205.4 2.6 %copy.282 = f32[4,20,32,1]{3,1,2,0:T(8,128)} copy(f32[4,20,32,1]{2,1,3,0:T(8,128)} %collective-permute-done.12) | data formatting | bytes 20480 | tf_op jit(solution)/shard_map/ppermute | solution.py:16
  208.0 2.6 %copy.283 = f32[4,20,32,1]{3,1,2,0:T(8,128)} copy(f32[4,20,32,1]{2,1,3,0:T(8,128)} %collective-permute-done.13) | data formatting | bytes 20480 | tf_op jit(solution)/shard_map/ppermute | solution.py:17
  211.9 2.2 collective-permute-start.14
  214.0 2.3 %collective-permute-start.15 = (f32[4,20,1,258]{3,1,2,0:T(8,128)S(1)}, f32[4,20,1,258]{3,1,2,0:T(8,128)S(1)}, u32[]{:S(2)}, u32[]{:S(2)}) collective-permute-start(f32[4,20,1,258]{3,1,2,0:T(8,128)S(1)} %get-tuple-element.87), channel_id=1, source_target_pairs={{16,0},{32,16},{48,32},{64,48},{80,64},{96,80},{112,96},{17,1},{33... | collective-permute-start | bytes 247688 | tf_op jit(solution)/shard_map/ppermute | solution.py:17
  217.0 3.5 %collective-permute-done.15 = f32[4,20,1,258]{3,1,2,0:T(8,128)S(1)} collective-permute-done((f32[4,20,1,258]{3,1,2,0:T(8,128)S(1)}, f32[4,20,1,258]{3,1,2,0:T(8,128)S(1)}, u32[]{:S(2)}, u32[]{:S(2)}) %collective-permute-start.15) | collective-permute-done | bytes 82592 | tf_op jit(solution)/shard_map/ppermute | solution.py:17
  220.5 5.0 %fusion.3 = f32[4,20,32,256]{3,1,2,0:T(8,128)S(1)} fusion(f32[4,20,32,256]{3,1,2,0:T(8,128)S(1)} %fusion.14, f32[4,20,32,1]{3,1,2,0:T(8,128)S(1)} %copy-done.16, f32[4,20,32,256]{3,1,2,0:T(8,128)S(1)} %copy-done.4, f32[4,20,32,1]{3,1,2,0:T(8,128)S(1)} %copy-done.15, f32[4,20,1,258]{3,1,2,0:T(8,128)S(1)} %collective-permute-done.15, ...), kind=kLoop, calls=%fused_computation.7 | loop fusion | flops 9830400 | bytes 8705280 | tf_op jit(solution)/shard_map/sub | solution.py:135
  225.6 2.3 %copy.286 = f32[4,20,32,256]{3,2,1,0:T(8,128)} copy(f32[4,20,32,256]{3,1,2,0:T(8,128)S(1)} %fusion.3) | data formatting | bytes 5242880
  (210 shorter events, 41.7 us)
Async XLA Ops:
  0.6 30.2 %copy-start = (bf16[64,4,128]{2,1,0:T(4,128)(2,1)S(1)}, bf16[64,4,128]{2,1,0:T(4,128)(2,1)}, u32[]{:S(2)}) copy-start(bf16[64,4,128]{2,1,0:T(4,128)(2,1)} %param.12) | copy-start | bytes 196612
  6.6 37.2 %all-to-all-start = ((s32[128,1,6]{2,1,0:T(1,128)}), s32[128,1,6]{2,1,0:T(1,128)}, u32[]{:S(2)}, u32[]{:S(2)}) async-start(s32[128,1,6]{2,1,0:T(1,128)} %bitcast.3), calls=%async_computation | async-start | bytes 131072 | tf_op jit(solution)/shard_map/all_to_all | solution.py:106
  25.0 31.4 %copy-start.22 = (f32[32,256]{1,0:T(8,128)}, f32[32,256]{1,0:T(8,128)S(1)}, u32[]{:S(2)}) copy-start(f32[32,256]{1,0:T(8,128)S(1)} %get-tuple-element.55) | copy-start | bytes 98308
  26.4 29.9 %copy-start.24 = (f32[32,256]{1,0:T(8,128)}, f32[32,256]{1,0:T(8,128)S(1)}, u32[]{:S(2)}) copy-start(f32[32,256]{1,0:T(8,128)S(1)} %get-tuple-element.59) | copy-start | bytes 98308
  26.4 29.9 %copy-start.26 = (f32[32,256]{1,0:T(8,128)}, f32[32,256]{1,0:T(8,128)S(1)}, u32[]{:S(2)}) copy-start(f32[32,256]{1,0:T(8,128)S(1)} %get-tuple-element.60) | copy-start | bytes 98308
  27.9 29.1 %copy-start.28 = (f32[32,256]{1,0:T(8,128)}, f32[32,256]{1,0:T(8,128)S(1)}, u32[]{:S(2)}) copy-start(f32[32,256]{1,0:T(8,128)S(1)} %get-tuple-element.64) | copy-start | bytes 98308
  42.3 12.0 %copy-start.52 = (f32[32,256]{1,0:T(8,128)S(1)}, f32[32,256]{1,0:T(8,128)}, u32[]{:S(2)}) copy-start(f32[32,256]{1,0:T(8,128)} %get-tuple-element.45) | copy-start | bytes 98308
  43.8 13.2 %copy-start.30 = (f32[32,256]{1,0:T(8,128)S(1)}, f32[32,256]{1,0:T(8,128)}, u32[]{:S(2)}) copy-start(f32[32,256]{1,0:T(8,128)} %get-tuple-element.65) | copy-start | bytes 98308
  43.8 13.2 %copy-start.31 = (f32[32,256]{1,0:T(8,128)S(1)}, f32[32,256]{1,0:T(8,128)}, u32[]{:S(2)}) copy-start(f32[32,256]{1,0:T(8,128)} %get-tuple-element.69) | copy-start | bytes 98308
  43.8 13.2 %copy-start.32 = (f32[32,256]{1,0:T(8,128)S(1)}, f32[32,256]{1,0:T(8,128)}, u32[]{:S(2)}) copy-start(f32[32,256]{1,0:T(8,128)} %get-tuple-element.70) | copy-start | bytes 98308
  43.8 13.8 %copy-start.33 = (f32[32,256]{1,0:T(8,128)S(1)}, f32[32,256]{1,0:T(8,128)}, u32[]{:S(2)}) copy-start(f32[32,256]{1,0:T(8,128)} %get-tuple-element.74) | copy-start | bytes 98308
  43.9 13.8 %copy-start.34 = (f32[32,256]{1,0:T(8,128)S(1)}, f32[32,256]{1,0:T(8,128)}, u32[]{:S(2)}) copy-start(f32[32,256]{1,0:T(8,128)} %get-tuple-element.75) | copy-start | bytes 98308
  43.9 39.3 %all-to-all-start.1 = ((f32[128,6,512]{2,1,0:T(8,128)}), f32[128,6,512]{2,1,0:T(8,128)S(1)}, u32[]{:S(2)}, u32[]{:S(2)}) async-start(f32[128,6,512]{2,1,0:T(8,128)} %reshape.155), calls=%async_computation.1 | async-start | bytes 4194304 | tf_op jit(solution)/shard_map/all_to_all | solution.py:99
  55.7 27.4 %copy-start.46 = (f32[32,256]{1,0:T(8,128)}, f32[32,256]{1,0:T(8,128)S(1)}, u32[]{:S(2)}) copy-start(f32[32,256]{1,0:T(8,128)S(1)} %get-tuple-element.82) | copy-start | bytes 98308
  55.7 27.4 %copy-start.48 = (f32[32,256]{1,0:T(8,128)}, f32[32,256]{1,0:T(8,128)S(1)}, u32[]{:S(2)}) copy-start(f32[32,256]{1,0:T(8,128)S(1)} %get-tuple-element.84) | copy-start | bytes 98308
  55.7 27.4 %copy-start.50 = (f32[32,256]{1,0:T(8,128)}, f32[32,256]{1,0:T(8,128)S(1)}, u32[]{:S(2)}) copy-start(f32[32,256]{1,0:T(8,128)S(1)} %get-tuple-element.85) | copy-start | bytes 98308
  95.3 9.6 %collective-permute-start = (f32[4,20,32,1]{2,1,3,0:T(8,128)S(1)}, f32[4,20,32,1]{2,1,3,0:T(8,128)S(1)}, u32[]{:S(2)}, u32[]{:S(2)}) collective-permute-start(f32[4,20,32,1]{2,1,3,0:T(8,128)S(1)} %copy.287), channel_id=1, source_target_pairs={{0,1},{1,2},{2,3},{3,4},{4,5},{5,6},{6,7},{7,8},{8,9},{9,10},{10,1... | collective-permute-start | bytes 30728 | tf_op jit(solution)/shard_map/ppermute | solution.py:16
  97.5 9.5 %collective-permute-start.1 = (f32[4,20,32,1]{2,1,3,0:T(8,128)}, f32[4,20,32,1]{2,1,3,0:T(8,128)S(1)}, u32[]{:S(2)}, u32[]{:S(2)}) collective-permute-start(f32[4,20,32,1]{2,1,3,0:T(8,128)} %copy.288), channel_id=1, source_target_pairs={{1,0},{2,1},{3,2},{4,3},{5,4},{6,5},{7,6},{8,7},{9,8},{10,9},{11,1... | collective-permute-start | bytes 30728 | tf_op jit(solution)/shard_map/ppermute | solution.py:17
  108.9 7.7 %copy-start.21 = (f32[20,32,256]{2,1,0:T(8,128)S(1)}, f32[20,32,256]{2,1,0:T(8,128)}, u32[]{:S(2)}) copy-start(f32[20,32,256]{2,1,0:T(8,128)} %param.21) | copy-start | bytes 1966084
  108.9 12.2 %copy-start.9 = (f32[4,20,32,1]{3,1,2,0:T(8,128)S(1)}, f32[4,20,32,1]{3,1,2,0:T(8,128)}, u32[]{:S(2)}) copy-start(f32[4,20,32,1]{3,1,2,0:T(8,128)} %copy.259) | copy-start | bytes 30724
  108.9 12.2 %copy-start.11 = (f32[4,20,32,1]{3,1,2,0:T(8,128)S(1)}, f32[4,20,32,1]{3,1,2,0:T(8,128)}, u32[]{:S(2)}) copy-start(f32[4,20,32,1]{3,1,2,0:T(8,128)} %copy.261) | copy-start | bytes 30724
  110.1 11.0 %copy-start.6 = (f32[4,20,32,256]{3,1,2,0:T(8,128)S(1)}, f32[4,20,32,256]{3,1,2,0:T(8,128)}, u32[]{:S(2)}) copy-start(f32[4,20,32,256]{3,1,2,0:T(8,128)} %copy-done.5) | copy-start | bytes 7864324
  110.1 7.9 %collective-permute-start.2 = (f32[4,20,1,258]{3,1,2,0:T(8,128)S(1)}, f32[4,20,1,258]{3,1,2,0:T(8,128)S(1)}, u32[]{:S(2)}, u32[]{:S(2)}) collective-permute-start(f32[4,20,1,258]{3,1,2,0:T(8,128)S(1)} %get-tuple-element.92), channel_id=1, source_target_pairs={{0,16},{16,32},{32,48},{48,64},{64,80},{80,96},{96,112},{1,17},{17... | collective-permute-start | bytes 247688 | tf_op jit(solution)/shard_map/ppermute | solution.py:16
  114.6 6.5 %collective-permute-start.3 = (f32[4,20,1,258]{3,1,2,0:T(8,128)S(1)}, f32[4,20,1,258]{3,1,2,0:T(8,128)S(1)}, u32[]{:S(2)}, u32[]{:S(2)}) collective-permute-start(f32[4,20,1,258]{3,1,2,0:T(8,128)S(1)} %get-tuple-element.93), channel_id=1, source_target_pairs={{16,0},{32,16},{48,32},{64,48},{80,64},{96,80},{112,96},{17,1},{33... | collective-permute-start | bytes 247688 | tf_op jit(solution)/shard_map/ppermute | solution.py:17
  125.1 15.9 %copy-start.2 = (f32[4,20,32,256]{3,1,2,0:T(8,128)}, f32[4,20,32,256]{3,1,2,0:T(8,128)S(1)}, u32[]{:S(2)}) copy-start(f32[4,20,32,256]{3,1,2,0:T(8,128)S(1)} %fusion.19) | copy-start | bytes 7864324
  129.6 6.9 %collective-permute-start.4 = (f32[4,20,32,1]{2,1,3,0:T(8,128)S(1)}, f32[4,20,32,1]{2,1,3,0:T(8,128)S(1)}, u32[]{:S(2)}, u32[]{:S(2)}) collective-permute-start(f32[4,20,32,1]{2,1,3,0:T(8,128)S(1)} %copy.267), channel_id=1, source_target_pairs={{0,1},{1,2},{2,3},{3,4},{4,5},{5,6},{6,7},{7,8},{8,9},{9,10},{10,1... | collective-permute-start | bytes 30728 | tf_op jit(solution)/shard_map/ppermute | solution.py:16
  131.7 6.6 %collective-permute-start.5 = (f32[4,20,32,1]{2,1,3,0:T(8,128)S(1)}, f32[4,20,32,1]{2,1,3,0:T(8,128)}, u32[]{:S(2)}, u32[]{:S(2)}) collective-permute-start(f32[4,20,32,1]{2,1,3,0:T(8,128)S(1)} %copy.268), channel_id=1, source_target_pairs={{1,0},{2,1},{3,2},{4,3},{5,4},{6,5},{7,6},{8,7},{9,8},{10,9},{11,1... | collective-permute-start | bytes 30728 | tf_op jit(solution)/shard_map/ppermute | solution.py:17
  141.0 10.3 %copy-start.8 = (f32[4,20,32,256]{3,2,1,0:T(8,128)S(1)}, f32[4,20,32,256]{3,2,1,0:T(8,128)}, u32[]{:S(2)}) copy-start(f32[4,20,32,256]{3,2,1,0:T(8,128)} %copy-done.7) | copy-start | bytes 7864324
  141.0 10.3 %copy-start.10 = (f32[4,20,32,1]{3,1,2,0:T(8,128)S(1)}, f32[4,20,32,1]{3,1,2,0:T(8,128)}, u32[]{:S(2)}) copy-start(f32[4,20,32,1]{3,1,2,0:T(8,128)} %copy.269) | copy-start | bytes 30724
  141.0 10.3 %copy-start.13 = (f32[4,20,32,1]{3,1,2,0:T(8,128)S(1)}, f32[4,20,32,1]{3,1,2,0:T(8,128)}, u32[]{:S(2)}) copy-start(f32[4,20,32,1]{3,1,2,0:T(8,128)} %copy.270) | copy-start | bytes 30724
  142.2 5.0 %collective-permute-start.6 = (f32[4,20,1,258]{3,1,2,0:T(8,128)S(1)}, f32[4,20,1,258]{3,1,2,0:T(8,128)S(1)}, u32[]{:S(2)}, u32[]{:S(2)}) collective-permute-start(f32[4,20,1,258]{3,1,2,0:T(8,128)S(1)} %get-tuple-element.90), channel_id=1, source_target_pairs={{0,16},{16,32},{32,48},{48,64},{64,80},{80,96},{96,112},{1,17},{17... | collective-permute-start | bytes 247688 | tf_op jit(solution)/shard_map/ppermute | solution.py:16
  144.8 6.5 %collective-permute-start.7 = (f32[4,20,1,258]{3,1,2,0:T(8,128)S(1)}, f32[4,20,1,258]{3,1,2,0:T(8,128)S(1)}, u32[]{:S(2)}, u32[]{:S(2)}) collective-permute-start(f32[4,20,1,258]{3,1,2,0:T(8,128)S(1)} %get-tuple-element.91), channel_id=1, source_target_pairs={{16,0},{32,16},{48,32},{64,48},{80,64},{96,80},{112,96},{17,1},{33... | collective-permute-start | bytes 247688 | tf_op jit(solution)/shard_map/ppermute | solution.py:17
  147.2 15.1 %copy-start.19 = (f32[20,32,256]{2,0,1:T(8,128)}, f32[20,32,256]{2,0,1:T(8,128)S(1)}, u32[]{:S(2)}) copy-start(f32[20,32,256]{2,0,1:T(8,128)S(1)} %copy.255) | copy-start | bytes 1966084
  166.5 7.8 %collective-permute-start.8 = (f32[4,20,32,1]{2,1,3,0:T(8,128)S(1)}, f32[4,20,32,1]{2,1,3,0:T(8,128)S(1)}, u32[]{:S(2)}, u32[]{:S(2)}) collective-permute-start(f32[4,20,32,1]{2,1,3,0:T(8,128)S(1)} %copy.274), channel_id=1, source_target_pairs={{0,1},{1,2},{2,3},{3,4},{4,5},{5,6},{6,7},{7,8},{8,9},{9,10},{10,1... | collective-permute-start | bytes 30728 | tf_op jit(solution)/shard_map/ppermute | solution.py:16
  168.8 7.2 %collective-permute-start.9 = (f32[4,20,32,1]{2,1,3,0:T(8,128)S(1)}, f32[4,20,32,1]{2,1,3,0:T(8,128)}, u32[]{:S(2)}, u32[]{:S(2)}) collective-permute-start(f32[4,20,32,1]{2,1,3,0:T(8,128)S(1)} %copy.275), channel_id=1, source_target_pairs={{1,0},{2,1},{3,2},{4,3},{5,4},{6,5},{7,6},{8,7},{9,8},{10,9},{11,1... | collective-permute-start | bytes 30728 | tf_op jit(solution)/shard_map/ppermute | solution.py:17
  178.6 10.1 %copy-start.12 = (f32[4,20,32,1]{3,1,2,0:T(8,128)S(1)}, f32[4,20,32,1]{3,1,2,0:T(8,128)}, u32[]{:S(2)}) copy-start(f32[4,20,32,1]{3,1,2,0:T(8,128)} %copy.276) | copy-start | bytes 30724
  178.7 10.1 %copy-start.14 = (f32[4,20,32,1]{3,1,2,0:T(8,128)S(1)}, f32[4,20,32,1]{3,1,2,0:T(8,128)}, u32[]{:S(2)}) copy-start(f32[4,20,32,1]{3,1,2,0:T(8,128)} %copy.277) | copy-start | bytes 30724
  178.7 10.1 %copy-start.18 = (f32[20,32,256]{2,0,1:T(8,128)S(1)}, f32[20,32,256]{2,0,1:T(8,128)}, u32[]{:S(2)}) copy-start(f32[20,32,256]{2,0,1:T(8,128)} %copy-done.17) | copy-start | bytes 1966084
  179.8 4.5 %collective-permute-start.10 = (f32[4,20,1,258]{3,1,2,0:T(8,128)S(1)}, f32[4,20,1,258]{3,1,2,0:T(8,128)S(1)}, u32[]{:S(2)}, u32[]{:S(2)}) collective-permute-start(f32[4,20,1,258]{3,1,2,0:T(8,128)S(1)} %get-tuple-element.88), channel_id=1, source_target_pairs={{0,16},{16,32},{32,48},{48,64},{64,80},{80,96},{96,112},{1,17},{17... | collective-permute-start | bytes 247688 | tf_op jit(solution)/shard_map/ppermute | solution.py:16
  182.2 6.5 %collective-permute-start.11 = (f32[4,20,1,258]{3,1,2,0:T(8,128)S(1)}, f32[4,20,1,258]{3,1,2,0:T(8,128)S(1)}, u32[]{:S(2)}, u32[]{:S(2)}) collective-permute-start(f32[4,20,1,258]{3,1,2,0:T(8,128)S(1)} %get-tuple-element.89), channel_id=1, source_target_pairs={{16,0},{32,16},{48,32},{64,48},{80,64},{96,80},{112,96},{17,1},{33... | collective-permute-start | bytes 247688 | tf_op jit(solution)/shard_map/ppermute | solution.py:17
  197.4 8.0 %collective-permute-start.12 = (f32[4,20,32,1]{2,1,3,0:T(8,128)S(1)}, f32[4,20,32,1]{2,1,3,0:T(8,128)}, u32[]{:S(2)}, u32[]{:S(2)}) collective-permute-start(f32[4,20,32,1]{2,1,3,0:T(8,128)S(1)} %copy.280), channel_id=1, source_target_pairs={{0,1},{1,2},{2,3},{3,4},{4,5},{5,6},{6,7},{7,8},{8,9},{9,10},{10,1... | collective-permute-start | bytes 30728 | tf_op jit(solution)/shard_map/ppermute | solution.py:16
  200.1 7.9 %collective-permute-start.13 = (f32[4,20,32,1]{2,1,3,0:T(8,128)}, f32[4,20,32,1]{2,1,3,0:T(8,128)}, u32[]{:S(2)}, u32[]{:S(2)}) collective-permute-start(f32[4,20,32,1]{2,1,3,0:T(8,128)} %copy.281), channel_id=1, source_target_pairs={{1,0},{2,1},{3,2},{4,3},{5,4},{6,5},{7,6},{8,7},{9,8},{10,9},{11,1... | collective-permute-start | bytes 30728 | tf_op jit(solution)/shard_map/ppermute | solution.py:17
  210.6 9.9 %copy-start.4 = (f32[4,20,32,256]{3,1,2,0:T(8,128)S(1)}, f32[4,20,32,256]{3,1,2,0:T(8,128)}, u32[]{:S(2)}) copy-start(f32[4,20,32,256]{3,1,2,0:T(8,128)} %copy-done.3) | copy-start | bytes 7864324
  210.6 9.9 %copy-start.15 = (f32[4,20,32,1]{3,1,2,0:T(8,128)S(1)}, f32[4,20,32,1]{3,1,2,0:T(8,128)}, u32[]{:S(2)}) copy-start(f32[4,20,32,1]{3,1,2,0:T(8,128)} %copy.282) | copy-start | bytes 30724
  210.6 9.9 %copy-start.16 = (f32[4,20,32,1]{3,1,2,0:T(8,128)S(1)}, f32[4,20,32,1]{3,1,2,0:T(8,128)}, u32[]{:S(2)}) copy-start(f32[4,20,32,1]{3,1,2,0:T(8,128)} %copy.283) | copy-start | bytes 30724
  211.9 5.2 %collective-permute-start.14 = (f32[4,20,1,258]{3,1,2,0:T(8,128)S(1)}, f32[4,20,1,258]{3,1,2,0:T(8,128)S(1)}, u32[]{:S(2)}, u32[]{:S(2)}) collective-permute-start(f32[4,20,1,258]{3,1,2,0:T(8,128)S(1)} %get-tuple-element.86), channel_id=1, source_target_pairs={{0,16},{16,32},{32,48},{48,64},{64,80},{80,96},{96,112},{1,17},{17... | collective-permute-start | bytes 247688 | tf_op jit(solution)/shard_map/ppermute | solution.py:16
  214.0 6.5 %collective-permute-start.15 = (f32[4,20,1,258]{3,1,2,0:T(8,128)S(1)}, f32[4,20,1,258]{3,1,2,0:T(8,128)S(1)}, u32[]{:S(2)}, u32[]{:S(2)}) collective-permute-start(f32[4,20,1,258]{3,1,2,0:T(8,128)S(1)} %get-tuple-element.87), channel_id=1, source_target_pairs={{16,0},{32,16},{48,32},{64,48},{80,64},{96,80},{112,96},{17,1},{33... | collective-permute-start | bytes 247688 | tf_op jit(solution)/shard_map/ppermute | solution.py:17
  220.5 7.3 %copy-start.1 = (bf16[64,4,128]{2,1,0:T(4,128)(2,1)S(1)}, bf16[64,4,128]{2,1,0:T(4,128)(2,1)}, u32[]{:S(2)}) copy-start(bf16[64,4,128]{2,1,0:T(4,128)(2,1)} %param.12) | copy-start | bytes 196612
  (33 other events, 113.2 us)
where the time goes:
time: 230 us; the launch traced here: 228 us
  starting transfers between devices  62.6 us (27%)
  local copies, waits for them, and re-layouts  62.5 us (27%)
  other arithmetic  56.2 us (24%)
  waiting for transfers between devices  37.5 us (16%)
  matrix products  7.28 us (3%)
    ppermute x8, starting transfers between devices, with_halo(): after = lax.ppermute(initial, axis, down)  27.9 us
    all_to_all x1, waiting for transfers between devices, body(): lax.all_to_all(payload.reshape(devices, capacity, fields * block_len), ('...  22.5 us
    sub x2, other arithmetic, body(): current = current - active[None] * second  16.1 us
    div x15, other arithmetic, mix_columns(): sweep_ratio = -lower_link / pivot_value  15.5 us
    ppermute x8, waiting for transfers between devices, with_halo(): after = lax.ppermute(initial, axis, down)  15 us
    slice x7, local copies, waits for them, and re-layouts, with_halo(): last = lax.slice_in_dim(array, length - width, length, axis=dim)  13.7 us
    ppermute x8, starting transfers between devices, with_halo(): before = lax.ppermute(last, axis, up)  12.9 us
    all_to_all x1, starting transfers between devices, body(): lax.all_to_all(targets.reshape(devices, capacity), ('oy', 'ox'), split_ax...  12 us
  transfers between devices with their start and end apart: 18, of which 5 were waited for; matrix products, arithmetic and copies ran while one was open for 24% of the time, Pallas kernels for 0%

commit v1 on v0

v1 whole, which is shorter than its diff:
```python
import functools

import jax
import jax.numpy as jnp
from jax import lax
from jax.experimental import pallas as pl
from jax.experimental.pallas import tpu as pltpu
from jax.sharding import PartitionSpec as P

SUBSTEPS = 2
CAP = 6
H = 4
CHUNKS = 12
OWN_ID = 64
NBR_ID = 72
LIMIT = 60 * 1024 * 1024

VMEM = pl.BlockSpec(memory_space=pltpu.VMEM)
SMEM = pl.BlockSpec(memory_space=pltpu.SMEM)
ANY = pl.BlockSpec(memory_space=pl.ANY)


def params():
    return pltpu.CompilerParams(vmem_limit_bytes=LIMIT)


def remap_kernel(n_ox, source, owner, block, flux, weights, payload, held, strips, count, sem):
    links = weights.shape[0]
    per = links // CHUNKS
    copies = [
        pltpu.make_async_copy(
            weights.at[pl.ds(c * per, per)], held.at[pl.ds(c * per, per)], sem.at[c]
        )
        for c in range(CHUNKS)
    ]
    for copy in copies:
        copy.start()
    devices = payload.shape[0]

    def clear(i, carry):
        payload[i] = jnp.zeros(payload.shape[1:], jnp.float32)
        strips[i] = jnp.zeros(strips.shape[1:], jnp.float32)
        count[i] = 0
        return carry

    lax.fori_loop(0, devices, clear, 0, unroll=4)
    lane = lax.broadcasted_iota(jnp.int32, (4, 128), 1)
    group = lane >> 2

    def link(k):
        tile = owner[k]
        b = block[k]
        x = flux[source[k]].astype(jnp.bfloat16)
        value = jnp.dot(x, held[k], preferred_element_type=jnp.float32)
        slot = count[tile]
        count[tile] = slot + 1
        payload[tile, slot] = value
        odd = b & 1
        column = lax.rem(tile, n_ox)
        nbr = tile - column + lax.rem(column + jnp.where(odd == 1, 1, n_ox - 1), n_ox)
        entry = slot + jnp.where(odd == 1, 0, CAP)
        moved = pltpu.roll(value, lax.rem(4 * entry + 4 * odd, 128), 1)
        ident = (b + 1).astype(jnp.float32)
        strips[tile] = jnp.where(lane == OWN_ID + slot, ident, strips[tile])
        strips[nbr] = jnp.where(
            group == entry, moved, jnp.where(lane == NBR_ID + entry, ident, strips[nbr])
        )

    unroll = 8
    for c in range(CHUNKS):
        copies[c].wait()

        def some(i, carry, c=c):
            for j in range(unroll):
                link(c * per + i * unroll + j)
            return carry

        lax.fori_loop(0, per // unroll, some, 0)

    def finish(i, carry):
        payload[i, CAP] = strips[i]
        return carry

    lax.fori_loop(0, devices, finish, 0, unroll=8)


def remap(flux, weights, source, owner, block, devices, n_ox):
    links = weights.shape[0]
    return pl.pallas_call(
        functools.partial(remap_kernel, n_ox),
        out_shape=jax.ShapeDtypeStruct((devices, CAP + 1, 4, 128), jnp.float32),
        in_specs=[SMEM, SMEM, SMEM, VMEM, ANY],
        out_specs=VMEM,
        scratch_shapes=[
            pltpu.VMEM((links, 128, 128), jnp.bfloat16),
            pltpu.VMEM((devices, 4, 128), jnp.float32),
            pltpu.SMEM((devices,), jnp.int32),
            pltpu.SemaphoreType.DMA((CHUNKS,)),
        ],
        compiler_params=params(),
        name="remap",
    )(source, owner, block, flux, weights)


def plane_of(tracers, diffusivity, viscosity, levels, p):
    nl = diffusivity.shape[0]
    nt = tracers.shape[0]
    if p < nt * nl:
        return tracers.at[p // nl, p % nl]
    if p < (nt + 1) * nl:
        return diffusivity.at[p - nt * nl]
    if p < (nt + 2) * nl:
        return viscosity.at[p - (nt + 1) * nl]
    return levels


def pack_kernel(planes, tracers, diffusivity, viscosity, levels, west, east, top, bottom):
    rows = levels.shape[0]
    width = levels.shape[1]
    group = lax.broadcasted_iota(jnp.int32, (rows, 128), 1) >> 2
    for g in range(-(-planes // 32)):
        left = jnp.zeros((rows, 128), jnp.float32)
        right = jnp.zeros((rows, 128), jnp.float32)
        for s in range(min(32, planes - 32 * g)):
            ref = plane_of(tracers, diffusivity, viscosity, levels, 32 * g + s)
            left = jnp.where(group == s, pltpu.roll(ref[:, 0:128], 4 * s, 1), left)
            right = jnp.where(
                group == s, pltpu.roll(ref[:, width - 128 : width], (4 * s + 4) % 128, 1), right
            )
            top[32 * g + s] = ref[0:H, :]
            bottom[32 * g + s] = ref[rows - H : rows, :]
        west[g] = left
        east[g] = right


def pack(tracers, diffusivity, viscosity, levels):
    nt, nl, rows, width = tracers.shape
    planes = (nt + 2) * nl + 1
    groups = -(-planes // 32)
    edge = jax.ShapeDtypeStruct((groups, rows, 128), jnp.float32)
    line = jax.ShapeDtypeStruct((planes, H, width), jnp.float32)
    return pl.pallas_call(
        functools.partial(pack_kernel, planes),
        out_shape=(edge, edge, line, line),
        in_specs=[VMEM] * 4,
        out_specs=(VMEM,) * 4,
        compiler_params=params(),
        name="pack",
    )(tracers, diffusivity, viscosity, levels)


def mix_kernel(
    planes,
    tracers, diffusivity, viscosity, levels,
    from_west, from_east, north, south, north_corner, south_corner,
    base, response, weight, levels_ext,
    diff_ext, ratios,
):
    nt, nl, rows, width = tracers.shape
    groups = from_west.shape[0]
    lane = lax.broadcasted_iota(jnp.int32, (rows, 128), 1)
    lane8 = lax.broadcasted_iota(jnp.int32, (2 * H, 128), 1)

    def target(p):
        if p < nt * nl:
            return base.at[p % nl, p // nl]
        if p < (nt + 1) * nl:
            return diff_ext.at[p - nt * nl]
        if p < (nt + 2) * nl:
            return weight.at[p - (nt + 1) * nl]
        return levels_ext

    for p in range(planes):
        g, s = p // 32, p % 32
        out = target(p)
        ref = plane_of(tracers, diffusivity, viscosity, levels, p)
        out[0:rows, 0:width] = ref[...]
        out[rows : rows + 2 * H, 0:width] = jnp.concatenate([south[p], north[p]], axis=0)

        def side(east, west, lanes):
            return jnp.where(
                lanes < H,
                pltpu.roll(east, (128 - 4 * s) % 128, 1),
                jnp.where(lanes >= 128 - H, pltpu.roll(west, (252 - 4 * s) % 128, 1), 0.0),
            )

        out[0:rows, width : width + 128] = side(from_east[g], from_west[g], lane)
        out[rows : rows + 2 * H, width : width + 128] = side(
            jnp.concatenate([south_corner[g], north_corner[g]], axis=0),
            jnp.concatenate([south_corner[groups + g], north_corner[groups + g]], axis=0),
            lane8,
        )

    across = (width + 128) // 128

    def tile(t, carry):
        r = pl.ds(pl.multiple_of((t // across) * 8, 8), 8)
        c = pl.ds(pl.multiple_of((t % across) * 128, 128), 128)
        depth = levels_ext[r, c]
        nothing = jnp.zeros((8, 128), jnp.float32)
        ratio, upper, single = nothing, nothing, nothing
        values = [nothing] * nt
        for level in range(nl):
            if level < nl - 1:
                lower = jnp.where(level + 1 < depth, diff_ext[level, r, c], 0.0)
            else:
                lower = nothing
            inverse = 1.0 / (1.0 + upper + lower + upper * ratio)
            ratio = -lower * inverse
            ratios[level] = ratio
            for f in range(nt):
                values[f] = (base[level, f, r, c] + upper * values[f]) * inverse
                base[level, f, r, c] = values[f]
            single = inverse if level == 0 else (upper * single) * inverse
            response[level, r, c] = single
            weight[level, r, c] = jnp.where(level < depth, weight[level, r, c], 0.0)
            upper = lower
        for level in range(nl - 2, -1, -1):
            ratio = ratios[level]
            for f in range(nt):
                values[f] = base[level, f, r, c] - ratio * values[f]
                base[level, f, r, c] = values[f]
            single = response[level, r, c] - ratio * single
            response[level, r, c] = single
        return carry

    lax.fori_loop(0, (rows + 2 * H) // 8 * across, tile, 0)


def mix(tracers, diffusivity, viscosity, levels, halo):
    nt, nl, rows, width = tracers.shape
    planes = (nt + 2) * nl + 1
    tall, wide = rows + 2 * H, width + 128
    f32 = jnp.float32
    return pl.pallas_call(
        functools.partial(mix_kernel, planes),
        out_shape=(
            jax.ShapeDtypeStruct((nl, nt, tall, wide), f32),
            jax.ShapeDtypeStruct((nl, tall, wide), f32),
            jax.ShapeDtypeStruct((nl, tall, wide), f32),
            jax.ShapeDtypeStruct((tall, wide), f32),
        ),
        in_specs=[VMEM] * 10,
        out_specs=(VMEM,) * 4,
        scratch_shapes=[pltpu.VMEM((nl, tall, wide), f32), pltpu.VMEM((nl, 8, 128), f32)],
        compiler_params=params(),
        name="mix",
    )(tracers, diffusivity, viscosity, levels, *halo)


def two(x):
    high = x.astype(jnp.bfloat16)
    return high, (x - high.astype(jnp.float32)).astype(jnp.bfloat16)


def collect_kernel(arrived, mask, ocean_flux, side, to_north, to_south):
    rows, width = mask.shape
    nt = ocean_flux.shape[0]
    stride = (CAP + 1) * nt
    devices = arrived.shape[0] // stride

    def slot(s):
        return jnp.concatenate(
            [arrived[pl.ds(s * nt + f, devices, stride=stride), :] for f in range(nt)], axis=1
        )

    idents = jnp.transpose(arrived[pl.ds(CAP * nt, devices, stride=stride), :]).astype(jnp.int32) - 1
    y = lax.broadcasted_iota(jnp.int32, (rows, devices), 0)
    places = jnp.concatenate([2 * y, 2 * y + 1], axis=0)
    total = jnp.zeros((2 * rows, nt * 128), jnp.float32)
    for s in range(CAP):
        pick = (places == idents[OWN_ID + s : OWN_ID + s + 1, :]).astype(jnp.bfloat16)
        for piece in two(slot(s)):
            total = total + jnp.dot(pick, piece, preferred_element_type=jnp.float32)
    keep = mask[...].astype(jnp.float32)
    main = []
    for f in range(nt):
        cells = slice(f * 128, (f + 1) * 128)
        main.append(jnp.concatenate([total[0:rows, cells], total[rows:, cells]], axis=1) * keep)
        ocean_flux[f] = main[f]
    pick = jnp.concatenate(
        [
            (y == (idents[NBR_ID + e : NBR_ID + e + 1, :] >> 1)).astype(jnp.bfloat16)
            for e in range(2 * CAP)
        ],
        axis=0,
    )
    high, low = two(slot(CAP))
    spread = jnp.dot(pick, high, preferred_element_type=jnp.float32) + jnp.dot(
        pick, low, preferred_element_type=jnp.float32
    )
    lane = lax.broadcasted_iota(jnp.int32, (rows, 128), 1)
    for f in range(nt):
        west = jnp.zeros((rows, 128), jnp.float32)
        east = jnp.zeros((rows, 128), jnp.float32)
        for e in range(CAP):
            part = spread[e * rows : (e + 1) * rows, f * 128 : (f + 1) * 128]
            west = west + pltpu.roll(part, (124 - 4 * e) % 128, 1)
            e = e + CAP
            part = spread[e * rows : (e + 1) * rows, f * 128 : (f + 1) * 128]
            east = east + pltpu.roll(part, (128 - 4 * e) % 128, 1)
        edge = jnp.where(lane < H, east, jnp.where(lane >= 128 - H, west, 0.0))
        side[f] = edge
        whole = jnp.concatenate([main[f], edge], axis=1)
        to_north[f] = whole[0:H]
        to_south[f] = whole[rows - H : rows]


def collect(arrived, mask, nt):
    rows, width = mask.shape
    f32 = jnp.float32
    line = jax.ShapeDtypeStruct((nt, H, width + 128), f32)
    return pl.pallas_call(
        collect_kernel,
        out_shape=(
            jax.ShapeDtypeStruct((nt, rows, width), f32),
            jax.ShapeDtypeStruct((nt, rows, 128), f32),
            line,
            line,
        ),
        in_specs=[VMEM] * 2,
        out_specs=(VMEM,) * 4,
        compiler_params=params(),
        name="collect",
    )(arrived, mask)


def laplace(v):
    tall, wide = v.shape
    return (
        pltpu.roll(v, 1, 0)
        + pltpu.roll(v, tall - 1, 0)
        + pltpu.roll(v, 1, 1)
        + pltpu.roll(v, wide - 1, 1)
        - 4.0 * v
    )


def diffuse_kernel(base, response, weight, levels, main, side, north, south, out, surface):
    nt, rows, width = main.shape
    level = pl.program_id(0)

    @pl.when(level == 0)
    def _():
        wet = levels[...] > 0.0
        for f in range(nt):
            top = jnp.concatenate([main[f], side[f]], axis=1)
            whole = jnp.concatenate([top, south[f], north[f]], axis=0)
            surface[f] = jnp.where(wet, whole, 0.0)

    active = (level.astype(jnp.float32) < levels[...]).astype(jnp.float32)
    for f in range(nt):
        v = base[0, f] + response[0] * surface[f]
        for substep in range(SUBSTEPS):
            v = v - active * laplace(weight[0] * laplace(v))
        out[f, 0] = v[0:rows, 0:width]


def diffuse(base, response, weight, levels, main, side, north, south):
    nl, nt, tall, wide = base.shape
    rows, width = main.shape[1:]

    def whole(x):
        return pl.BlockSpec(x.shape, lambda i: (0,) * len(x.shape))

    layer = pl.BlockSpec((1, tall, wide), lambda i: (i, 0, 0))
    return pl.pallas_call(
        diffuse_kernel,
        grid=(nl,),
        out_shape=jax.ShapeDtypeStruct((nt, nl, rows, width), jnp.float32),
        in_specs=[
            pl.BlockSpec((1, nt, tall, wide), lambda i: (i, 0, 0, 0)),
            layer,
            layer,
            whole(levels),
            whole(main),
            whole(side),
            whole(north),
            whole(south),
        ],
        out_specs=pl.BlockSpec((nt, 1, rows, width), lambda i: (0, i, 0, 0)),
        scratch_shapes=[pltpu.VMEM((nt, tall, wide), jnp.float32)],
        compiler_params=params(),
        name="diffuse",
    )(base, response, weight, levels, main, side, north, south)


def body(
    atm_flux,
    remap_weights,
    link_source,
    link_owner,
    link_block,
    ocean_mask,
    level_count,
    tracers,
    diffusivity,
    viscosity,
):
    n_oy = lax.axis_size("oy")
    n_ox = lax.axis_size("ox")
    devices = n_oy * n_ox
    nt = tracers.shape[0]
    rows = tracers.shape[2]
    payload = remap(
        atm_flux.astype(jnp.float32),
        remap_weights,
        link_source,
        link_owner[:, 0],
        link_block,
        devices,
        n_ox,
    )
    arrived = lax.all_to_all(payload, ("oy", "ox"), split_axis=0, concat_axis=0, tiled=True)
    arrived = arrived.reshape(devices * (CAP + 1) * nt, 128)

    levels = (level_count * ocean_mask).astype(jnp.float32)
    eastward = [(i, (i + 1) % n_ox) for i in range(n_ox)]
    westward = [(j, i) for i, j in eastward]
    southward = [(i, i + 1) for i in range(n_oy - 1)]
    northward = [(j, i) for i, j in southward]
    west, east, top, bottom = pack(tracers, diffusivity, viscosity, levels)
    from_west = lax.ppermute(east, "ox", eastward)
    from_east = lax.ppermute(west, "ox", westward)
    north = lax.ppermute(bottom, "oy", southward)
    south = lax.ppermute(top, "oy", northward)
    both = jnp.concatenate([from_east, from_west], axis=0)
    north_corner = lax.ppermute(both[:, rows - H :], "oy", southward)
    south_corner = lax.ppermute(both[:, :H], "oy", northward)
    halo = (from_west, from_east, north, south, north_corner, south_corner)
    base, response, weight, levels_ext = mix(tracers, diffusivity, viscosity, levels, halo)

    ocean_flux, side, to_north, to_south = collect(arrived, ocean_mask, nt)
    flux_north = lax.ppermute(to_south, "oy", southward)
    flux_south = lax.ppermute(to_north, "oy", northward)
    mixed = diffuse(
        base, response, weight, levels_ext, ocean_flux, side, flux_north, flux_south
    )
    return mixed, ocean_flux


def solution(mesh):
    placed = (
        P(("oy", "ox"), None, None),
        P(("oy", "ox"), None, None),
        P(("oy", "ox")),
        P(("oy", "ox"), None),
        P(("oy", "ox")),
        P("oy", "ox"),
        P("oy", "ox"),
        P(None, None, "oy", "ox"),
        P(None, "oy", "ox"),
        P(None, "oy", "ox"),
    )
    return jax.shard_map(
        body,
        mesh=mesh,
        in_specs=placed,
        out_specs=(P(None, None, "oy", "ox"), P(None, "oy", "ox")),
        check_vma=False,
    )
```

time: 230 us -> 111 us (0.48)
  local copies, waits for them, and re-layouts: 62.5 us -> 3.43 us
  Pallas kernels: 0 us -> 57.5 us
  other arithmetic: 56.2 us -> 3.4 us
  starting transfers between devices: 62.6 us -> 33.8 us
  waiting for transfers between devices: 37.5 us -> 11.9 us
  matrix products: 7.28 us -> 0 us
    pallas_call x0 -> x5, Pallas kernels: none -> 57.5 us  [the longest x1 23.8 us: diffuse(): pl.pallas_call(diffuse_kernel, grid=(nl,), out_shape=jax.ShapeDtypeStruct...]
    all_to_all x2 -> x1, waiting for transfers between devices: 22.5 us -> 0.01 us  [body(): lax.all_to_all(payload, ('oy', 'ox'), split_axis=0, concat_axis=0, tiled=...]
    slice x10 -> x1, local copies, waits for them, and re-layouts: 20.4 us -> 0.01 us  [body(): south_corner = lax.ppermute(both[:, :H], 'oy', northward)]
    ppermute x16 -> x8, starting transfers between devices: 40.8 us -> 22.3 us  [the longest x1 5.57 us: body(): from_east = lax.ppermute(west, 'ox', westward)]
    ppermute x8 -> x0, local copies, waits for them, and re-layouts: 18 us -> none  [the longest x4 9.62 us: with_halo(): after = lax.ppermute(initial, axis, down)]
    sub x4 -> x0, other arithmetic: 17.6 us -> none  [the longest x2 16.1 us: body(): current = current - active[None] * second]
    div x15 -> x0, other arithmetic: 15.5 us -> none  [mix_columns(): sweep_ratio = -lower_link / pivot_value]
    all_to_all x2 -> x1, starting transfers between devices: 21.7 us -> 11.5 us  [body(): lax.all_to_all(payload, ('oy', 'ox'), split_axis=0, concat_axis=0, tiled=...]
  transfers between devices with their start and end apart: 18 -> 9, of which waited for: 5 -> 3; matrix products, arithmetic and copies ran while one was open for 24% -> 1% of each run, Pallas kernels for 0% -> 16%
where the time goes in v1:
time: 111 us
  Pallas kernels  57.5 us (52%)
  starting transfers between devices  33.8 us (30%)
  waiting for transfers between devices  11.9 us (11%)
  local copies, waits for them, and re-layouts  3.43 us (3%)
  other arithmetic  3.4 us (3%)
    pallas_call x1, Pallas kernels, diffuse(): pl.pallas_call(diffuse_kernel, grid=(nl,), out_shape=jax.ShapeDtypeStruct...  23.8 us
    pallas_call x1, Pallas kernels, remap(): pl.pallas_call(functools.partial(remap_kernel, n_ox), out_shape=jax.Shape...  16 us
    all_to_all x1, starting transfers between devices, body(): lax.all_to_all(payload, ('oy', 'ox'), split_axis=0, concat_axis=0, tiled=...  11.5 us
    pallas_call x1, Pallas kernels, mix(): pl.pallas_call(functools.partial(mix_kernel, planes), out_shape=(jax.Shap...  10.5 us
    ppermute x1, waiting for transfers between devices, body(): from_east = lax.ppermute(west, 'ox', westward)  6.78 us
    ppermute x1, starting transfers between devices, body(): from_east = lax.ppermute(west, 'ox', westward)  5.57 us
    pallas_call x1, Pallas kernels, pack(): pl.pallas_call(functools.partial(pack_kernel, planes), out_shape=(edge, e...  4.24 us
    ppermute x1, waiting for transfers between devices, body(): from_west = lax.ppermute(east, 'ox', eastward)  4.21 us
  transfers between devices with their start and end apart: 9, of which 3 were waited for; matrix products, arithmetic and copies ran while one was open for 1% of the time, Pallas kernels for 16%

profile of v1, /device:TPU:1, one launch (start us, length us, event | category | flops | bytes accessed | tf_op | source)
XLA Modules:
  0.0 110.8 jit_solution(5637839796204234226)
XLA Ops:
  0.6 1.5 %convert_element_type.7.flux = f32[64,4,128]{2,1,0:T(4,128)} convert(bf16[64,4,128]{2,1,0:T(4,128)(2,1)} %param.10) | non-fusion elementwise | flops 32768 | bytes 196608 | tf_op jit(solution)/shard_map/convert_element_type | solution.py:406
  2.1 1.3 %reduce.owner = s32[384]{0:T(512)} reduce(s32[384,1]{0,1:T(1,128)} %param.13, s32[]{:T(128)} %constant.1), dimensions={1}, to_apply=%param.13.reduce_sub_computation | reduce | bytes 3076 | tf_op args[3]
  3.4 16.0 %remap.1 = f32[128,7,4,128]{3,2,1,0:T(4,128)} custom-call(s32[384]{0:T(512)} %source.1, s32[384]{0:T(512)} %reduce.owner, s32[384]{0:T(512)} %block.1, f32[64,4,128]{2,1,0:T(4,128)} %convert_element_type.7.flux, bf16[384,128,128]{2,1,0:T(8,128)(2,1)} %weights.1), custom_call_target="tpu_custom_call" | custom-call | tf_op jit(solution)/shard_map/remap/pallas_call | solution.py:89
  19.4 0.0 copy-start.5
  19.4 0.0 copy-start.6
  19.4 11.5 %all-to-all-start = ((f32[128,7,4,128]{3,2,1,0:T(4,128)}), f32[128,7,4,128]{3,2,1,0:T(4,128)S(1)}, u32[]{:S(2)}, u32[]{:S(2)}) async-start(f32[128,7,4,128]{3,2,1,0:T(4,128)} %remap.1), calls=%async_computation | async-start | bytes 3670016 | tf_op jit(solution)/shard_map/all_to_all | solution.py:414
  30.9 0.0 copy-done.5
  30.9 0.0 copy-done.6
  31.0 0.6 multiply_convert_fusion.levels
  31.6 4.2 %pack.1 = (f32[4,32,128]{2,1,0:T(8,128)}, f32[4,32,128]{2,1,0:T(8,128)}, f32[121,4,256]{2,1,0:T(4,128)}, f32[121,4,256]{2,1,0:T(4,128)}) custom-call(f32[4,20,32,256]{3,2,1,0:T(8,128)} %tracers.3, f32[20,32,256]{2,1,0:T(8,128)} %diffusivity.3, f32[20,32,256]{2,1,0:T(8,128)} %viscosity.3, f32[32,256]{1,0:T(8,128)} %multiply_convert_fusion.levels), custom_call_target="tpu_custom_call" | custom-call | tf_op jit(solution)/shard_map/pack/pallas_call | solution.py:142
  35.8 5.6 %collective-permute-start.1 = (f32[4,32,128]{2,1,0:T(8,128)}, f32[4,32,128]{2,1,0:T(8,128)S(1)}, u32[]{:S(2)}, u32[]{:S(2)}) collective-permute-start(f32[4,32,128]{2,1,0:T(8,128)} %get-tuple-element.15), channel_id=1, source_target_pairs={{1,0},{2,1},{3,2},{4,3},{5,4},{6,5},{7,6},{8,7},{9,8},{10,9},{11,1... | collective-permute-start | bytes 196616 | tf_op jit(solution)/shard_map/ppermute | solution.py:424
  41.4 3.6 %collective-permute-start.2 = (f32[121,4,256]{2,1,0:T(4,128)}, f32[121,4,256]{2,1,0:T(4,128)S(1)}, u32[]{:S(2)}, u32[]{:S(2)}) collective-permute-start(f32[121,4,256]{2,1,0:T(4,128)} %get-tuple-element.16), channel_id=1, source_target_pairs={{0,16},{16,32},{32,48},{48,64},{64,80},{80,96},{96,112},{1,17},{17... | collective-permute-start | bytes 1486856 | tf_op jit(solution)/shard_map/ppermute | solution.py:425
  45.0 1.9 %collective-permute-start.3 = (f32[121,4,256]{2,1,0:T(4,128)}, f32[121,4,256]{2,1,0:T(4,128)S(1)}, u32[]{:S(2)}, u32[]{:S(2)}) collective-permute-start(f32[121,4,256]{2,1,0:T(4,128)} %get-tuple-element.17), channel_id=1, source_target_pairs={{16,0},{32,16},{48,32},{64,48},{80,64},{96,80},{112,96},{17,1},{33... | collective-permute-start | bytes 1486856 | tf_op jit(solution)/shard_map/ppermute | solution.py:426
  46.9 0.1 collective-permute-start
  47.0 6.8 %collective-permute-done.1.from_east = f32[4,32,128]{2,1,0:T(8,128)S(1)} collective-permute-done((f32[4,32,128]{2,1,0:T(8,128)}, f32[4,32,128]{2,1,0:T(8,128)S(1)}, u32[]{:S(2)}, u32[]{:S(2)}) %collective-permute-start.1) | collective-permute-done | bytes 65568 | tf_op jit(solution)/shard_map/ppermute | solution.py:424
  53.8 0.0 copy-start.3
  53.8 4.2 %collective-permute-done.from_west = f32[4,32,128]{2,1,0:T(8,128)S(1)} collective-permute-done((f32[4,32,128]{2,1,0:T(8,128)}, f32[4,32,128]{2,1,0:T(8,128)S(1)}, u32[]{:S(2)}, u32[]{:S(2)}) %collective-permute-start) | collective-permute-done | bytes 65568 | tf_op jit(solution)/shard_map/ppermute | solution.py:423
  58.0 0.0 copy-start.4
  58.1 2.4 %collective-permute-start.5 = (f32[8,4,128]{2,1,0:T(4,128)S(1)}, f32[8,4,128]{2,1,0:T(4,128)S(1)}, u32[]{:S(2)}, u32[]{:S(2)}) collective-permute-start(f32[8,4,128]{2,1,0:T(4,128)S(1)} %get-tuple-element.26), channel_id=1, source_target_pairs={{16,0},{32,16},{48,32},{64,48},{80,64},{96,80},{112,96},{17,1},{33... | collective-permute-start | bytes 49160 | tf_op jit(solution)/shard_map/ppermute | solution.py:429
  60.5 0.0 all-to-all-done
  60.5 0.0 copy-start
  60.5 1.2 %copy-done = f32[128,7,4,128]{3,2,1,0:T(4,128)} copy-done((f32[128,7,4,128]{3,2,1,0:T(4,128)}, f32[128,7,4,128]{3,2,1,0:T(4,128)S(1)}, u32[]{:S(2)}) %copy-start) | copy-done | bytes 1835032
  61.8 3.0 %collect.1 = (f32[4,32,256]{2,1,0:T(8,128)}, f32[4,32,128]{2,1,0:T(8,128)}, f32[4,4,384]{2,1,0:T(4,128)}, f32[4,4,384]{2,1,0:T(4,128)}) custom-call(f32[3584,128]{1,0:T(8,128)} %bitcast.1, s32[32,256]{1,0:T(8,128)} %mask.1), custom_call_target="tpu_custom_call" | custom-call | tf_op jit(solution)/shard_map/collect/pallas_call | solution.py:313
  64.7 3.1 %collective-permute-start.6 = (f32[4,4,384]{2,1,0:T(4,128)}, f32[4,4,384]{2,1,0:T(4,128)S(1)}, u32[]{:S(2)}, u32[]{:S(2)}) collective-permute-start(f32[4,4,384]{2,1,0:T(4,128)} %get-tuple-element.24), channel_id=1, source_target_pairs={{0,16},{16,32},{32,48},{48,64},{64,80},{80,96},{96,112},{1,17},{17... | collective-permute-start | bytes 73736 | tf_op jit(solution)/shard_map/ppermute | solution.py:434
  67.9 1.9 %collective-permute-start.7 = (f32[4,4,384]{2,1,0:T(4,128)}, f32[4,4,384]{2,1,0:T(4,128)S(1)}, u32[]{:S(2)}, u32[]{:S(2)}) collective-permute-start(f32[4,4,384]{2,1,0:T(4,128)} %get-tuple-element.25), channel_id=1, source_target_pairs={{16,0},{32,16},{48,32},{64,48},{80,64},{96,80},{112,96},{17,1},{33... | collective-permute-start | bytes 73736 | tf_op jit(solution)/shard_map/ppermute | solution.py:435
  69.8 0.0 collective-permute-done.5.south_corner
  69.8 0.0 copy-start.9
  69.8 3.6 %collective-permute-start.4 = (f32[8,4,128]{2,1,0:T(4,128)S(1)}, f32[8,4,128]{2,1,0:T(4,128)S(1)}, u32[]{:S(2)}, u32[]{:S(2)}) collective-permute-start(f32[8,4,128]{2,1,0:T(4,128)S(1)} %get-tuple-element.27), channel_id=1, source_target_pairs={{0,16},{16,32},{32,48},{48,64},{64,80},{80,96},{96,112},{1,17},{17... | collective-permute-start | bytes 49160 | tf_op jit(solution)/shard_map/ppermute | solution.py:428
  73.5 0.8 collective-permute-done.4.north_corner
  74.3 0.0 copy-start.10
  74.3 0.0 collective-permute-done.2.north
  74.3 0.0 copy-start.1
  74.3 0.0 collective-permute-done.3.south
  74.3 0.0 copy-done.3
  74.3 0.0 copy-done.4
  74.4 0.0 copy-done.9
  74.4 0.6 copy-done.10
  74.9 0.2 copy-done.1
  75.1 0.0 copy-start.2
  75.1 0.8 copy-done.2
  75.9 10.5 %mix.1 = (f32[20,4,40,384]{3,2,1,0:T(8,128)}, f32[20,40,384]{2,1,0:T(8,128)}, f32[20,40,384]{2,1,0:T(8,128)}, f32[40,384]{1,0:T(8,128)}) custom-call(f32[4,20,32,256]{3,2,1,0:T(8,128)} %tracers.3, f32[20,32,256]{2,1,0:T(8,128)} %diffusivity.3, f32[20,32,256]{2,1,0:T(8,128)} %viscosity.3, f32[32,256]{1,0:T(8,128)} %multiply_convert_fusion.levels, ...), custom_call_target="tpu_custom_call" | custom-call | tf_op jit(solution)/shard_map/mix/pallas_call | solution.py:235
  86.4 0.0 collective-permute-done.6.north
  86.4 0.0 copy-start.7
  86.4 0.0 collective-permute-done.7.south
  86.4 0.0 copy-start.8
  86.4 0.6 copy-done.7
  87.0 0.0 copy-done.8
  87.0 23.8 %diffuse.1 = f32[4,20,32,256]{3,2,1,0:T(8,128)} custom-call(f32[20,4,40,384]{3,2,1,0:T(8,128)} %get-tuple-element.18.base, f32[20,40,384]{2,1,0:T(8,128)} %get-tuple-element.19.response, f32[20,40,384]{2,1,0:T(8,128)} %get-tuple-element.20.weight, f32[40,384]{1,0:T(8,128)} %get-tuple-element.21.levels, f32[4,32,256]{2,1,0:T(8,128)} %get-tuple-element.13.main, ...), custom_call_target="tpu_custom_call" | custom-call | tf_op jit(solution)/shard_map/diffuse/pallas_call | solution.py:367
  (3 shorter events, 0.0 us)
Async XLA Ops:
  19.4 11.5 %copy-start.5 = (s32[32,256]{1,0:T(8,128)S(1)}, s32[32,256]{1,0:T(8,128)}, u32[]{:S(2)}) copy-start(s32[32,256]{1,0:T(8,128)} %mask.1) | copy-start | bytes 98308
  19.4 11.5 %copy-start.6 = (s32[32,256]{1,0:T(8,128)S(1)}, s32[32,256]{1,0:T(8,128)}, u32[]{:S(2)}) copy-start(s32[32,256]{1,0:T(8,128)} %param.16) | copy-start | bytes 98308
  19.4 41.1 %all-to-all-start = ((f32[128,7,4,128]{3,2,1,0:T(4,128)}), f32[128,7,4,128]{3,2,1,0:T(4,128)S(1)}, u32[]{:S(2)}, u32[]{:S(2)}) async-start(f32[128,7,4,128]{3,2,1,0:T(4,128)} %remap.1), calls=%async_computation | async-start | bytes 3670016 | tf_op jit(solution)/shard_map/all_to_all | solution.py:414
  35.8 18.0 %collective-permute-start.1 = (f32[4,32,128]{2,1,0:T(8,128)}, f32[4,32,128]{2,1,0:T(8,128)S(1)}, u32[]{:S(2)}, u32[]{:S(2)}) collective-permute-start(f32[4,32,128]{2,1,0:T(8,128)} %get-tuple-element.15), channel_id=1, source_target_pairs={{1,0},{2,1},{3,2},{4,3},{5,4},{6,5},{7,6},{8,7},{9,8},{10,9},{11,1... | collective-permute-start | bytes 196616 | tf_op jit(solution)/shard_map/ppermute | solution.py:424
  41.4 32.9 %collective-permute-start.2 = (f32[121,4,256]{2,1,0:T(4,128)}, f32[121,4,256]{2,1,0:T(4,128)S(1)}, u32[]{:S(2)}, u32[]{:S(2)}) collective-permute-start(f32[121,4,256]{2,1,0:T(4,128)} %get-tuple-element.16), channel_id=1, source_target_pairs={{0,16},{16,32},{32,48},{48,64},{64,80},{80,96},{96,112},{1,17},{17... | collective-permute-start | bytes 1486856 | tf_op jit(solution)/shard_map/ppermute | solution.py:425
  45.0 29.3 %collective-permute-start.3 = (f32[121,4,256]{2,1,0:T(4,128)}, f32[121,4,256]{2,1,0:T(4,128)S(1)}, u32[]{:S(2)}, u32[]{:S(2)}) collective-permute-start(f32[121,4,256]{2,1,0:T(4,128)} %get-tuple-element.17), channel_id=1, source_target_pairs={{16,0},{32,16},{48,32},{64,48},{80,64},{96,80},{112,96},{17,1},{33... | collective-permute-start | bytes 1486856 | tf_op jit(solution)/shard_map/ppermute | solution.py:426
  46.9 11.1 %collective-permute-start = (f32[4,32,128]{2,1,0:T(8,128)}, f32[4,32,128]{2,1,0:T(8,128)S(1)}, u32[]{:S(2)}, u32[]{:S(2)}) collective-permute-start(f32[4,32,128]{2,1,0:T(8,128)} %get-tuple-element.14), channel_id=1, source_target_pairs={{0,1},{1,2},{2,3},{3,4},{4,5},{5,6},{6,7},{7,8},{8,9},{9,10},{10,1... | collective-permute-start | bytes 196616 | tf_op jit(solution)/shard_map/ppermute | solution.py:423
  53.8 20.5 %copy-start.3 = (f32[4,32,128]{2,1,0:T(8,128)}, f32[4,32,128]{2,1,0:T(8,128)S(1)}, u32[]{:S(2)}) copy-start(f32[4,32,128]{2,1,0:T(8,128)S(1)} %collective-permute-done.1.from_east) | copy-start | bytes 196612
  58.0 16.3 %copy-start.4 = (f32[4,32,128]{2,1,0:T(8,128)}, f32[4,32,128]{2,1,0:T(8,128)S(1)}, u32[]{:S(2)}) copy-start(f32[4,32,128]{2,1,0:T(8,128)S(1)} %collective-permute-done.from_west) | copy-start | bytes 196612
  58.1 11.8 %collective-permute-start.5 = (f32[8,4,128]{2,1,0:T(4,128)S(1)}, f32[8,4,128]{2,1,0:T(4,128)S(1)}, u32[]{:S(2)}, u32[]{:S(2)}) collective-permute-start(f32[8,4,128]{2,1,0:T(4,128)S(1)} %get-tuple-element.26), channel_id=1, source_target_pairs={{16,0},{32,16},{48,32},{64,48},{80,64},{96,80},{112,96},{17,1},{33... | collective-permute-start | bytes 49160 | tf_op jit(solution)/shard_map/ppermute | solution.py:429
  60.5 1.2 %copy-start = (f32[128,7,4,128]{3,2,1,0:T(4,128)}, f32[128,7,4,128]{3,2,1,0:T(4,128)S(1)}, u32[]{:S(2)}) copy-start(f32[128,7,4,128]{3,2,1,0:T(4,128)S(1)} %all-to-all-done) | copy-start | bytes 5505028
  64.7 21.6 %collective-permute-start.6 = (f32[4,4,384]{2,1,0:T(4,128)}, f32[4,4,384]{2,1,0:T(4,128)S(1)}, u32[]{:S(2)}, u32[]{:S(2)}) collective-permute-start(f32[4,4,384]{2,1,0:T(4,128)} %get-tuple-element.24), channel_id=1, source_target_pairs={{0,16},{16,32},{32,48},{48,64},{64,80},{80,96},{96,112},{1,17},{17... | collective-permute-start | bytes 73736 | tf_op jit(solution)/shard_map/ppermute | solution.py:434
  67.9 18.5 %collective-permute-start.7 = (f32[4,4,384]{2,1,0:T(4,128)}, f32[4,4,384]{2,1,0:T(4,128)S(1)}, u32[]{:S(2)}, u32[]{:S(2)}) collective-permute-start(f32[4,4,384]{2,1,0:T(4,128)} %get-tuple-element.25), channel_id=1, source_target_pairs={{16,0},{32,16},{48,32},{64,48},{80,64},{96,80},{112,96},{17,1},{33... | collective-permute-start | bytes 73736 | tf_op jit(solution)/shard_map/ppermute | solution.py:435
  69.8 4.5 %copy-start.9 = (f32[8,4,128]{2,1,0:T(4,128)}, f32[8,4,128]{2,1,0:T(4,128)S(1)}, u32[]{:S(2)}) copy-start(f32[8,4,128]{2,1,0:T(4,128)S(1)} %collective-permute-done.5.south_corner) | copy-start | bytes 49156
  69.8 4.5 %collective-permute-start.4 = (f32[8,4,128]{2,1,0:T(4,128)S(1)}, f32[8,4,128]{2,1,0:T(4,128)S(1)}, u32[]{:S(2)}, u32[]{:S(2)}) collective-permute-start(f32[8,4,128]{2,1,0:T(4,128)S(1)} %get-tuple-element.27), channel_id=1, source_target_pairs={{0,16},{16,32},{32,48},{48,64},{64,80},{80,96},{96,112},{1,17},{17... | collective-permute-start | bytes 49160 | tf_op jit(solution)/shard_map/ppermute | solution.py:428
  74.3 0.6 copy-start.10
  74.3 0.8 copy-start.1
  75.1 0.8 copy-start.2
  86.4 0.6 copy-start.7
  86.4 0.6 copy-start.8

commit v2 on v1

v2 whole, which is shorter than its diff:
```python
import functools

import jax
import jax.numpy as jnp
from jax import lax
from jax.experimental import pallas as pl
from jax.experimental.pallas import tpu as pltpu
from jax.sharding import PartitionSpec as P

SUBSTEPS = 2
CAP = 6
H = 4
CHUNKS = 12
OWN_ID = 64
NBR_ID = 72
MIB = 1024 * 1024

VMEM = pl.BlockSpec(memory_space=pltpu.VMEM)
SMEM = pl.BlockSpec(memory_space=pltpu.SMEM)
ANY = pl.BlockSpec(memory_space=pl.ANY)
F32 = jnp.float32
BF16 = jnp.bfloat16


def params(mib):
    return pltpu.CompilerParams(vmem_limit_bytes=mib * MIB)


def shaped(*shape):
    return jax.ShapeDtypeStruct(shape, F32)


def remap_kernel(
    n_ox, source, owner, block, owner_row, block_row, flux, weights,
    payload, held, flux32, table, strips, count, sem,
):
    links = weights.shape[0]
    per = links // CHUNKS
    copies = [
        pltpu.make_async_copy(
            weights.at[pl.ds(c * per, per)], held.at[pl.ds(c * per, per)], sem.at[c]
        )
        for c in range(CHUNKS)
    ]
    for copy in copies:
        copy.start()
    devices = payload.shape[0]
    flux32[...] = flux[...].astype(F32)

    owners = owner_row[...]
    blocks = block_row[...]
    tiles = lax.broadcasted_iota(jnp.int32, (devices, links), 0)
    mine = tiles == owners
    onehot = mine.astype(BF16)
    before = (
        lax.broadcasted_iota(jnp.int32, (links, links), 0)
        < lax.broadcasted_iota(jnp.int32, (links, links), 1)
    ).astype(BF16)
    ranks = jnp.dot(onehot, before, preferred_element_type=F32)
    rank = jnp.sum(jnp.where(mine, ranks, 0.0), axis=0, keepdims=True).astype(jnp.int32)
    odds = blocks & 1
    columns = lax.rem(owners, n_ox)
    nbrs = owners - columns + lax.rem(columns + jnp.where(odds == 1, 1, n_ox - 1), n_ox)
    entries = rank + jnp.where(odds == 1, 0, CAP)
    idents = (blocks + 1).astype(F32)
    spot = lax.broadcasted_iota(jnp.int32, (128, links), 0)
    across = (((1,), (1,)), ((), ()))
    table[...] = lax.dot_general(
        onehot,
        jnp.where(spot == OWN_ID + rank, idents, 0.0).astype(BF16),
        across,
        preferred_element_type=F32,
    ) + lax.dot_general(
        (tiles == nbrs).astype(BF16),
        jnp.where(spot == NBR_ID + entries, idents, 0.0).astype(BF16),
        across,
        preferred_element_type=F32,
    )

    def clear(i, carry):
        payload[i] = jnp.zeros(payload.shape[1:], F32)
        strips[i] = jnp.broadcast_to(table[pl.ds(i, 1), :], (4, 128))
        count[i] = 0
        return carry

    lax.fori_loop(0, devices, clear, 0, unroll=4)
    group = lax.broadcasted_iota(jnp.int32, (4, 128), 1) >> 2
    unroll = 16

    def links_of(start):
        waiting = []
        for j in range(unroll):
            k = start + j
            x = flux32[source[k]].astype(BF16)
            waiting.append(jnp.dot(x, held[k], preferred_element_type=F32))
        moves = []
        for j in range(unroll):
            k = start + j
            tile = owner[0, k]
            slot = count[tile]
            count[tile] = slot + 1
            payload[tile, slot] = waiting[j]
            odd = block[k] & 1
            column = lax.rem(tile, n_ox)
            nbr = tile - column + lax.rem(column + jnp.where(odd == 1, 1, n_ox - 1), n_ox)
            entry = slot + jnp.where(odd == 1, 0, CAP)
            moved = pltpu.roll(waiting[j], lax.rem(4 * entry + 4 * odd, 128), 1)
            moves.append((nbr, entry, moved))
        for nbr, entry, moved in moves:
            strips[nbr] = jnp.where(group == entry, moved, strips[nbr])

    for c in range(CHUNKS):
        copies[c].wait()

        def some(i, carry, c=c):
            links_of(c * per + i * unroll)
            return carry

        lax.fori_loop(0, per // unroll, some, 0)

    def finish(i, carry):
        payload[i, CAP] = strips[i]
        return carry

    lax.fori_loop(0, devices, finish, 0, unroll=8)


def remap(flux, weights, source, owner, block, devices, n_ox):
    links = weights.shape[0]
    owner = owner.T
    return pl.pallas_call(
        functools.partial(remap_kernel, n_ox),
        out_shape=shaped(devices, CAP + 1, 4, 128),
        in_specs=[SMEM, SMEM, SMEM, VMEM, VMEM, VMEM, ANY],
        out_specs=VMEM,
        scratch_shapes=[
            pltpu.VMEM((links, 128, 128), BF16),
            pltpu.VMEM(flux.shape, F32),
            pltpu.VMEM((devices, 128), F32),
            pltpu.VMEM((devices, 4, 128), F32),
            pltpu.SMEM((devices,), jnp.int32),
            pltpu.SemaphoreType.DMA((CHUNKS,)),
        ],
        compiler_params=params(60),
        name="remap",
    )(source, owner, block, owner, block.reshape(1, links), flux, weights)


def mix_kernel(
    tracers, diffusivity, viscosity, mask, count,
    base, response, weight, levels, west, east, top, bottom,
    ratios,
):
    nt, nl, rows, width = tracers.shape
    levels[...] = (count[...] * mask[...]).astype(F32)
    across = width // 128

    def tile(t, carry):
        r = pl.ds(pl.multiple_of((t // across) * 8, 8), 8)
        c = pl.ds(pl.multiple_of((t % across) * 128, 128), 128)
        depth = levels[r, c]
        nothing = jnp.zeros((8, 128), F32)
        ratio, upper, single = nothing, nothing, nothing
        values = [nothing] * nt
        for level in range(nl):
            if level < nl - 1:
                lower = jnp.where(level + 1 < depth, diffusivity[level, r, c], 0.0)
            else:
                lower = nothing
            inverse = 1.0 / (1.0 + upper + lower + upper * ratio)
            ratio = -lower * inverse
            ratios[level] = ratio
            for f in range(nt):
                values[f] = (tracers[f, level, r, c] + upper * values[f]) * inverse
                base[f, level, r, c] = values[f]
            single = inverse if level == 0 else (upper * single) * inverse
            response[level, r, c] = single
            weight[level, r, c] = jnp.where(level < depth, viscosity[level, r, c], 0.0)
            upper = lower
        for level in range(nl - 2, -1, -1):
            ratio = ratios[level]
            for f in range(nt):
                values[f] = base[f, level, r, c] - ratio * values[f]
                base[f, level, r, c] = values[f]
            single = response[level, r, c] - ratio * single
            response[level, r, c] = single
        return carry

    lax.fori_loop(0, rows // 8 * across, tile, 0)

    group = lax.broadcasted_iota(jnp.int32, (rows, 128), 1) >> 2
    planes = (nt + 2) * nl + 1
    for g in range(-(-planes // 32)):
        left = jnp.zeros((rows, 128), F32)
        right = jnp.zeros((rows, 128), F32)
        for s in range(min(32, planes - 32 * g)):
            p = 32 * g + s
            ref = plane_of(base, response, weight, levels, p)
            left = jnp.where(group == s, pltpu.roll(ref[:, 0:128], 4 * s, 1), left)
            right = jnp.where(
                group == s, pltpu.roll(ref[:, width - 128 : width], (4 * s + 4) % 128, 1), right
            )
            top[p] = ref[0:H, :]
            bottom[p] = ref[rows - H : rows, :]
        west[g] = left
        east[g] = right


def plane_of(base, response, weight, levels, p):
    nt, nl = base.shape[:2]
    if p < nt * nl:
        return base.at[p // nl, p % nl]
    if p < (nt + 1) * nl:
        return response.at[p - nt * nl]
    if p < (nt + 2) * nl:
        return weight.at[p - (nt + 1) * nl]
    return levels


def mix(tracers, diffusivity, viscosity, mask, count):
    nt, nl, rows, width = tracers.shape
    planes = (nt + 2) * nl + 1
    groups = -(-planes // 32)
    out = (
        shaped(nt, nl, rows, width),
        shaped(nl, rows, width),
        shaped(nl, rows, width),
        shaped(rows, width),
        shaped(groups, rows, 128),
        shaped(groups, rows, 128),
        shaped(planes + groups, H, width),
        shaped(planes + groups, H, width),
    )
    return pl.pallas_call(
        mix_kernel,
        out_shape=out,
        in_specs=[VMEM] * 5,
        out_specs=(VMEM,) * len(out),
        scratch_shapes=[pltpu.VMEM((nl, 8, 128), F32)],
        compiler_params=params(16),
        name="mix",
    )(tracers, diffusivity, viscosity, mask, count)


def middle(left, right, lane):
    return jnp.where(lane >= 64, left, right)


def spread_middle(mid, lane, nt):
    out = pltpu.roll(mid, 12, 1)
    for f in range(1, nt):
        out = jnp.where((lane >> 5) == f, pltpu.roll(mid, 32 * f + 12, 1), out)
    return out


def arrange_kernel(
    base, response, weight, levels,
    from_west, from_east, north, south,
    jobs, responses, weights, depth,
):
    nt, nl, rows, width = base.shape
    tall = rows + 2 * H
    planes = (nt + 2) * nl + 1
    lane = lax.broadcasted_iota(jnp.int32, (tall, 128), 1)

    def whole(p):
        g, s = p // 32, p % 32
        ref = plane_of(base, response, weight, levels, p)
        full = jnp.concatenate([ref[...], jnp.concatenate([south[p], north[p]], axis=0)], axis=0)
        corner = jnp.concatenate([south[planes + g], north[planes + g]], axis=0)
        west = jnp.concatenate([from_west[g], corner[:, 0:128]], axis=0)
        east = jnp.concatenate([from_east[g], corner[:, 128:256]], axis=0)
        left, right = full[:, 0:128], full[:, width - 128 : width]
        mid = middle(left, right, lane)
        left = jnp.where(lane >= 128 - H, pltpu.roll(west, (252 - 4 * s) % 128, 1), left)
        right = jnp.where(lane < H, pltpu.roll(east, (128 - 4 * s) % 128, 1), right)
        return left, right, mid

    half = nl - 16
    for level in range(nl):
        block, i = level // 8, level % 8
        packed = jnp.zeros((tall, 128), F32)
        for f in range(nt):
            left, right, mid = whole(f * nl + level)
            packed = jnp.where((lane >> 5) == f, pltpu.roll(mid, (32 * f + 12) % 128, 1), packed)
            if block < 2:
                group, place = 2 * f + block, i
            else:
                group, place = 8 + f // 2, (f % 2) * half + i
            jobs[3 + group, pl.ds(place * tall, tall), :] = left
            jobs[13 + group, pl.ds(place * tall, tall), :] = right
        jobs[block, pl.ds(i * tall, tall), :] = packed
        if block == 2:
            jobs[block, pl.ds((half + i) * tall, tall), :] = packed
        for q, out in ((nt, responses), (nt + 1, weights)):
            left, right, mid = whole(q * nl + level)
            spread = spread_middle(mid, lane, nt)
            for at in (level,) if block < 2 else (level, level + half):
                out[0, pl.ds(at * tall, tall), :] = spread
                out[1, pl.ds(at * tall, tall), :] = left
                out[2, pl.ds(at * tall, tall), :] = right
    left, right, mid = whole((nt + 2) * nl)
    depth[0] = spread_middle(mid, lane, nt)
    depth[1] = left
    depth[2] = right


def arrange(base, response, weight, levels, halo):
    nt, nl, rows, width = base.shape
    tall = rows + 2 * H
    out = (
        shaped(23, 8 * tall, 128),
        shaped(3, 24 * tall, 128),
        shaped(3, 24 * tall, 128),
        shaped(3, tall, 128),
    )
    return pl.pallas_call(
        arrange_kernel,
        out_shape=out,
        in_specs=[VMEM] * (4 + len(halo)),
        out_specs=(VMEM,) * 4,
        compiler_params=params(20),
        name="arrange",
    )(base, response, weight, levels, *halo)


def two(x):
    high = x.astype(jnp.bfloat16)
    return high, (x - high.astype(jnp.float32)).astype(jnp.bfloat16)


def collect_kernel(arrived, mask, ocean_flux, side, to_north, to_south):
    rows, width = mask.shape
    nt = ocean_flux.shape[0]
    stride = (CAP + 1) * nt
    devices = arrived.shape[0] // stride

    def slot(s):
        return jnp.concatenate(
            [arrived[pl.ds(s * nt + f, devices, stride=stride), :] for f in range(nt)], axis=1
        )

    idents = jnp.transpose(arrived[pl.ds(CAP * nt, devices, stride=stride), :]).astype(jnp.int32) - 1
    y = lax.broadcasted_iota(jnp.int32, (rows, devices), 0)
    places = jnp.concatenate([2 * y, 2 * y + 1], axis=0)
    total = jnp.zeros((2 * rows, nt * 128), jnp.float32)
    for s in range(CAP):
        pick = (places == idents[OWN_ID + s : OWN_ID + s + 1, :]).astype(jnp.bfloat16)
        for piece in two(slot(s)):
            total = total + jnp.dot(pick, piece, preferred_element_type=jnp.float32)
    keep = mask[...].astype(jnp.float32)
    main = []
    for f in range(nt):
        cells = slice(f * 128, (f + 1) * 128)
        main.append(jnp.concatenate([total[0:rows, cells], total[rows:, cells]], axis=1) * keep)
        ocean_flux[f] = main[f]
    pick = jnp.concatenate(
        [
            (y == (idents[NBR_ID + e : NBR_ID + e + 1, :] >> 1)).astype(jnp.bfloat16)
            for e in range(2 * CAP)
        ],
        axis=0,
    )
    high, low = two(slot(CAP))
    spread = jnp.dot(pick, high, preferred_element_type=jnp.float32) + jnp.dot(
        pick, low, preferred_element_type=jnp.float32
    )
    lane = lax.broadcasted_iota(jnp.int32, (rows, 128), 1)
    for f in range(nt):
        west = jnp.zeros((rows, 128), jnp.float32)
        east = jnp.zeros((rows, 128), jnp.float32)
        for e in range(CAP):
            part = spread[e * rows : (e + 1) * rows, f * 128 : (f + 1) * 128]
            west = west + pltpu.roll(part, (124 - 4 * e) % 128, 1)
            e = e + CAP
            part = spread[e * rows : (e + 1) * rows, f * 128 : (f + 1) * 128]
            east = east + pltpu.roll(part, (128 - 4 * e) % 128, 1)
        edge = jnp.where(lane < H, east, jnp.where(lane >= 128 - H, west, 0.0))
        side[f] = edge
        whole = jnp.concatenate([main[f], edge], axis=1)
        to_north[f] = whole[0:H]
        to_south[f] = whole[rows - H : rows]


def collect(arrived, mask, nt):
    rows, width = mask.shape
    f32 = jnp.float32
    line = jax.ShapeDtypeStruct((nt, H, width + 128), f32)
    return pl.pallas_call(
        collect_kernel,
        out_shape=(
            jax.ShapeDtypeStruct((nt, rows, width), f32),
            jax.ShapeDtypeStruct((nt, rows, 128), f32),
            line,
            line,
        ),
        in_specs=[VMEM] * 2,
        out_specs=(VMEM,) * 4,
        compiler_params=params(12),
        name="collect",
    )(arrived, mask)


def diffuse_kernel(
    jobs, responses, weights, depth, main, side, north, south,
    out, surface, start, done, merged, sem,
):
    nt, rows, width = main.shape
    tall = rows + 2 * H
    lane = lax.broadcasted_iota(jnp.int32, (tall, 128), 1)

    packed = jnp.zeros((tall, 128), F32)
    for f in range(nt):
        beyond = jnp.concatenate([south[f], north[f]], axis=0)
        left = jnp.concatenate([main[f, :, 0:128], beyond[:, 0:128]], axis=0)
        right = jnp.concatenate([main[f, :, 128:256], beyond[:, 128:256]], axis=0)
        edges = jnp.concatenate([side[f], beyond[:, 256:384]], axis=0)
        mid = middle(left, right, lane)
        packed = jnp.where((lane >> 5) == f, pltpu.roll(mid, (32 * f + 12) % 128, 1), packed)
        left = jnp.where(lane >= 128 - H, edges, left)
        right = jnp.where(lane < H, edges, right)
        surface[1, f] = jnp.where(depth[1] > 0.0, left, 0.0)
        surface[2, f] = jnp.where(depth[2] > 0.0, right, 0.0)
    surface[0, 0] = jnp.where(depth[0] > 0.0, packed, 0.0)

    sub = lax.broadcasted_iota(jnp.int32, (8, 128), 0)

    def row(y):
        return y if y >= 0 else y + tall

    def run(job, part, first, f0, f4):
        for i in range(8):
            at = pl.ds(i * tall, tall)
            beside = pl.ds(pl.multiple_of((first + i) * tall, 8), tall)
            start[at, :] = jobs[job, at, :] + responses[part, beside, :] * surface[
                part, f0 if i < 4 else f4
            ]
        level = (jnp.where(first == 16, sub & 3, sub) + first).astype(F32)

        def laplace(v, y):
            c = v[y]
            return (
                (v[y - 1] + v[y + 1]) + (pltpu.roll(c, 1, 1) + pltpu.roll(c, 127, 1))
            ) - 4.0 * c

        v, w, scaled, active = {}, {}, {}, {}
        for y in range(-H, rows + H):
            v[y] = start[pl.ds(row(y), 8, stride=tall), :]
            w[y] = weights[part, pl.ds(first * tall + row(y), 8, stride=tall), :]
            active[y] = level < depth[part, pl.ds(row(y), 1), :]
        now = v
        for substep in range(SUBSTEPS):
            out_of = 2 * substep + 1
            for y in range(-H + out_of, rows + H - out_of):
                scaled[substep, y] = w[y] * laplace(now, y)
            these = {y: scaled[substep, y] for y in range(-H + out_of, rows + H - out_of)}
            out_of += 1
            now = {
                y: now[y] - jnp.where(active[y], laplace(these, y), 0.0)
                for y in range(-H + out_of, rows + H - out_of)
            }
        for y in range(rows):
            done[job, pl.ds(y, 8, stride=rows), :] = now[y]

    def strips(m, carry):
        run(m, 0, 8 * m, 0, 0)
        return carry

    lax.fori_loop(0, 3, strips, 0)
    wide = lax.broadcasted_iota(jnp.int32, (rows, 128), 1)

    def send(group):
        if group < 8:
            return [(group // 2, 8 * (group % 2), 0, 8)]
        return [(2 * (group - 8), 16, 0, 4), (2 * (group - 8) + 1, 16, 4, 4)]

    def both(group, carry):
        last = group >= 8
        f0 = jnp.where(last, 2 * (group - 8), group // 2)
        f4 = jnp.where(last, f0 + 1, f0)
        first = jnp.where(last, 16, 8 * (group % 2))
        run(3 + group, 1, first, f0, f4)
        run(13 + group, 2, first, f0, f4)
        for i in range(8):
            f = f0 if i < 4 else f4
            at = pl.ds(i * rows, rows)
            strip = done[first // 8, at, :]
            turn = pltpu.roll(strip, lax.rem(244 - 32 * f, 128), 1)
            merged[group, i, :, 0:128] = jnp.where(wide < 120, done[3 + group, at, :], turn)
            turn = pltpu.roll(strip, lax.rem(244 - 32 * f, 128), 1)
            merged[group, i, :, 128:256] = jnp.where(wide >= 8, done[13 + group, at, :], turn)
        return carry

    def copies(group):
        return [
            pltpu.make_async_copy(
                merged.at[group, pl.ds(i, n)], out.at[f, pl.ds(level, n)], sem.at[group, k]
            )
            for k, (f, level, i, n) in enumerate(send(group))
        ]

    for group in range(10):
        both(jnp.int32(group), 0)
        for copy in copies(group):
            copy.start()
    for group in range(10):
        for copy in copies(group):
            copy.wait()


def diffuse(jobs, responses, weights, depth, main, side, north, south, nl):
    nt, rows, width = main.shape
    tall = rows + 2 * H
    return pl.pallas_call(
        diffuse_kernel,
        out_shape=shaped(nt, nl, rows, width),
        in_specs=[VMEM] * 8,
        out_specs=ANY,
        scratch_shapes=[
            pltpu.VMEM((3, nt, tall, 128), F32),
            pltpu.VMEM((8 * tall, 128), F32),
            pltpu.VMEM((23, 8 * rows, 128), F32),
            pltpu.VMEM((10, 8, rows, width), F32),
            pltpu.SemaphoreType.DMA((10, 2)),
        ],
        compiler_params=params(24),
        name="diffuse",
    )(jobs, responses, weights, depth, main, side, north, south)


def body(
    atm_flux,
    remap_weights,
    link_source,
    link_owner,
    link_block,
    ocean_mask,
    level_count,
    tracers,
    diffusivity,
    viscosity,
):
    n_oy = lax.axis_size("oy")
    n_ox = lax.axis_size("ox")
    devices = n_oy * n_ox
    nt, nl, rows, width = tracers.shape
    payload = remap(
        atm_flux, remap_weights, link_source, link_owner, link_block, devices, n_ox
    )
    arrived = lax.all_to_all(payload, ("oy", "ox"), split_axis=0, concat_axis=0, tiled=True)
    arrived = arrived.reshape(devices * (CAP + 1) * nt, 128)

    def moved(x, dy, dx):
        pairs = []
        for i in range(n_oy):
            for j in range(n_ox):
                if 0 <= i + dy < n_oy:
                    pairs.append((i * n_ox + j, (i + dy) * n_ox + (j + dx) % n_ox))
        return lax.ppermute(x, ("oy", "ox"), pairs)

    base, response, weight, levels, west, east, top, bottom = mix(
        tracers, diffusivity, viscosity, ocean_mask, level_count
    )
    from_west = moved(east, 0, 1)
    from_east = moved(west, 0, -1)

    def with_corners(line, first):
        corners = jnp.concatenate(
            [from_west[:, first : first + H], from_east[:, first : first + H]], axis=2
        )
        return lax.dynamic_update_slice(line, corners, (line.shape[0] - corners.shape[0], 0, 0))

    north = moved(with_corners(bottom, rows - H), 1, 0)
    south = moved(with_corners(top, 0), -1, 0)
    halo = (from_west, from_east, north, south)
    tiles = arrange(base, response, weight, levels, halo)

    ocean_flux, side, to_north, to_south = collect(arrived, ocean_mask, nt)
    flux_north = moved(to_south, 1, 0)
    flux_south = moved(to_north, -1, 0)
    mixed = diffuse(*tiles, ocean_flux, side, flux_north, flux_south, nl)
    return mixed, ocean_flux


def solution(mesh):
    placed = (
        P(("oy", "ox"), None, None),
        P(("oy", "ox"), None, None),
        P(("oy", "ox")),
        P(("oy", "ox"), None),
        P(("oy", "ox")),
        P("oy", "ox"),
        P("oy", "ox"),
        P(None, None, "oy", "ox"),
        P(None, "oy", "ox"),
        P(None, "oy", "ox"),
    )
    return jax.shard_map(
        body,
        mesh=mesh,
        in_specs=placed,
        out_specs=(P(None, None, "oy", "ox"), P(None, "oy", "ox")),
        check_vma=False,
    )
```

time: 111 us -> 81.1 us (0.73)
  Pallas kernels: 57.5 us -> 30.2 us
  starting transfers between devices: 33.8 us -> 27.8 us
  local copies, waits for them, and re-layouts: 3.43 us -> 8.41 us
  other arithmetic: 3.4 us -> 1.22 us
    pallas_call x4, Pallas kernels: 54.5 us -> 29.1 us  [the longest x1 11.5 us: remap(): pl.pallas_call(functools.partial(remap_kernel, n_ox), out_shape=shaped(de...]
    ppermute x8 -> x6, starting transfers between devices: 22.3 us -> 16.3 us  [moved(): return lax.ppermute(x, ('oy', 'ox'), pairs)]
    unnamed x23 -> x16, local copies, waits for them, and re-layouts: 3.42 us -> 7.16 us
    convert_element_type x2 -> x0, other arithmetic: 2.13 us -> none  [the longest x1 1.51 us: body(): atm_flux.astype(jnp.float32)]
    pallas_call x1, Pallas kernels: 3 us -> 1.12 us  [collect(): pl.pallas_call(collect_kernel, out_shape=(jax.ShapeDtypeStruct((nt, rows,...]
    unnamed x1 -> x0, other arithmetic: 1.27 us -> none
    reshape x0 -> x1, local copies, waits for them, and re-layouts: none -> 1.25 us  [remap(): block.reshape(1, links)]
    dynamic_update_slice x0 -> x2, other arithmetic: none -> 1.22 us  [with_corners(): lax.dynamic_update_slice(line, corners, (line.shape[0] - corners.shape[0]...]
  transfers between devices with their start and end apart: 9 -> 7, of which waited for: 3 -> 2; matrix products, arithmetic and copies ran while one was open for 1% -> 2% of each run, Pallas kernels for 16% -> 11%
where the time goes in v2:
time: 81.1 us; the launch traced here: 80.4 us
  Pallas kernels  30.2 us (37%)
  starting transfers between devices  27.8 us (34%)
  waiting for transfers between devices  11.8 us (15%)
  local copies, waits for them, and re-layouts  8.41 us (10%)
  other arithmetic  1.22 us (2%)
  between operations  0.95 us (1%)
    ppermute x6, starting transfers between devices, moved(): return lax.ppermute(x, ('oy', 'ox'), pairs)  16.3 us
    ppermute x6, waiting for transfers between devices, moved(): return lax.ppermute(x, ('oy', 'ox'), pairs)  11.8 us
    pallas_call x1, Pallas kernels, remap(): pl.pallas_call(functools.partial(remap_kernel, n_ox), out_shape=shaped(de...  11.5 us
    all_to_all x1, starting transfers between devices, body(): lax.all_to_all(payload, ('oy', 'ox'), split_axis=0, concat_axis=0, tiled=...  11.5 us
    pallas_call x1, Pallas kernels, diffuse(): pl.pallas_call(diffuse_kernel, out_shape=shaped(nt, nl, rows, width), in_...  9.5 us
    unnamed x16, local copies, waits for them, and re-layouts  7.16 us
    pallas_call x1, Pallas kernels, mix(): pl.pallas_call(mix_kernel, out_shape=out, in_specs=[VMEM] * 5, out_specs=...  4.25 us
    pallas_call x1, Pallas kernels, arrange(): pl.pallas_call(arrange_kernel, out_shape=out, in_specs=[VMEM] * (4 + len(...  3.81 us
  transfers between devices with their start and end apart: 7, of which 2 were waited for; matrix products, arithmetic and copies ran while one was open for 2% of the time, Pallas kernels for 11%

profile of v2, /device:TPU:1, one launch (start us, length us, event | category | flops | bytes accessed | tf_op | source)
XLA Modules:
  0.0 80.4 jit_solution(14068531317397338611)
XLA Ops:
  0.6 1.2 %reshape.10.block_row = s32[1,384]{1,0:T(1,128)} reshape(s32[384]{0:T(512)} %block.1) | data formatting | bytes 3072 | tf_op jit(solution)/shard_map/reshape | solution.py:146
  1.9 11.5 %remap.1 = f32[128,7,4,128]{3,2,1,0:T(4,128)} custom-call(s32[384]{0:T(512)} %source.1, s32[1,384]{1,0:T(1,128)} %bitcast.3, s32[384]{0:T(512)} %block.1, s32[1,384]{1,0:T(1,128)} %bitcast.4, s32[1,384]{1,0:T(1,128)} %reshape.10.block_row, bf16[64,4,128]{2,1,0:T(4,128)(2,1)} %flux.1, bf16[384,128,128]{2,1,0:T(8,128)(2,1)} %weights.1), custom_call_target="tpu_custom_call" | custom-call | tf_op jit(solution)/shard_map/remap/pallas_call | solution.py:131
  13.4 0.0 copy-start.6
  13.4 0.0 copy-start.7
  13.4 11.5 %all-to-all-start = ((f32[128,7,4,128]{3,2,1,0:T(4,128)}), f32[128,7,4,128]{3,2,1,0:T(4,128)S(1)}, u32[]{:S(2)}, u32[]{:S(2)}) async-start(f32[128,7,4,128]{3,2,1,0:T(4,128)} %remap.1), calls=%async_computation | async-start | bytes 3670016 | tf_op jit(solution)/shard_map/all_to_all | solution.py:550
  24.9 0.0 copy-done.6
  24.9 0.0 copy-done.7
  24.9 0.0 copy-start.2
  25.0 1.7 %copy-done.2 = f32[4,20,32,256]{3,2,1,0:T(8,128)S(1)} copy-done((f32[4,20,32,256]{3,2,1,0:T(8,128)S(1)}, f32[4,20,32,256]{3,2,1,0:T(8,128)}, u32[]{:S(2)}) %copy-start.2) | copy-done | bytes 2621464
  26.7 0.0 copy-start.3
  26.7 1.1 %copy-done.3 = f32[20,32,256]{2,1,0:T(8,128)S(1)} copy-done((f32[20,32,256]{2,1,0:T(8,128)S(1)}, f32[20,32,256]{2,1,0:T(8,128)}, u32[]{:S(2)}) %copy-start.3) | copy-done | bytes 655384
  27.8 0.0 copy-start.4
  27.8 1.1 %copy-done.4 = f32[20,32,256]{2,1,0:T(8,128)S(1)} copy-done((f32[20,32,256]{2,1,0:T(8,128)S(1)}, f32[20,32,256]{2,1,0:T(8,128)}, u32[]{:S(2)}) %copy-start.4) | copy-done | bytes 655384
  28.9 4.3 %mix.1 = (f32[4,20,32,256]{3,2,1,0:T(8,128)S(1)}, f32[20,32,256]{2,1,0:T(8,128)S(1)}, f32[20,32,256]{2,1,0:T(8,128)S(1)}, f32[32,256]{1,0:T(8,128)S(1)}, f32[4,3...) custom-call(f32[4,20,32,256]{3,2,1,0:T(8,128)S(1)} %copy-done.2, ...), custom_call_target="tpu_custom_call" | custom-call | tf_op jit(solution)/shard_map/mix/pallas_call | solution.py:234
  33.1 0.0 copy-start
  33.1 1.5 %copy-done = f32[4,20,32,256]{3,2,1,0:T(8,128)} copy-done((f32[4,20,32,256]{3,2,1,0:T(8,128)}, f32[4,20,32,256]{3,2,1,0:T(8,128)S(1)}, u32[]{:S(2)}) %copy-start) | copy-done | bytes 2621464
  34.6 1.5 %collective-permute-start = (f32[4,32,128]{2,1,0:T(8,128)S(1)}, f32[4,32,128]{2,1,0:T(8,128)S(1)}, u32[]{:S(2)}, u32[]{:S(2)}) collective-permute-start(f32[4,32,128]{2,1,0:T(8,128)S(1)} %get-tuple-element.22), channel_id=1, source_target_pairs={{0,1},{1,2},{2,3},{3,4},{4,5},{5,6},{6,7},{7,8},{8,9},{9,10},{10,1... | collective-permute-start | bytes 196616 | tf_op jit(solution)/shard_map/ppermute | solution.py:559
  36.1 4.1 %collective-permute-start.1 = (f32[4,32,128]{2,1,0:T(8,128)S(1)}, f32[4,32,128]{2,1,0:T(8,128)S(1)}, u32[]{:S(2)}, u32[]{:S(2)}) collective-permute-start(f32[4,32,128]{2,1,0:T(8,128)S(1)} %get-tuple-element.23), channel_id=1, source_target_pairs={{0,15},{1,0},{2,1},{3,2},{4,3},{5,4},{6,5},{7,6},{8,7},{9,8},{10,9... | collective-permute-start | bytes 196616 | tf_op jit(solution)/shard_map/ppermute | solution.py:559
  40.2 11.1 %collective-permute-done.from_west = f32[4,32,128]{2,1,0:T(8,128)S(1)} collective-permute-done((f32[4,32,128]{2,1,0:T(8,128)S(1)}, f32[4,32,128]{2,1,0:T(8,128)S(1)}, u32[]{:S(2)}, u32[]{:S(2)}) %collective-permute-start) | collective-permute-done | bytes 65568 | tf_op jit(solution)/shard_map/ppermute | solution.py:559
  51.3 0.0 collective-permute-done.1.from_east
  51.3 0.6 maximum_dynamic-update-slice_fusion.1
  51.9 3.2 %collective-permute-start.3 = (f32[125,4,256]{2,1,0:T(4,128)}, f32[125,4,256]{2,1,0:T(4,128)}, u32[]{:S(2)}, u32[]{:S(2)}) collective-permute-start(f32[125,4,256]{2,1,0:T(4,128)} %maximum_dynamic-update-slice_fusion.1), channel_id=1, source_target_pairs={{16,0},{17,1},{18,2},{19,3},{20,4},{21,5},{22,6},{23,7},{24,8},{25... | collective-permute-start | bytes 1536008 | tf_op jit(solution)/shard_map/ppermute | solution.py:559
  55.2 0.6 maximum_dynamic-update-slice_fusion
  55.8 3.1 %collective-permute-start.2 = (f32[125,4,256]{2,1,0:T(4,128)}, f32[125,4,256]{2,1,0:T(4,128)}, u32[]{:S(2)}, u32[]{:S(2)}) collective-permute-start(f32[125,4,256]{2,1,0:T(4,128)} %maximum_dynamic-update-slice_fusion), channel_id=1, source_target_pairs={{0,16},{1,17},{2,18},{3,19},{4,20},{5,21},{6,22},{7,23},{8,24},{9,... | collective-permute-start | bytes 1536008 | tf_op jit(solution)/shard_map/ppermute | solution.py:559
  58.8 0.0 all-to-all-done
  58.8 1.1 %collect.1 = (f32[4,32,256]{2,1,0:T(8,128)}, f32[4,32,128]{2,1,0:T(8,128)S(1)}, f32[4,4,384]{2,1,0:T(4,128)S(1)}, f32[4,4,384]{2,1,0:T(4,128)S(1)}) custom-call(f32[3584,128]{1,0:T(8,128)S(1)} %bitcast.2, s32[32,256]{1,0:T(8,128)S(1)} %copy-done.6), custom_call_target="tpu_custom_call" | custom-call | tf_op jit(solution)/shard_map/collect/pallas_call | solution.py:389
  60.0 2.4 %collective-permute-start.4 = (f32[4,4,384]{2,1,0:T(4,128)S(1)}, f32[4,4,384]{2,1,0:T(4,128)S(1)}, u32[]{:S(2)}, u32[]{:S(2)}) collective-permute-start(f32[4,4,384]{2,1,0:T(4,128)S(1)} %get-tuple-element.32), channel_id=1, source_target_pairs={{0,16},{1,17},{2,18},{3,19},{4,20},{5,21},{6,22},{7,23},{8,24},{9,... | collective-permute-start | bytes 73736 | tf_op jit(solution)/shard_map/ppermute | solution.py:559
  62.4 2.1 %collective-permute-start.5 = (f32[4,4,384]{2,1,0:T(4,128)S(1)}, f32[4,4,384]{2,1,0:T(4,128)S(1)}, u32[]{:S(2)}, u32[]{:S(2)}) collective-permute-start(f32[4,4,384]{2,1,0:T(4,128)S(1)} %get-tuple-element.33), channel_id=1, source_target_pairs={{16,0},{17,1},{18,2},{19,3},{20,4},{21,5},{22,6},{23,7},{24,8},{25... | collective-permute-start | bytes 73736 | tf_op jit(solution)/shard_map/ppermute | solution.py:559
  64.5 0.0 collective-permute-done.3.south
  64.5 0.6 collective-permute-done.2.north
  65.1 0.0 copy-start.1
  65.1 1.7 %copy-done.1 = f32[4,20,32,256]{3,2,1,0:T(8,128)S(1)} copy-done((f32[4,20,32,256]{3,2,1,0:T(8,128)S(1)}, f32[4,20,32,256]{3,2,1,0:T(8,128)}, u32[]{:S(2)}) %copy-start.1) | copy-done | bytes 2621464
  66.9 0.0 copy-start.5
  66.9 3.8 %arrange.1 = (f32[23,320,128]{2,1,0:T(8,128)S(1)}, f32[3,960,128]{2,1,0:T(8,128)S(1)}, f32[3,960,128]{2,1,0:T(8,128)S(1)}, f32[3,40,128]{2,1,0:T(8,128)S(1)}) custom-call(f32[4,20,32,256]{3,2,1,0:T(8,128)S(1)} %copy-done.1, f32[20,32,256]{2,1,0:T(8,128)S(1)} %get-tuple-element.19.response, f32[20,32,256]{2,1,0:T(8,128)S(1)} %get-tuple-element.20.weight, ...), custom_call_target="tpu_custom_call" | custom-call | tf_op jit(solution)/shard_map/arrange/pallas_call | solution.py:317
  70.7 0.0 collective-permute-done.4.north
  70.7 0.0 collective-permute-done.5.south
  70.7 0.0 copy-done.5
  70.7 9.5 %diffuse.1 = f32[4,20,32,256]{3,2,1,0:T(8,128)} custom-call(f32[23,320,128]{2,1,0:T(8,128)S(1)} %get-tuple-element.26.jobs, f32[3,960,128]{2,1,0:T(8,128)S(1)} %get-tuple-element.27.responses, f32[3,960,128]{2,1,0:T(8,128)S(1)} %get-tuple-element.28.weights, f32[3,40,128]{2,1,0:T(8,128)S(1)} %get-tuple-element.29.depth, f32[4,32,256]{2,1,0:T(8,128)S(1)} %copy-done.5, ...), custom_call_target="tpu_custom_call" | custom-call | tf_op jit(solution)/shard_map/diffuse/pallas_call | solution.py:514
  (2 shorter events, 0.0 us)
Async XLA Ops:
  13.4 11.5 %copy-start.6 = (s32[32,256]{1,0:T(8,128)S(1)}, s32[32,256]{1,0:T(8,128)}, u32[]{:S(2)}) copy-start(s32[32,256]{1,0:T(8,128)} %mask.3) | copy-start | bytes 98308
  13.4 11.5 %copy-start.7 = (s32[32,256]{1,0:T(8,128)S(1)}, s32[32,256]{1,0:T(8,128)}, u32[]{:S(2)}) copy-start(s32[32,256]{1,0:T(8,128)} %count.1) | copy-start | bytes 98308
  13.4 45.4 %all-to-all-start = ((f32[128,7,4,128]{3,2,1,0:T(4,128)}), f32[128,7,4,128]{3,2,1,0:T(4,128)S(1)}, u32[]{:S(2)}, u32[]{:S(2)}) async-start(f32[128,7,4,128]{3,2,1,0:T(4,128)} %remap.1), calls=%async_computation | async-start | bytes 3670016 | tf_op jit(solution)/shard_map/all_to_all | solution.py:550
  24.9 1.7 %copy-start.2 = (f32[4,20,32,256]{3,2,1,0:T(8,128)S(1)}, f32[4,20,32,256]{3,2,1,0:T(8,128)}, u32[]{:S(2)}) copy-start(f32[4,20,32,256]{3,2,1,0:T(8,128)} %tracers.1) | copy-start | bytes 7864324
  26.7 1.1 %copy-start.3 = (f32[20,32,256]{2,1,0:T(8,128)S(1)}, f32[20,32,256]{2,1,0:T(8,128)}, u32[]{:S(2)}) copy-start(f32[20,32,256]{2,1,0:T(8,128)} %diffusivity.1) | copy-start | bytes 1966084
  27.8 1.1 %copy-start.4 = (f32[20,32,256]{2,1,0:T(8,128)S(1)}, f32[20,32,256]{2,1,0:T(8,128)}, u32[]{:S(2)}) copy-start(f32[20,32,256]{2,1,0:T(8,128)} %viscosity.1) | copy-start | bytes 1966084
  33.1 1.5 %copy-start = (f32[4,20,32,256]{3,2,1,0:T(8,128)}, f32[4,20,32,256]{3,2,1,0:T(8,128)S(1)}, u32[]{:S(2)}) copy-start(f32[4,20,32,256]{3,2,1,0:T(8,128)S(1)} %get-tuple-element.18.base) | copy-start | bytes 7864324
  34.6 16.7 %collective-permute-start = (f32[4,32,128]{2,1,0:T(8,128)S(1)}, f32[4,32,128]{2,1,0:T(8,128)S(1)}, u32[]{:S(2)}, u32[]{:S(2)}) collective-permute-start(f32[4,32,128]{2,1,0:T(8,128)S(1)} %get-tuple-element.22), channel_id=1, source_target_pairs={{0,1},{1,2},{2,3},{3,4},{4,5},{5,6},{6,7},{7,8},{8,9},{9,10},{10,1... | collective-permute-start | bytes 196616 | tf_op jit(solution)/shard_map/ppermute | solution.py:559
  36.1 15.2 %collective-permute-start.1 = (f32[4,32,128]{2,1,0:T(8,128)S(1)}, f32[4,32,128]{2,1,0:T(8,128)S(1)}, u32[]{:S(2)}, u32[]{:S(2)}) collective-permute-start(f32[4,32,128]{2,1,0:T(8,128)S(1)} %get-tuple-element.23), channel_id=1, source_target_pairs={{0,15},{1,0},{2,1},{3,2},{4,3},{5,4},{6,5},{7,6},{8,7},{9,8},{10,9... | collective-permute-start | bytes 196616 | tf_op jit(solution)/shard_map/ppermute | solution.py:559
  51.9 12.5 %collective-permute-start.3 = (f32[125,4,256]{2,1,0:T(4,128)}, f32[125,4,256]{2,1,0:T(4,128)}, u32[]{:S(2)}, u32[]{:S(2)}) collective-permute-start(f32[125,4,256]{2,1,0:T(4,128)} %maximum_dynamic-update-slice_fusion.1), channel_id=1, source_target_pairs={{16,0},{17,1},{18,2},{19,3},{20,4},{21,5},{22,6},{23,7},{24,8},{25... | collective-permute-start | bytes 1536008 | tf_op jit(solution)/shard_map/ppermute | solution.py:559
  55.8 9.3 %collective-permute-start.2 = (f32[125,4,256]{2,1,0:T(4,128)}, f32[125,4,256]{2,1,0:T(4,128)}, u32[]{:S(2)}, u32[]{:S(2)}) collective-permute-start(f32[125,4,256]{2,1,0:T(4,128)} %maximum_dynamic-update-slice_fusion), channel_id=1, source_target_pairs={{0,16},{1,17},{2,18},{3,19},{4,20},{5,21},{6,22},{7,23},{8,24},{9,... | collective-permute-start | bytes 1536008 | tf_op jit(solution)/shard_map/ppermute | solution.py:559
  60.0 10.7 %collective-permute-start.4 = (f32[4,4,384]{2,1,0:T(4,128)S(1)}, f32[4,4,384]{2,1,0:T(4,128)S(1)}, u32[]{:S(2)}, u32[]{:S(2)}) collective-permute-start(f32[4,4,384]{2,1,0:T(4,128)S(1)} %get-tuple-element.32), channel_id=1, source_target_pairs={{0,16},{1,17},{2,18},{3,19},{4,20},{5,21},{6,22},{7,23},{8,24},{9,... | collective-permute-start | bytes 73736 | tf_op jit(solution)/shard_map/ppermute | solution.py:559
  62.4 8.3 %collective-permute-start.5 = (f32[4,4,384]{2,1,0:T(4,128)S(1)}, f32[4,4,384]{2,1,0:T(4,128)S(1)}, u32[]{:S(2)}, u32[]{:S(2)}) collective-permute-start(f32[4,4,384]{2,1,0:T(4,128)S(1)} %get-tuple-element.33), channel_id=1, source_target_pairs={{16,0},{17,1},{18,2},{19,3},{20,4},{21,5},{22,6},{23,7},{24,8},{25... | collective-permute-start | bytes 73736 | tf_op jit(solution)/shard_map/ppermute | solution.py:559
  65.1 1.7 %copy-start.1 = (f32[4,20,32,256]{3,2,1,0:T(8,128)S(1)}, f32[4,20,32,256]{3,2,1,0:T(8,128)}, u32[]{:S(2)}) copy-start(f32[4,20,32,256]{3,2,1,0:T(8,128)} %copy-done) | copy-start | bytes 7864324
  66.9 3.8 %copy-start.5 = (f32[4,32,256]{2,1,0:T(8,128)S(1)}, f32[4,32,256]{2,1,0:T(8,128)}, u32[]{:S(2)}) copy-start(f32[4,32,256]{2,1,0:T(8,128)} %get-tuple-element.17.main) | copy-start | bytes 393220

commit v3 on v1

v3 whole, which is shorter than its diff:
```python
import functools

import jax
import jax.numpy as jnp
from jax import lax
from jax.experimental import pallas as pl
from jax.experimental.pallas import tpu as pltpu
from jax.sharding import PartitionSpec as P

SUBSTEPS = 2
CAP = 6
H = 4
CHUNKS = 12
OWN_ID = 64
NBR_ID = 72
MIB = 1024 * 1024
PITCH = 40
MIX_MIB, ARRANGE_MIB, DIFFUSE_MIB = 60, 16, 24

VMEM = pl.BlockSpec(memory_space=pltpu.VMEM)
SMEM = pl.BlockSpec(memory_space=pltpu.SMEM)
ANY = pl.BlockSpec(memory_space=pl.ANY)
HBM = pl.BlockSpec(memory_space=pltpu.HBM)
F32 = jnp.float32
BF16 = jnp.bfloat16


def params(mib):
    return pltpu.CompilerParams(vmem_limit_bytes=mib * MIB)


def shaped(*shape):
    return jax.ShapeDtypeStruct(shape, F32)


def remap_kernel(
    n_ox, source, owner_row, block_row, flux, weights,
    payload, held, flux32, table, strips, codes, places, sem, sent,
):
    links = weights.shape[0]
    per = links // CHUNKS
    copies = [
        pltpu.make_async_copy(
            weights.at[pl.ds(c * per, per)], held.at[pl.ds(c * per, per)], sem.at[c]
        )
        for c in range(CHUNKS)
    ]
    for copy in copies:
        copy.start()
    devices = payload.shape[0]

    owners = owner_row[...]
    blocks = block_row[...].reshape(1, links)
    tiles = lax.broadcasted_iota(jnp.int32, (devices, links), 0)
    mine = tiles == owners
    onehot = mine.astype(BF16)
    before = (
        lax.broadcasted_iota(jnp.int32, (links, links), 0)
        < lax.broadcasted_iota(jnp.int32, (links, links), 1)
    ).astype(BF16)
    ranks = jnp.dot(onehot, before, preferred_element_type=F32)
    rank = jnp.sum(jnp.where(mine, ranks, 0.0), axis=0, keepdims=True).astype(jnp.int32)
    odds = blocks & 1
    columns = lax.rem(owners, n_ox)
    nbrs = owners - columns + lax.rem(columns + jnp.where(odds == 1, 1, n_ox - 1), n_ox)
    entries = rank + jnp.where(odds == 1, 0, CAP)
    codes[0:1, :] = owners
    codes[1:2, :] = rank
    codes[2:3, :] = nbrs
    codes[3:4, :] = entries
    codes[4:5, :] = (4 * entries + 4 * odds) & 127
    send = pltpu.make_async_copy(codes, places, sent)
    send.start()
    flux32[...] = flux[...].astype(F32)

    idents = (blocks + 1).astype(F32)
    spot = lax.broadcasted_iota(jnp.int32, (128, links), 0)
    across = (((1,), (1,)), ((), ()))
    table[...] = lax.dot_general(
        onehot,
        jnp.where(spot == OWN_ID + rank, idents, 0.0).astype(BF16),
        across,
        preferred_element_type=F32,
    ) + lax.dot_general(
        (tiles == nbrs).astype(BF16),
        jnp.where(spot == NBR_ID + entries, idents, 0.0).astype(BF16),
        across,
        preferred_element_type=F32,
    )

    def clear(i, carry):
        payload[i] = jnp.zeros(payload.shape[1:], F32)
        strips[i] = jnp.broadcast_to(table[pl.ds(i, 1), :], (4, 128))
        return carry

    lax.fori_loop(0, devices, clear, 0, unroll=4)
    send.wait()
    group = lax.broadcasted_iota(jnp.int32, (4, 128), 1) >> 2

    for c in range(CHUNKS):
        copies[c].wait()

        def chunk(_, carry, c=c):
            values, moves = [], []
            for k in range(c * per, (c + 1) * per, 2):
                two_x = jnp.concatenate([flux32[source[k]], flux32[source[k + 1]]], axis=0)
                two_w = jnp.concatenate([held[k], held[k + 1]], axis=1)
                product = jnp.dot(two_x.astype(BF16), two_w, preferred_element_type=F32)
                values += [(k, product[0:4, 0:128]), (k + 1, product[4:8, 128:256])]
            for k, value in values:
                payload[places[0, k], places[1, k]] = value
                moves.append((k, pltpu.roll(value, places[4, k], 1)))
            for k, moved in moves:
                nbr = places[2, k]
                strips[nbr] = jnp.where(group == places[3, k], moved, strips[nbr])
            return carry

        chunk(0, 0)

    def finish(i, carry):
        payload[i, CAP] = strips[i]
        return carry

    lax.fori_loop(0, devices, finish, 0, unroll=8)


def remap(flux, weights, source, owner, block, devices, n_ox):
    links = weights.shape[0]
    return pl.pallas_call(
        functools.partial(remap_kernel, n_ox),
        out_shape=shaped(devices, CAP + 1, 4, 128),
        in_specs=[SMEM, VMEM, VMEM, VMEM, ANY],
        out_specs=VMEM,
        scratch_shapes=[
            pltpu.VMEM((links, 128, 128), BF16),
            pltpu.VMEM(flux.shape, F32),
            pltpu.VMEM((devices, 128), F32),
            pltpu.VMEM((devices, 4, 128), F32),
            pltpu.VMEM((8, links), jnp.int32),
            pltpu.SMEM((8, links), jnp.int32),
            pltpu.SemaphoreType.DMA((CHUNKS,)),
            pltpu.SemaphoreType.DMA,
        ],
        compiler_params=params(60),
        name="remap",
    )(source, owner.T, block, flux, weights)


def job_place(f, level, nl):
    if level < 16:
        return 2 * f + level // 8, level % 8
    return 8 + f // 2, (f % 2) * (nl - 16) + level - 16


def level_places(level, nl):
    return (level,) if level < 16 else (level, level + nl - 16)


def middle(left, right, lane):
    return jnp.where(lane >= 64, left, right)


def spread_middle(mid, lane, nt):
    out = pltpu.roll(mid, 12, 1)
    for f in range(1, nt):
        out = jnp.where((lane >> 5) == f, pltpu.roll(mid, 32 * f + 12, 1), out)
    return out


def pack_middle(mids, lane):
    out = pltpu.roll(mids[0], 12, 1)
    for f in range(1, len(mids)):
        out = jnp.where((lane >> 5) == f, pltpu.roll(mids[f], 32 * f + 12, 1), out)
    return out


def mix_kernel(
    tracers, diffusivity, viscosity, mask, count,
    mids, sides, responses, weights, depth, west, east, top, bottom,
    ratios,
):
    nt, nl, rows, width = tracers.shape
    levels = (count[...] * mask[...]).astype(F32)
    lane = lax.broadcasted_iota(jnp.int32, (rows, 128), 1)
    depth[1] = levels[:, 0:128]
    depth[2] = levels[:, 128:256]
    depth[0] = spread_middle(middle(levels[:, 0:128], levels[:, 128:256], lane), lane, nt)
    across = width // 128

    def tile(t, carry):
        first = pl.multiple_of((t // across) * 8, 8)
        half = t % across
        r = pl.ds(first, 8)
        c = pl.ds(pl.multiple_of(half * 128, 128), 128)

        def plane(f, level):
            group, place = job_place(f, level, nl)
            return 10 * half + group, pl.ds(first + place * rows, 8)

        bottomless = depth[1 + half, r, :]
        nothing = jnp.zeros((8, 128), F32)
        ratio, upper, single = nothing, nothing, nothing
        values = [nothing] * nt
        for level in range(nl):
            if level < nl - 1:
                lower = jnp.where(level + 1 < bottomless, diffusivity[level, r, c], 0.0)
            else:
                lower = nothing
            inverse = 1.0 / (1.0 + upper + lower + upper * ratio)
            ratio = -lower * inverse
            ratios[level] = ratio
            for f in range(nt):
                values[f] = (tracers[f, level, r, c] + upper * values[f]) * inverse
                at = plane(f, level)
                sides[at[0], at[1], :] = values[f]
            single = inverse if level == 0 else (upper * single) * inverse
            weight = jnp.where(level < bottomless, viscosity[level, r, c], 0.0)
            for place in level_places(level, nl):
                responses[1 + half, pl.ds(first + place * rows, 8), :] = single
                weights[1 + half, pl.ds(first + place * rows, 8), :] = weight
            upper = lower
        for level in range(nl - 2, -1, -1):
            ratio = ratios[level]
            for f in range(nt):
                at = plane(f, level)
                values[f] = sides[at[0], at[1], :] - ratio * values[f]
                sides[at[0], at[1], :] = values[f]
            single = responses[1 + half, pl.ds(first + level * rows, 8), :] - ratio * single
            for place in level_places(level, nl):
                responses[1 + half, pl.ds(first + place * rows, 8), :] = single
        return carry

    lax.fori_loop(0, rows // 8 * across, tile, 0)

    def halves(p):
        if p < nt * nl:
            group, place = job_place(p // nl, p % nl, nl)
            at = pl.ds(place * rows, rows)
            return sides[group, at, :], sides[10 + group, at, :]
        if p < (nt + 2) * nl:
            ref = (responses, weights)[p // nl - nt]
            at = pl.ds(p % nl * rows, rows)
            return ref[1, at, :], ref[2, at, :]
        return depth[1], depth[2]

    part = lane >> 2
    planes = (nt + 2) * nl + 1
    for g in range(-(-planes // 32)):
        to_west = jnp.zeros((rows, 128), F32)
        to_east = jnp.zeros((rows, 128), F32)
        for s in range(min(32, planes - 32 * g)):
            p = 32 * g + s
            left, right = halves(p)
            to_west = jnp.where(part == s, pltpu.roll(left, 4 * s, 1), to_west)
            to_east = jnp.where(part == s, pltpu.roll(right, (4 * s + 4) % 128, 1), to_east)
            top[p, :, 0:128] = left[0:H]
            top[p, :, 128:256] = right[0:H]
            bottom[p, :, 0:128] = left[rows - H : rows]
            bottom[p, :, 128:256] = right[rows - H : rows]
        west[g] = to_west
        east[g] = to_east
    for level in range(nl):
        packed = pack_middle(
            [middle(*halves(f * nl + level), lane) for f in range(nt)], lane
        )
        for place in level_places(level, nl):
            mids[level // 8, pl.ds((place - level // 8 * 8) * rows, rows), :] = packed
        for q, ref in ((nt, responses), (nt + 1, weights)):
            spread = spread_middle(middle(*halves(q * nl + level), lane), lane, nt)
            for place in level_places(level, nl):
                ref[0, pl.ds(place * rows, rows), :] = spread


def mix(tracers, diffusivity, viscosity, mask, count):
    nt, nl, rows, width = tracers.shape
    planes = (nt + 2) * nl + 1
    groups = -(-planes // 32)
    out = (
        shaped(3, 8 * rows, 128),
        shaped(20, 8 * rows, 128),
        shaped(3, 24 * rows, 128),
        shaped(3, 24 * rows, 128),
        shaped(3, rows, 128),
        shaped(groups, rows, 128),
        shaped(groups, rows, 128),
        shaped(planes, H, width),
        shaped(planes, H, width),
    )
    return pl.pallas_call(
        mix_kernel,
        out_shape=out,
        in_specs=[VMEM] * 5,
        out_specs=(VMEM,) * len(out),
        scratch_shapes=[pltpu.VMEM((nl, 8, 128), F32)],
        compiler_params=params(MIX_MIB),
        name="mix",
    )(tracers, diffusivity, viscosity, mask, count)


def arrange_kernel(
    nt, nl,
    mids_in, sides_in, responses_in, weights_in, depth_in,
    west_in, east_in, north_in, south_in,
    mids, sides, responses, weights, depth,
    halo_jobs, halo_responses, halo_weights, halo_depth,
    from_west, from_east, north, south, sem,
):
    pairs = (
        (west_in, from_west),
        (east_in, from_east),
        (north_in, north),
        (south_in, south),
        (responses_in, responses),
        (weights_in, weights),
        (depth_in, depth),
        (sides_in, sides),
        (mids_in, mids),
    )
    copies = [pltpu.make_async_copy(a, b, sem.at[k]) for k, (a, b) in enumerate(pairs)]
    for copy in copies:
        copy.start()
    rows = depth.shape[1]
    lane = lax.broadcasted_iota(jnp.int32, (rows, 128), 1)
    lane8 = lax.broadcasted_iota(jnp.int32, (2 * H, 128), 1)

    def patch(p, ref, left, right, at):
        g, s = p // 32, p % 32
        ref[left, at, :] = jnp.where(
            lane >= 128 - H, pltpu.roll(from_west[g], (252 - 4 * s) % 128, 1), ref[left, at, :]
        )
        ref[right, at, :] = jnp.where(
            lane < H, pltpu.roll(from_east[g], (128 - 4 * s) % 128, 1), ref[right, at, :]
        )

    def beyond(p):
        both = jnp.concatenate([south[p], north[p]], axis=0)
        left, right = both[:, 0:128], both[:, 128:256]
        return left, right, middle(left, right, lane8)

    for copy in copies[:4]:
        copy.wait()
    for level in range(nl):
        packed = []
        for f in range(nt):
            group, place = job_place(f, level, nl)
            at = pl.ds(place * 8, 8)
            near, far, mid = beyond(f * nl + level)
            halo_jobs[3 + group, at, :] = near
            halo_jobs[13 + group, at, :] = far
            packed.append(mid)
        packed = pack_middle(packed, lane8)
        for place in level_places(level, nl):
            halo_jobs[level // 8, pl.ds((place - level // 8 * 8) * 8, 8), :] = packed
        for q, halo in ((nt, halo_responses), (nt + 1, halo_weights)):
            near, far, mid = beyond(q * nl + level)
            mid = spread_middle(mid, lane8, nt)
            for place in level_places(level, nl):
                at = pl.ds(place * 8, 8)
                halo[0, at, :] = mid
                halo[1, at, :] = near
                halo[2, at, :] = far
    near, far, mid = beyond((nt + 2) * nl)
    halo_depth[0] = spread_middle(mid, lane8, nt)
    halo_depth[1] = near
    halo_depth[2] = far
    for copy in copies[4:7]:
        copy.wait()
    for level in range(nl):
        for q, ref in ((nt, responses), (nt + 1, weights)):
            for place in level_places(level, nl):
                patch(q * nl + level, ref, 1, 2, pl.ds(place * rows, rows))
    patch((nt + 2) * nl, depth, 1, 2, slice(None))
    copies[7].wait()
    for level in range(nl):
        for f in range(nt):
            group, place = job_place(f, level, nl)
            patch(f * nl + level, sides, group, 10 + group, pl.ds(place * rows, rows))
    copies[8].wait()


def arrange(nt, nl, mixed, halo):
    operands = (*mixed, *halo)
    out = tuple(shaped(*x.shape) for x in mixed) + (
        shaped(23, 64, 128),
        shaped(3, 24 * 8, 128),
        shaped(3, 24 * 8, 128),
        shaped(3, 8, 128),
    )
    return pl.pallas_call(
        functools.partial(arrange_kernel, nt, nl),
        out_shape=out,
        in_specs=[HBM] * len(operands),
        out_specs=(VMEM,) * len(out),
        scratch_shapes=[pltpu.VMEM(x.shape, F32) for x in halo]
        + [pltpu.SemaphoreType.DMA((len(operands),))],
        compiler_params=params(ARRANGE_MIB),
        name="arrange",
    )(*operands)


def two(x):
    high = x.astype(jnp.bfloat16)
    return high, (x - high.astype(jnp.float32)).astype(jnp.bfloat16)


def collect_kernel(
    arrived, mask, corners, ocean_flux, side, to_north, to_south,
):
    rows, width = mask.shape
    nt = ocean_flux.shape[0]
    stride = (CAP + 1) * nt
    devices = arrived.shape[0] // stride

    def slot(s):
        return jnp.concatenate(
            [arrived[pl.ds(s * nt + f, devices, stride=stride), :] for f in range(nt)], axis=1
        )

    idents = jnp.transpose(arrived[pl.ds(CAP * nt, devices, stride=stride), :]).astype(jnp.int32) - 1
    y = lax.broadcasted_iota(jnp.int32, (rows, devices), 0)
    places = jnp.concatenate([2 * y, 2 * y + 1], axis=0)
    total = jnp.zeros((2 * rows, nt * 128), jnp.float32)
    for s in range(CAP):
        pick = (places == idents[OWN_ID + s : OWN_ID + s + 1, :]).astype(jnp.bfloat16)
        for piece in two(slot(s)):
            total = total + jnp.dot(pick, piece, preferred_element_type=jnp.float32)
    keep = mask[...].astype(jnp.float32)
    main = []
    for f in range(nt):
        cells = slice(f * 128, (f + 1) * 128)
        main.append(jnp.concatenate([total[0:rows, cells], total[rows:, cells]], axis=1) * keep)
        ocean_flux[f] = main[f]
    pick = jnp.concatenate(
        [
            (y == (idents[NBR_ID + e : NBR_ID + e + 1, :] >> 1)).astype(jnp.bfloat16)
            for e in range(2 * CAP)
        ],
        axis=0,
    )
    high, low = two(slot(CAP))
    spread = jnp.dot(pick, high, preferred_element_type=jnp.float32) + jnp.dot(
        pick, low, preferred_element_type=jnp.float32
    )
    lane = lax.broadcasted_iota(jnp.int32, (rows, 128), 1)
    for f in range(nt):
        west = jnp.zeros((rows, 128), jnp.float32)
        east = jnp.zeros((rows, 128), jnp.float32)
        for e in range(CAP):
            part = spread[e * rows : (e + 1) * rows, f * 128 : (f + 1) * 128]
            west = west + pltpu.roll(part, (124 - 4 * e) % 128, 1)
            e = e + CAP
            part = spread[e * rows : (e + 1) * rows, f * 128 : (f + 1) * 128]
            east = east + pltpu.roll(part, (128 - 4 * e) % 128, 1)
        edge = jnp.where(lane < H, east, jnp.where(lane >= 128 - H, west, 0.0))
        side[f] = edge
        for t, lanes in enumerate((main[f][:, 0:128], main[f][:, 128:256], edge)):
            to_north[3 * f + t] = lanes[0:H]
            to_south[3 * f + t] = lanes[rows - H : rows]
    groups = corners.shape[0]
    for g in range(groups):
        to_north[3 * nt + g] = corners[g, 0:H]
        to_south[3 * nt + g] = corners[g, H : 2 * H]


def collect(arrived, mask, corners, nt):
    rows, width = mask.shape
    f32 = jnp.float32
    line = shaped(3 * nt + corners.shape[0], H, 128)
    return pl.pallas_call(
        collect_kernel,
        out_shape=(
            jax.ShapeDtypeStruct((nt, rows, width), f32),
            jax.ShapeDtypeStruct((nt, rows, 128), f32),
            line,
            line,
        ),
        in_specs=[VMEM] * 3,
        out_specs=(VMEM,) * 4,
        compiler_params=params(12),
        name="collect",
    )(arrived, mask, corners)


def diffuse_kernel(
    nl,
    mids, sides, responses, weights, depth,
    halo_jobs, halo_responses, halo_weights, halo_depth, main, side, north, south,
    out, surface, surface_halo, start, start_halo, far_weights, far_depth, corners,
    done, merged, sem,
):
    nt, rows, width = main.shape
    lane = lax.broadcasted_iota(jnp.int32, (rows, 128), 1)
    lane8 = lax.broadcasted_iota(jnp.int32, (2 * H, 128), 1)
    planes = (nt + 2) * nl + 1
    groups = -(-planes // 32)
    for g in range(2 * groups):
        corners[g] = jnp.concatenate([south[3 * nt + g], north[3 * nt + g]], axis=0)

    def patched(p, left, right):
        g, s = p // 32, p % 32
        return (
            jnp.where(lane8 >= 128 - H, pltpu.roll(corners[g], (252 - 4 * s) % 128, 1), left),
            jnp.where(lane8 < H, pltpu.roll(corners[groups + g], (128 - 4 * s) % 128, 1), right),
        )

    far_depth[0] = halo_depth[0]
    far_depth[1], far_depth[2] = patched(planes - 1, halo_depth[1], halo_depth[2])

    packed, packed8 = [], []
    for f in range(nt):
        left, right = main[f, :, 0:128], main[f, :, 128:256]
        packed.append(middle(left, right, lane))
        left = jnp.where(lane >= 128 - H, side[f], left)
        right = jnp.where(lane < H, side[f], right)
        surface[1, f] = jnp.where(depth[1] > 0.0, left, 0.0)
        surface[2, f] = jnp.where(depth[2] > 0.0, right, 0.0)
        left, right, edge = [
            jnp.concatenate([south[3 * f + t], north[3 * f + t]], axis=0) for t in range(3)
        ]
        packed8.append(middle(left, right, lane8))
        left = jnp.where(lane8 >= 128 - H, edge, left)
        right = jnp.where(lane8 < H, edge, right)
        surface_halo[1, f] = jnp.where(far_depth[1] > 0.0, left, 0.0)
        surface_halo[2, f] = jnp.where(far_depth[2] > 0.0, right, 0.0)
    surface[0, 0] = jnp.where(depth[0] > 0.0, pack_middle(packed, lane), 0.0)
    surface_halo[0, 0] = jnp.where(far_depth[0] > 0.0, pack_middle(packed8, lane8), 0.0)

    for level in range(nl):
        p = (nt + 1) * nl + level
        for place in level_places(level, nl):
            at = pl.ds(place * 8, 8)
            far_weights[0, at, :] = halo_weights[0, at, :]
            far_weights[1, at, :], far_weights[2, at, :] = patched(
                p, halo_weights[1, at, :], halo_weights[2, at, :]
            )
        at = pl.ds(level * 8, 8)
        mid = halo_responses[0, at, :]
        near, far = patched(nt * nl + level, halo_responses[1, at, :], halo_responses[2, at, :])
        for place in level_places(level, nl):
            at = pl.ds((place - level // 8 * 8) * 8, 8)
            start_halo[level // 8, at, :] = (
                halo_jobs[level // 8, at, :] + mid * surface_halo[0, 0]
            )
        for f in range(nt):
            group, place = job_place(f, level, nl)
            at = pl.ds(place * 8, 8)
            left, right = patched(
                f * nl + level, halo_jobs[3 + group, at, :], halo_jobs[13 + group, at, :]
            )
            start_halo[3 + group, at, :] = left + near * surface_halo[1, f]
            start_halo[13 + group, at, :] = right + far * surface_halo[2, f]

    sub = lax.broadcasted_iota(jnp.int32, (8, 128), 0)

    def laplace(v, y):
        c = v[y]
        return (
            (v[y - 1] + v[y + 1]) + (pltpu.roll(c, 1, 1) + pltpu.roll(c, 127, 1))
        ) - 4.0 * c

    def begin(slot, job, part, first, f0, f4, values, at_job):
        for i in range(8):
            at = pl.ds(i * rows, rows)
            beside = pl.ds(pl.multiple_of((first + i) * rows, 8), rows)
            start[slot, pl.ds(i * PITCH, rows), :] = values[at_job, at, :] + responses[part, beside, :] * surface[
                part, f0 if i < 4 else f4
            ]
        level = (jnp.where(first == 16, sub & 3, sub) + first).astype(F32)
        v, w, stages = {}, {}, [{} for _ in range(2 * SUBSTEPS)]

        def update(now, y, change):
            if 0 <= y < rows:
                deep = depth[part, pl.ds(y, 1), :]
            else:
                deep = far_depth[part, pl.ds(y + 2 * H if y < 0 else y - rows, 1), :]
            return now[y] - jnp.where(level < deep, change, 0.0)

        def load(y):
            if 0 <= y < rows:
                v[y] = start[slot, pl.ds(y, 8, stride=PITCH), :]
                w[y] = weights[part, pl.ds(first * rows + y, 8, stride=rows), :]
            else:
                r = y + 2 * H if y < 0 else y - rows
                v[y] = start_halo[job, pl.ds(r, 8, stride=8), :]
                w[y] = far_weights[part, pl.ds(first * 8 + r, 8, stride=8), :]

        def advance(stage, y):
            k, edge = y, H - stage - 1
            if -edge <= k < rows + edge:
                now = v if stage < 2 else stages[stage // 2 * 2 - 1]
                if stage % 2 == 0:
                    stages[stage][k] = w[k] * laplace(now, k)
                else:
                    stages[stage][k] = update(now, k, laplace(stages[stage - 1], k))

        def store(k):
            if 0 <= k < rows:
                done[job, pl.ds(k, 8, stride=PITCH), :] = stages[-1][k]

        return load, advance, store

    def run(jobs):
        ys = range(-H, rows + H)
        for load, advance, store in jobs:
            for y in ys:
                load(y)
            for stage in range(2 * SUBSTEPS):
                for y in ys:
                    advance(stage, y)
            for y in ys:
                store(y)

    def strip(slot, m):
        return begin(slot, m, 0, 8 * m, 0, 0, mids, m)

    for m in range(3):
        run([strip(m % 2, jnp.int32(m))])

    def both(group, first, f0, f4):
        for half in range(2):
            job = 10 * half + group
            run([begin(half, 3 + job, 1 + half, first, f0, f4, sides, job)])
        for i in range(8):
            f = f0 if i < 4 else f4
            at = pl.ds(i * PITCH, rows)
            turn = pltpu.roll(done[first // 8, at, :], lax.rem(244 - 32 * f, 128), 1)
            merged[group, i, :, 0:128] = jnp.where(lane < 120, done[3 + group, at, :], turn)
            merged[group, i, :, 128:256] = jnp.where(lane >= 8, done[13 + group, at, :], turn)

    def whole_copy(group):
        first = pl.multiple_of(8 * (group % 2), 8)
        return pltpu.make_async_copy(
            merged.at[group], out.at[group // 2, pl.ds(first, 8)], sem.at[group, 0]
        )

    def half_copies(group):
        return [
            pltpu.make_async_copy(
                merged.at[group, pl.ds((nl - 16) * k, nl - 16)],
                out.at[2 * (group - 8) + k, pl.ds(16, nl - 16)],
                sem.at[group, k],
            )
            for k in range(2)
        ]

    def wholes(group):
        f = group // 2
        both(group, 8 * (group % 2), f, f)
        whole_copy(group).start()

    def pairs(group):
        f = 2 * (group - 8)
        both(group, 16 + 0 * group, f, f + 1)
        for copy in half_copies(group):
            copy.start()

    for group in range(8):
        wholes(jnp.int32(group))
    for group in range(8, 10):
        pairs(jnp.int32(group))
    for group in range(8):
        whole_copy(group).wait()
    for group in range(8, 10):
        for copy in half_copies(group):
            copy.wait()


def diffuse(arranged, main, side, north, south, nl):
    nt, rows, width = main.shape
    operands = (*arranged, main, side, north, south)
    return pl.pallas_call(
        functools.partial(diffuse_kernel, nl),
        out_shape=shaped(nt, nl, rows, width),
        in_specs=[VMEM] * len(operands),
        out_specs=ANY,
        scratch_shapes=[
            pltpu.VMEM((3, nt, rows, 128), F32),
            pltpu.VMEM((3, nt, 8, 128), F32),
            pltpu.VMEM((2, 8 * PITCH, 128), F32),
            pltpu.VMEM((23, 64, 128), F32),
            pltpu.VMEM((3, 24 * 8, 128), F32),
            pltpu.VMEM((3, 8, 128), F32),
            pltpu.VMEM((north.shape[0] - 3 * nt, 8, 128), F32),
            pltpu.VMEM((23, 8 * PITCH, 128), F32),
            pltpu.VMEM((10, 8, rows, width), F32),
            pltpu.SemaphoreType.DMA((10, 2)),
        ],
        compiler_params=params(DIFFUSE_MIB),
        name="diffuse",
    )(*operands)


def body(
    atm_flux,
    remap_weights,
    link_source,
    link_owner,
    link_block,
    ocean_mask,
    level_count,
    tracers,
    diffusivity,
    viscosity,
):
    n_oy = lax.axis_size("oy")
    n_ox = lax.axis_size("ox")
    devices = n_oy * n_ox
    nt, nl, rows, width = tracers.shape
    payload = remap(
        atm_flux, remap_weights, link_source, link_owner, link_block, devices, n_ox
    )
    arrived = lax.all_to_all(payload, ("oy", "ox"), split_axis=0, concat_axis=0, tiled=True)
    arrived = arrived.reshape(devices * (CAP + 1) * nt, 128)

    eastward = [(i, (i + 1) % n_ox) for i in range(n_ox)]
    westward = [(j, i) for i, j in eastward]
    southward = [(i, i + 1) for i in range(n_oy - 1)]
    northward = [(j, i) for i, j in southward]
    mids, sides, responses, weights, depth, west, east, top, bottom = mix(
        tracers, diffusivity, viscosity, ocean_mask, level_count
    )
    from_west = lax.ppermute(east, "ox", eastward)
    from_east = lax.ppermute(west, "ox", westward)
    north = lax.ppermute(bottom, "oy", southward)
    south = lax.ppermute(top, "oy", northward)
    arranged = arrange(
        nt, nl, (mids, sides, responses, weights, depth), (from_west, from_east, north, south)
    )
    strips = jnp.concatenate([from_west, from_east], axis=0)
    corners = jnp.concatenate([strips[:, :H], strips[:, rows - H :]], axis=1)
    ocean_flux, side, to_north, to_south = collect(arrived, ocean_mask, corners, nt)
    flux_north = lax.ppermute(to_south, "oy", southward)
    flux_south = lax.ppermute(to_north, "oy", northward)
    mixed = diffuse(arranged, ocean_flux, side, flux_north, flux_south, nl)
    return mixed, ocean_flux


def solution(mesh):
    placed = (
        P(("oy", "ox"), None, None),
        P(("oy", "ox"), None, None),
        P(("oy", "ox")),
        P(("oy", "ox"), None),
        P(("oy", "ox")),
        P("oy", "ox"),
        P("oy", "ox"),
        P(None, None, "oy", "ox"),
        P(None, "oy", "ox"),
        P(None, "oy", "ox"),
    )
    return jax.shard_map(
        body,
        mesh=mesh,
        in_specs=placed,
        out_specs=(P(None, None, "oy", "ox"), P(None, "oy", "ox")),
        check_vma=False,
    )
```

time: 111 us -> 72.2 us (0.65)
  Pallas kernels: 57.5 us -> 30.2 us
  waiting for transfers between devices: 11.9 us -> 6.2 us
  starting transfers between devices: 33.8 us -> 29.2 us
  other arithmetic: 3.4 us -> 0.62 us
    pallas_call x4, Pallas kernels: 54.5 us -> 28.8 us  [the longest x1 9.1 us: diffuse(): pl.pallas_call(functools.partial(diffuse_kernel, nl), out_shape=shaped(nt...]
    ppermute x1, waiting for transfers between devices: 6.78 us -> 0.01 us  [body(): from_east = lax.ppermute(west, 'ox', westward)]
    ppermute x2 -> x0, starting transfers between devices: 6.08 us -> none  [the longest x1 3.64 us: body(): north_corner = lax.ppermute(both[:, rows - H:], 'oy', southward)]
    convert_element_type x2 -> x0, other arithmetic: 2.13 us -> none  [the longest x1 1.51 us: body(): atm_flux.astype(jnp.float32)]
    ppermute x1, waiting for transfers between devices: 4.21 us -> 6.18 us  [body(): from_west = lax.ppermute(east, 'ox', eastward)]
    pallas_call x1, Pallas kernels: 3 us -> 1.45 us  [collect(): pl.pallas_call(collect_kernel, out_shape=(jax.ShapeDtypeStruct((nt, rows,...]
    ppermute x1, starting transfers between devices: 0.07 us -> 1.58 us  [body(): from_west = lax.ppermute(east, 'ox', eastward)]
    ppermute x1, starting transfers between devices: 5.57 us -> 4.14 us  [body(): from_east = lax.ppermute(west, 'ox', westward)]
  transfers between devices with their start and end apart: 9 -> 7, of which waited for: 3 -> 1; matrix products, arithmetic and copies ran while one was open for 1% -> 1% of each run, Pallas kernels for 16% -> 19%
where the time goes in v3:
time: 72.2 us; the launch traced here: 71.8 us
  Pallas kernels  30.2 us (42%)
  starting transfers between devices  29.2 us (40%)
  waiting for transfers between devices  6.2 us (9%)
  local copies, waits for them, and re-layouts  4.45 us (6%)
  between operations  1.01 us (1%)
    all_to_all x1, starting transfers between devices, body(): lax.all_to_all(payload, ('oy', 'ox'), split_axis=0, concat_axis=0, tiled=...  11.5 us
    pallas_call x1, Pallas kernels, diffuse(): pl.pallas_call(functools.partial(diffuse_kernel, nl), out_shape=shaped(nt...  9.1 us
    pallas_call x1, Pallas kernels, mix(): pl.pallas_call(mix_kernel, out_shape=out, in_specs=[VMEM] * 5, out_specs=...  8.89 us
    pallas_call x1, Pallas kernels, remap(): pl.pallas_call(functools.partial(remap_kernel, n_ox), out_shape=shaped(de...  7.69 us
    ppermute x1, waiting for transfers between devices, body(): from_west = lax.ppermute(east, 'ox', eastward)  6.18 us
    unnamed x25, local copies, waits for them, and re-layouts  4.44 us
    ppermute x1, starting transfers between devices, body(): flux_north = lax.ppermute(to_south, 'oy', southward)  4.37 us
    ppermute x1, starting transfers between devices, body(): from_east = lax.ppermute(west, 'ox', westward)  4.14 us
  transfers between devices with their start and end apart: 7, of which 1 were waited for; matrix products, arithmetic and copies ran while one was open for 1% of the time, Pallas kernels for 19%

profile of v3, /device:TPU:1, one launch (start us, length us, event | category | flops | bytes accessed | tf_op | source)
XLA Modules:
  0.0 71.8 jit_solution(469995286302458430)
XLA Ops:
  0.6 7.7 %remap.1 = f32[128,7,4,128]{3,2,1,0:T(4,128)} custom-call(s32[384]{0:T(512)} %source.1, s32[1,384]{1,0:T(1,128)} %bitcast.3, s32[384]{0:T(512)} %block_row.1, bf16[64,4,128]{2,1,0:T(4,128)(2,1)} %flux.1, bf16[384,128,128]{2,1,0:T(8,128)(2,1)} %weights.1), custom_call_target="tpu_custom_call" | custom-call | tf_op jit(solution)/shard_map/remap/pallas_call | solution.py:129
  8.3 11.5 %all-to-all-start = ((f32[128,7,4,128]{3,2,1,0:T(4,128)}), f32[128,7,4,128]{3,2,1,0:T(4,128)S(1)}, u32[]{:S(2)}, u32[]{:S(2)}) async-start(f32[128,7,4,128]{3,2,1,0:T(4,128)} %remap.1), calls=%async_computation | async-start | bytes 3670016 | tf_op jit(solution)/shard_map/all_to_all | solution.py:712
  19.8 0.0 copy-start.9
  19.8 8.9 %mix.1 = (f32[3,256,128]{2,1,0:T(8,128)}, f32[20,256,128]{2,1,0:T(8,128)}, f32[3,768,128]{2,1,0:T(8,128)}, f32[3,768,128]{2,1,0:T(8,128)}, f32[3,32,128]{2,1,0:T...) custom-call(f32[4,20,32,256]{3,2,1,0:T(8,128)} %tracers.1, ...), custom_call_target="tpu_custom_call" | custom-call | tf_op jit(solution)/shard_map/mix/pallas_call | solution.py:289
  28.7 0.0 copy-start.1
  28.7 1.6 %collective-permute-start = (f32[4,32,128]{2,1,0:T(8,128)}, f32[4,32,128]{2,1,0:T(8,128)S(1)}, u32[]{:S(2)}, u32[]{:S(2)}) collective-permute-start(f32[4,32,128]{2,1,0:T(8,128)} %get-tuple-element.29), channel_id=1, source_target_pairs={{0,1},{1,2},{2,3},{3,4},{4,5},{5,6},{6,7},{7,8},{8,9},{9,10},{10,1... | collective-permute-start | bytes 196616 | tf_op jit(solution)/shard_map/ppermute | solution.py:722
  30.3 4.1 %collective-permute-start.1 = (f32[4,32,128]{2,1,0:T(8,128)}, f32[4,32,128]{2,1,0:T(8,128)S(1)}, u32[]{:S(2)}, u32[]{:S(2)}) collective-permute-start(f32[4,32,128]{2,1,0:T(8,128)} %get-tuple-element.30), channel_id=1, source_target_pairs={{1,0},{2,1},{3,2},{4,3},{5,4},{6,5},{7,6},{8,7},{9,8},{10,9},{11,1... | collective-permute-start | bytes 196616 | tf_op jit(solution)/shard_map/ppermute | solution.py:723
  34.5 3.6 %collective-permute-start.2 = (f32[121,4,256]{2,1,0:T(4,128)}, f32[121,4,256]{2,1,0:T(4,128)S(1)}, u32[]{:S(2)}, u32[]{:S(2)}) collective-permute-start(f32[121,4,256]{2,1,0:T(4,128)} %get-tuple-element.31), channel_id=1, source_target_pairs={{0,16},{16,32},{32,48},{48,64},{64,80},{80,96},{96,112},{1,17},{17... | collective-permute-start | bytes 1486856 | tf_op jit(solution)/shard_map/ppermute | solution.py:724
  38.1 1.9 %collective-permute-start.3 = (f32[121,4,256]{2,1,0:T(4,128)}, f32[121,4,256]{2,1,0:T(4,128)}, u32[]{:S(2)}, u32[]{:S(2)}) collective-permute-start(f32[121,4,256]{2,1,0:T(4,128)} %get-tuple-element.32), channel_id=1, source_target_pairs={{16,0},{32,16},{48,32},{64,48},{80,64},{96,80},{112,96},{17,1},{33... | collective-permute-start | bytes 1486856 | tf_op jit(solution)/shard_map/ppermute | solution.py:725
  40.0 6.2 %collective-permute-done.west_in = f32[4,32,128]{2,1,0:T(8,128)S(1)} collective-permute-done((f32[4,32,128]{2,1,0:T(8,128)}, f32[4,32,128]{2,1,0:T(8,128)S(1)}, u32[]{:S(2)}, u32[]{:S(2)}) %collective-permute-start) | collective-permute-done | bytes 65568 | tf_op jit(solution)/shard_map/ppermute | solution.py:722
  46.2 0.0 copy-start.4
  46.2 0.0 collective-permute-done.1.east_in
  46.2 0.0 copy-start.6
  46.3 0.6 copy-done.4
  46.8 0.0 copy-done.6
  46.9 0.6 pad_maximum_fusion.corners
  47.5 0.0 all-to-all-done
  47.5 0.0 copy-start.3
  47.5 0.0 copy-start.5
  47.5 0.0 copy-start.7
  47.5 0.0 copy-done.9
  47.5 0.0 copy-start.10
  47.5 0.8 %copy-done.10 = f32[8,8,128]{2,1,0:T(8,128)S(1)} copy-done((f32[8,8,128]{2,1,0:T(8,128)S(1)}, f32[8,8,128]{2,1,0:T(8,128)}, u32[]{:S(2)}) %copy-start.10) | copy-done | bytes 32792
  48.3 0.0 copy-start.11
  48.3 1.5 %collect.1 = (f32[4,32,256]{2,1,0:T(8,128)}, f32[4,32,128]{2,1,0:T(8,128)S(1)}, f32[20,4,128]{2,1,0:T(4,128)S(1)}, f32[20,4,128]{2,1,0:T(4,128)S(1)}) custom-call(f32[3584,128]{1,0:T(8,128)S(1)} %bitcast.2, s32[32,256]{1,0:T(8,128)S(1)} %copy-done.9, f32[8,8,128]{2,1,0:T(8,128)S(1)} %copy-done.10), custom_call_target="tpu_custom_call" | custom-call | tf_op jit(solution)/shard_map/collect/pallas_call | solution.py:469
  49.8 4.4 %collective-permute-start.4 = (f32[20,4,128]{2,1,0:T(4,128)S(1)}, f32[20,4,128]{2,1,0:T(4,128)S(1)}, u32[]{:S(2)}, u32[]{:S(2)}) collective-permute-start(f32[20,4,128]{2,1,0:T(4,128)S(1)} %get-tuple-element.44), channel_id=1, source_target_pairs={{0,16},{16,32},{32,48},{48,64},{64,80},{80,96},{96,112},{1,17},{17... | collective-permute-start | bytes 122888 | tf_op jit(solution)/shard_map/ppermute | solution.py:732
  54.1 2.1 %collective-permute-start.5 = (f32[20,4,128]{2,1,0:T(4,128)S(1)}, f32[20,4,128]{2,1,0:T(4,128)S(1)}, u32[]{:S(2)}, u32[]{:S(2)}) collective-permute-start(f32[20,4,128]{2,1,0:T(4,128)S(1)} %get-tuple-element.45), channel_id=1, source_target_pairs={{16,0},{32,16},{48,32},{64,48},{80,64},{96,80},{112,96},{17,1},{33... | collective-permute-start | bytes 122888 | tf_op jit(solution)/shard_map/ppermute | solution.py:733
  56.3 0.0 collective-permute-done.2.north_in
  56.3 0.0 collective-permute-done.3.south_in
  56.3 0.0 copy-done.1
  56.3 0.0 copy-done.3
  56.3 0.0 copy-done.5
  56.3 0.0 copy-done.7
  56.3 0.0 copy-done.11
  56.3 0.0 copy-start
  56.3 1.7 %copy-done = f32[20,256,128]{2,1,0:T(8,128)S(1)} copy-done((f32[20,256,128]{2,1,0:T(8,128)S(1)}, f32[20,256,128]{2,1,0:T(8,128)}, u32[]{:S(2)}) %copy-start) | copy-done | bytes 2621464
  58.1 0.0 copy-start.2
  58.1 1.3 %copy-done.2 = f32[3,768,128]{2,1,0:T(8,128)S(1)} copy-done((f32[3,768,128]{2,1,0:T(8,128)S(1)}, f32[3,768,128]{2,1,0:T(8,128)}, u32[]{:S(2)}) %copy-start.2) | copy-done | bytes 1179672
  59.3 0.0 copy-start.8
  59.3 3.1 %arrange.1 = (f32[3,256,128]{2,1,0:T(8,128)S(1)}, f32[20,256,128]{2,1,0:T(8,128)S(1)}, f32[3,768,128]{2,1,0:T(8,128)S(1)}, f32[3,768,128]{2,1,0:T(8,128)S(1)}, f...) custom-call(f32[3,256,128]{2,1,0:T(8,128)S(1)} %copy-done.3, ...), custom_call_target="tpu_custom_call" | custom-call | tf_op jit(solution)/shard_map/arrange/pallas_call | solution.py:389
  62.5 0.0 collective-permute-done.4.north
  62.5 0.0 collective-permute-done.5.south
  62.5 0.0 copy-done.8
  62.5 9.1 %diffuse.1 = f32[4,20,32,256]{3,2,1,0:T(8,128)} custom-call(f32[3,256,128]{2,1,0:T(8,128)S(1)} %get-tuple-element.33.mids, f32[20,256,128]{2,1,0:T(8,128)S(1)} %get-tuple-element.34.sides, f32[3,768,128]{2,1,0:T(8,128)S(1)} %get-tuple-element.35.responses, f32[3,768,128]{2,1,0:T(8,128)S(1)} %get-tuple-element.36.weights, ...), custom_call_target="tpu_custom_call" | custom-call | tf_op jit(solution)/shard_map/diffuse/pallas_call | solution.py:671
  (3 shorter events, 0.0 us)
Async XLA Ops:
  8.3 39.2 %all-to-all-start = ((f32[128,7,4,128]{3,2,1,0:T(4,128)}), f32[128,7,4,128]{3,2,1,0:T(4,128)S(1)}, u32[]{:S(2)}, u32[]{:S(2)}) async-start(f32[128,7,4,128]{3,2,1,0:T(4,128)} %remap.1), calls=%async_computation | async-start | bytes 3670016 | tf_op jit(solution)/shard_map/all_to_all | solution.py:712
  19.8 27.7 %copy-start.9 = (s32[32,256]{1,0:T(8,128)S(1)}, s32[32,256]{1,0:T(8,128)}, u32[]{:S(2)}) copy-start(s32[32,256]{1,0:T(8,128)} %mask.3) | copy-start | bytes 98308
  28.7 27.5 %copy-start.1 = (f32[3,768,128]{2,1,0:T(8,128)S(1)}, f32[3,768,128]{2,1,0:T(8,128)}, u32[]{:S(2)}) copy-start(f32[3,768,128]{2,1,0:T(8,128)} %get-tuple-element.26.responses_in) | copy-start | bytes 3538948
  28.7 17.5 %collective-permute-start = (f32[4,32,128]{2,1,0:T(8,128)}, f32[4,32,128]{2,1,0:T(8,128)S(1)}, u32[]{:S(2)}, u32[]{:S(2)}) collective-permute-start(f32[4,32,128]{2,1,0:T(8,128)} %get-tuple-element.29), channel_id=1, source_target_pairs={{0,1},{1,2},{2,3},{3,4},{4,5},{5,6},{6,7},{7,8},{8,9},{9,10},{10,1... | collective-permute-start | bytes 196616 | tf_op jit(solution)/shard_map/ppermute | solution.py:722
  30.3 15.9 %collective-permute-start.1 = (f32[4,32,128]{2,1,0:T(8,128)}, f32[4,32,128]{2,1,0:T(8,128)S(1)}, u32[]{:S(2)}, u32[]{:S(2)}) collective-permute-start(f32[4,32,128]{2,1,0:T(8,128)} %get-tuple-element.30), channel_id=1, source_target_pairs={{1,0},{2,1},{3,2},{4,3},{5,4},{6,5},{7,6},{8,7},{9,8},{10,9},{11,1... | collective-permute-start | bytes 196616 | tf_op jit(solution)/shard_map/ppermute | solution.py:723
  34.5 21.8 %collective-permute-start.2 = (f32[121,4,256]{2,1,0:T(4,128)}, f32[121,4,256]{2,1,0:T(4,128)S(1)}, u32[]{:S(2)}, u32[]{:S(2)}) collective-permute-start(f32[121,4,256]{2,1,0:T(4,128)} %get-tuple-element.31), channel_id=1, source_target_pairs={{0,16},{16,32},{32,48},{48,64},{64,80},{80,96},{96,112},{1,17},{17... | collective-permute-start | bytes 1486856 | tf_op jit(solution)/shard_map/ppermute | solution.py:724
  38.1 18.2 %collective-permute-start.3 = (f32[121,4,256]{2,1,0:T(4,128)}, f32[121,4,256]{2,1,0:T(4,128)}, u32[]{:S(2)}, u32[]{:S(2)}) collective-permute-start(f32[121,4,256]{2,1,0:T(4,128)} %get-tuple-element.32), channel_id=1, source_target_pairs={{16,0},{32,16},{48,32},{64,48},{80,64},{96,80},{112,96},{17,1},{33... | collective-permute-start | bytes 1486856 | tf_op jit(solution)/shard_map/ppermute | solution.py:725
  46.2 0.6 copy-start.4
  46.2 0.6 copy-start.6
  47.5 8.8 %copy-start.3 = (f32[3,256,128]{2,1,0:T(8,128)S(1)}, f32[3,256,128]{2,1,0:T(8,128)}, u32[]{:S(2)}) copy-start(f32[3,256,128]{2,1,0:T(8,128)} %get-tuple-element.24.mids_in) | copy-start | bytes 1179652
  47.5 8.8 %copy-start.5 = (f32[4,32,128]{2,1,0:T(8,128)S(1)}, f32[4,32,128]{2,1,0:T(8,128)}, u32[]{:S(2)}) copy-start(f32[4,32,128]{2,1,0:T(8,128)} %copy-done.4) | copy-start | bytes 196612
  47.5 8.8 %copy-start.7 = (f32[4,32,128]{2,1,0:T(8,128)S(1)}, f32[4,32,128]{2,1,0:T(8,128)}, u32[]{:S(2)}) copy-start(f32[4,32,128]{2,1,0:T(8,128)} %copy-done.6) | copy-start | bytes 196612
  47.5 0.8 %copy-start.10 = (f32[8,8,128]{2,1,0:T(8,128)S(1)}, f32[8,8,128]{2,1,0:T(8,128)}, u32[]{:S(2)}) copy-start(f32[8,8,128]{2,1,0:T(8,128)} %pad_maximum_fusion.corners) | copy-start | bytes 98308
  48.3 8.0 %copy-start.11 = (f32[3,32,128]{2,1,0:T(8,128)S(1)}, f32[3,32,128]{2,1,0:T(8,128)}, u32[]{:S(2)}) copy-start(f32[3,32,128]{2,1,0:T(8,128)} %get-tuple-element.28.depth_in) | copy-start | bytes 147460
  49.8 12.7 %collective-permute-start.4 = (f32[20,4,128]{2,1,0:T(4,128)S(1)}, f32[20,4,128]{2,1,0:T(4,128)S(1)}, u32[]{:S(2)}, u32[]{:S(2)}) collective-permute-start(f32[20,4,128]{2,1,0:T(4,128)S(1)} %get-tuple-element.44), channel_id=1, source_target_pairs={{0,16},{16,32},{32,48},{48,64},{64,80},{80,96},{96,112},{1,17},{17... | collective-permute-start | bytes 122888 | tf_op jit(solution)/shard_map/ppermute | solution.py:732
  54.1 8.3 %collective-permute-start.5 = (f32[20,4,128]{2,1,0:T(4,128)S(1)}, f32[20,4,128]{2,1,0:T(4,128)S(1)}, u32[]{:S(2)}, u32[]{:S(2)}) collective-permute-start(f32[20,4,128]{2,1,0:T(4,128)S(1)} %get-tuple-element.45), channel_id=1, source_target_pairs={{16,0},{32,16},{48,32},{64,48},{80,64},{96,80},{112,96},{17,1},{33... | collective-permute-start | bytes 122888 | tf_op jit(solution)/shard_map/ppermute | solution.py:733
  56.3 1.7 %copy-start = (f32[20,256,128]{2,1,0:T(8,128)S(1)}, f32[20,256,128]{2,1,0:T(8,128)}, u32[]{:S(2)}) copy-start(f32[20,256,128]{2,1,0:T(8,128)} %get-tuple-element.25.sides_in) | copy-start | bytes 7864324
  58.1 1.3 %copy-start.2 = (f32[3,768,128]{2,1,0:T(8,128)S(1)}, f32[3,768,128]{2,1,0:T(8,128)}, u32[]{:S(2)}) copy-start(f32[3,768,128]{2,1,0:T(8,128)} %get-tuple-element.27.weights_in) | copy-start | bytes 3538948
  59.3 3.1 %copy-start.8 = (f32[4,32,256]{2,1,0:T(8,128)S(1)}, f32[4,32,256]{2,1,0:T(8,128)}, u32[]{:S(2)}) copy-start(f32[4,32,256]{2,1,0:T(8,128)} %get-tuple-element.23.main) | copy-start | bytes 393220

commit v4 on v3

--- a/solution.py
+++ b/solution.py
@@ -174,11 +174,33 @@
     return out
 
 
+STORE = 400
+MOVES = 23
+
+
+def moves(store, mids, sides, responses, weights, depth, sem, back):
+    rows = depth.shape[1]
+    pairs = []
+    for q, ref in enumerate((responses, weights)):
+        for part in range(3):
+            for third in range(3):
+                block = ref.at[part, pl.ds(8 * rows * third, 8 * rows)]
+                pairs.append((block, store.at[23 + 9 * q + 3 * part + third]))
+    for part in range(3):
+        pairs.append((depth.at[part], store.at[41 + part, pl.ds(0, rows)]))
+    pairs.append((mids, store.at[pl.ds(0, 3)]))
+    pairs.append((sides, store.at[pl.ds(3, 20)]))
+    if back:
+        pairs = [(b, a) for a, b in pairs]
+    return [pltpu.make_async_copy(a, b, sem.at[k]) for k, (a, b) in enumerate(pairs)]
+
+
 def mix_kernel(
     tracers, diffusivity, viscosity, mask, count,
-    mids, sides, responses, weights, depth, west, east, top, bottom,
-    ratios,
+    store, west, east, top, bottom,
+    mids, sides, responses, weights, depth, ratios, sem,
 ):
+    copies = moves(store, mids, sides, responses, weights, depth, sem, False)
     nt, nl, rows, width = tracers.shape
     levels = (count[...] * mask[...]).astype(F32)
     lane = lax.broadcasted_iota(jnp.int32, (rows, 128), 1)
@@ -243,6 +265,7 @@
             return ref[1, at, :], ref[2, at, :]
         return depth[1], depth[2]
 
+    copies[MOVES - 1].start()
     part = lane >> 2
     planes = (nt + 2) * nl + 1
     for g in range(-(-planes // 32)):
@@ -269,6 +292,10 @@
             spread = spread_middle(middle(*halves(q * nl + level), lane), lane, nt)
             for place in level_places(level, nl):
                 ref[0, pl.ds(place * rows, rows), :] = spread
+    for copy in copies[: MOVES - 1]:
+        copy.start()
+    for copy in copies:
+        copy.wait()
 
 
 def mix(tracers, diffusivity, viscosity, mask, count):
@@ -276,11 +303,7 @@
     planes = (nt + 2) * nl + 1
     groups = -(-planes // 32)
     out = (
-        shaped(3, 8 * rows, 128),
-        shaped(20, 8 * rows, 128),
-        shaped(3, 24 * rows, 128),
-        shaped(3, 24 * rows, 128),
-        shaped(3, rows, 128),
+        shaped(STORE, 8 * rows, 128),
         shaped(groups, rows, 128),
         shaped(groups, rows, 128),
         shaped(planes, H, width),
@@ -290,8 +313,16 @@
         mix_kernel,
         out_shape=out,
         in_specs=[VMEM] * 5,
-        out_specs=(VMEM,) * len(out),
-        scratch_shapes=[pltpu.VMEM((nl, 8, 128), F32)],
+        out_specs=(HBM,) + (VMEM,) * 4,
+        scratch_shapes=[
+            pltpu.VMEM((3, 8 * rows, 128), F32),
+            pltpu.VMEM((20, 8 * rows, 128), F32),
+            pltpu.VMEM((3, 24 * rows, 128), F32),
+            pltpu.VMEM((3, 24 * rows, 128), F32),
+            pltpu.VMEM((3, rows, 128), F32),
+            pltpu.VMEM((nl, 8, 128), F32),
+            pltpu.SemaphoreType.DMA((MOVES,)),
+        ],
         compiler_params=params(MIX_MIB),
         name="mix",
     )(tracers, diffusivity, viscosity, mask, count)
@@ -299,24 +330,19 @@
 
 def arrange_kernel(
     nt, nl,
-    mids_in, sides_in, responses_in, weights_in, depth_in,
-    west_in, east_in, north_in, south_in,
+    store, west_in, east_in, north_in, south_in,
     mids, sides, responses, weights, depth,
     halo_jobs, halo_responses, halo_weights, halo_depth,
-    from_west, from_east, north, south, sem,
+    from_west, from_east, north, south, sem, moved,
 ):
     pairs = (
         (west_in, from_west),
         (east_in, from_east),
         (north_in, north),
         (south_in, south),
-        (responses_in, responses),
-        (weights_in, weights),
-        (depth_in, depth),
-        (sides_in, sides),
-        (mids_in, mids),
     )
     copies = [pltpu.make_async_copy(a, b, sem.at[k]) for k, (a, b) in enumerate(pairs)]
+    copies += moves(store, mids, sides, responses, weights, depth, moved, True)
     for copy in copies:
         copy.start()
     rows = depth.shape[1]
@@ -363,24 +389,30 @@
     halo_depth[0] = spread_middle(mid, lane8, nt)
     halo_depth[1] = near
     halo_depth[2] = far
-    for copy in copies[4:7]:
+    for copy in copies[4:25]:
         copy.wait()
     for level in range(nl):
         for q, ref in ((nt, responses), (nt + 1, weights)):
             for place in level_places(level, nl):
                 patch(q * nl + level, ref, 1, 2, pl.ds(place * rows, rows))
     patch((nt + 2) * nl, depth, 1, 2, slice(None))
-    copies[7].wait()
+    copies[26].wait()
     for level in range(nl):
         for f in range(nt):
             group, place = job_place(f, level, nl)
             patch(f * nl + level, sides, group, 10 + group, pl.ds(place * rows, rows))
-    copies[8].wait()
-
-
-def arrange(nt, nl, mixed, halo):
-    operands = (*mixed, *halo)
-    out = tuple(shaped(*x.shape) for x in mixed) + (
+    copies[25].wait()
+
+
+def arrange(nt, nl, store, halo):
+    operands = (store, *halo)
+    rows = store.shape[1] // 8
+    out = (
+        shaped(3, 8 * rows, 128),
+        shaped(20, 8 * rows, 128),
+        shaped(3, 24 * rows, 128),
+        shaped(3, 24 * rows, 128),
+        shaped(3, rows, 128),
         shaped(23, 64, 128),
         shaped(3, 24 * 8, 128),
         shaped(3, 24 * 8, 128),
@@ -392,7 +424,7 @@
         in_specs=[HBM] * len(operands),
         out_specs=(VMEM,) * len(out),
         scratch_shapes=[pltpu.VMEM(x.shape, F32) for x in halo]
-        + [pltpu.SemaphoreType.DMA((len(operands),))],
+        + [pltpu.SemaphoreType.DMA((4,)), pltpu.SemaphoreType.DMA((MOVES,))],
         compiler_params=params(ARRANGE_MIB),
         name="arrange",
     )(*operands)
@@ -716,16 +748,14 @@
     westward = [(j, i) for i, j in eastward]
     southward = [(i, i + 1) for i in range(n_oy - 1)]
     northward = [(j, i) for i, j in southward]
-    mids, sides, responses, weights, depth, west, east, top, bottom = mix(
+    store, west, east, top, bottom = mix(
         tracers, diffusivity, viscosity, ocean_mask, level_count
     )
     from_west = lax.ppermute(east, "ox", eastward)
     from_east = lax.ppermute(west, "ox", westward)
     north = lax.ppermute(bottom, "oy", southward)
     south = lax.ppermute(top, "oy", northward)
-    arranged = arrange(
-        nt, nl, (mids, sides, responses, weights, depth), (from_west, from_east, north, south)
-    )
+    arranged = arrange(nt, nl, store, (from_west, from_east, north, south))
     strips = jnp.concatenate([from_west, from_east], axis=0)
     corners = jnp.concatenate([strips[:, :H], strips[:, rows - H :]], axis=1)
     ocean_flux, side, to_north, to_south = collect(arrived, ocean_mask, corners, nt)

time: 72.2 us -> 68.5 us (0.949)
  local copies, waits for them, and re-layouts: 4.45 us -> 0.03 us
  Pallas kernels: 30.2 us -> 32.8 us
    unnamed x25 -> x5, local copies, waits for them, and re-layouts: 4.44 us -> 0.02 us
    pallas_call x1, Pallas kernels: 3.11 us -> 4.48 us  [arrange(): pl.pallas_call(functools.partial(arrange_kernel, nt, nl), out_shape=out,...]
    ppermute x1, waiting for transfers between devices: 6.18 us -> 5.23 us  [body(): from_west = lax.ppermute(east, 'ox', eastward)]
    pallas_call x1, Pallas kernels: 8.89 us -> 9.84 us  [mix(): pl.pallas_call(mix_kernel, out_shape=out, in_specs=[VMEM] * 5, out_specs=...]
  transfers between devices with their start and end apart: 7 -> 7, of which waited for: 1 -> 2; matrix products, arithmetic and copies ran while one was open for 1% -> 0% of each run, Pallas kernels for 19% -> 23%
where the time goes in v4:
time: 68.5 us; the launch traced here: 68.2 us
  Pallas kernels  32.8 us (48%)
  starting transfers between devices  28.8 us (42%)
  waiting for transfers between devices  5.7 us (8%)
  between operations  0.94 us (1%)
    all_to_all x1, starting transfers between devices, body(): lax.all_to_all(payload, ('oy', 'ox'), split_axis=0, concat_axis=0, tiled=...  11.5 us
    pallas_call x1, Pallas kernels, mix(): pl.pallas_call(mix_kernel, out_shape=out, in_specs=[VMEM] * 5, out_specs=...  9.84 us
    pallas_call x1, Pallas kernels, diffuse(): pl.pallas_call(functools.partial(diffuse_kernel, nl), out_shape=shaped(nt...  9.33 us
    pallas_call x1, Pallas kernels, remap(): pl.pallas_call(functools.partial(remap_kernel, n_ox), out_shape=shaped(de...  7.64 us
    ppermute x1, waiting for transfers between devices, body(): from_west = lax.ppermute(east, 'ox', eastward)  5.23 us
    pallas_call x1, Pallas kernels, arrange(): pl.pallas_call(functools.partial(arrange_kernel, nt, nl), out_shape=out,...  4.48 us
    ppermute x1, starting transfers between devices, body(): from_east = lax.ppermute(west, 'ox', westward)  4.14 us
    ppermute x1, starting transfers between devices, body(): flux_north = lax.ppermute(to_south, 'oy', southward)  3.92 us
  transfers between devices with their start and end apart: 7, of which 2 were waited for; matrix products, arithmetic and copies ran while one was open for 0% of the time, Pallas kernels for 23%

profile of v4, /device:TPU:1, one launch (start us, length us, event | category | flops | bytes accessed | tf_op | source)
XLA Modules:
  0.0 68.2 jit_solution(16178020355981872304)
XLA Ops:
  0.6 7.6 %remap.1 = f32[128,7,4,128]{3,2,1,0:T(4,128)} custom-call(s32[384]{0:T(512)} %source.1, s32[1,384]{1,0:T(1,128)} %bitcast.3, s32[384]{0:T(512)} %block_row.1, bf16[64,4,128]{2,1,0:T(4,128)(2,1)} %flux.1, bf16[384,128,128]{2,1,0:T(8,128)(2,1)} %weights.1), custom_call_target="tpu_custom_call" | custom-call | tf_op jit(solution)/shard_map/remap/pallas_call | solution.py:129
  8.3 11.5 %all-to-all-start = ((f32[128,7,4,128]{3,2,1,0:T(4,128)}), f32[128,7,4,128]{3,2,1,0:T(4,128)S(1)}, u32[]{:S(2)}, u32[]{:S(2)}) async-start(f32[128,7,4,128]{3,2,1,0:T(4,128)} %remap.1), calls=%async_computation | async-start | bytes 3670016 | tf_op jit(solution)/shard_map/all_to_all | solution.py:744
  19.8 0.0 copy-start.1
  19.8 9.8 %mix.1 = (f32[400,256,128]{2,1,0:T(8,128)}, f32[4,32,128]{2,1,0:T(8,128)}, f32[4,32,128]{2,1,0:T(8,128)}, f32[121,4,256]{2,1,0:T(4,128)}, f32[121,4,256]{2,1,0:T(4,128)}) custom-call(f32[4,20,32,256]{3,2,1,0:T(8,128)} %tracers.1, f32[20,32,256]{2,1,0:T(8,128)} %diffusivity.1, f32[20,32,256]{2,1,0:T(8,128)} %viscosity.1, s32[32,256]{1,0:T(8,128)} %mask.3, ...), custom_call_target="tpu_custom_call" | custom-call | tf_op jit(solution)/shard_map/mix/pallas_call | solution.py:312
  29.7 1.6 %collective-permute-start = (f32[4,32,128]{2,1,0:T(8,128)}, f32[4,32,128]{2,1,0:T(8,128)S(1)}, u32[]{:S(2)}, u32[]{:S(2)}) collective-permute-start(f32[4,32,128]{2,1,0:T(8,128)} %get-tuple-element.21), channel_id=1, source_target_pairs={{0,1},{1,2},{2,3},{3,4},{4,5},{5,6},{6,7},{7,8},{8,9},{9,10},{10,1... | collective-permute-start | bytes 196616 | tf_op jit(solution)/shard_map/ppermute | solution.py:754
  31.2 4.1 %collective-permute-start.1 = (f32[4,32,128]{2,1,0:T(8,128)}, f32[4,32,128]{2,1,0:T(8,128)S(1)}, u32[]{:S(2)}, u32[]{:S(2)}) collective-permute-start(f32[4,32,128]{2,1,0:T(8,128)} %get-tuple-element.22), channel_id=1, source_target_pairs={{1,0},{2,1},{3,2},{4,3},{5,4},{6,5},{7,6},{8,7},{9,8},{10,9},{11,1... | collective-permute-start | bytes 196616 | tf_op jit(solution)/shard_map/ppermute | solution.py:755
  35.4 3.6 %collective-permute-start.2 = (f32[121,4,256]{2,1,0:T(4,128)}, f32[121,4,256]{2,1,0:T(4,128)S(1)}, u32[]{:S(2)}, u32[]{:S(2)}) collective-permute-start(f32[121,4,256]{2,1,0:T(4,128)} %get-tuple-element.23), channel_id=1, source_target_pairs={{0,16},{16,32},{32,48},{48,64},{64,80},{80,96},{96,112},{1,17},{17... | collective-permute-start | bytes 1486856 | tf_op jit(solution)/shard_map/ppermute | solution.py:756
  39.0 1.9 %collective-permute-start.3 = (f32[121,4,256]{2,1,0:T(4,128)}, f32[121,4,256]{2,1,0:T(4,128)S(1)}, u32[]{:S(2)}, u32[]{:S(2)}) collective-permute-start(f32[121,4,256]{2,1,0:T(4,128)} %get-tuple-element.24), channel_id=1, source_target_pairs={{16,0},{32,16},{48,32},{64,48},{80,64},{96,80},{112,96},{17,1},{33... | collective-permute-start | bytes 1486856 | tf_op jit(solution)/shard_map/ppermute | solution.py:757
  40.9 5.2 %collective-permute-done.west_in = f32[4,32,128]{2,1,0:T(8,128)S(1)} collective-permute-done((f32[4,32,128]{2,1,0:T(8,128)}, f32[4,32,128]{2,1,0:T(8,128)S(1)}, u32[]{:S(2)}, u32[]{:S(2)}) %collective-permute-start) | collective-permute-done | bytes 65568 | tf_op jit(solution)/shard_map/ppermute | solution.py:754
  46.2 0.0 collective-permute-done.1.east_in
  46.2 0.5 all-to-all-done
  46.7 0.0 copy-done.1
  46.7 1.5 %collect.1 = (f32[4,32,256]{2,1,0:T(8,128)}, f32[4,32,128]{2,1,0:T(8,128)S(1)}, f32[20,4,128]{2,1,0:T(4,128)S(1)}, f32[20,4,128]{2,1,0:T(4,128)S(1)}) custom-call(f32[3584,128]{1,0:T(8,128)S(1)} %bitcast.2, s32[32,256]{1,0:T(8,128)S(1)} %copy-done.1, f32[8,8,128]{2,1,0:T(8,128)S(1)} %pad_maximum_fusion.corners), custom_call_target="tpu_custom_call" | custom-call | tf_op jit(solution)/shard_map/collect/pallas_call | solution.py:501
  48.1 3.9 %collective-permute-start.4 = (f32[20,4,128]{2,1,0:T(4,128)S(1)}, f32[20,4,128]{2,1,0:T(4,128)S(1)}, u32[]{:S(2)}, u32[]{:S(2)}) collective-permute-start(f32[20,4,128]{2,1,0:T(4,128)S(1)} %get-tuple-element.36), channel_id=1, source_target_pairs={{0,16},{16,32},{32,48},{48,64},{64,80},{80,96},{96,112},{1,17},{17... | collective-permute-start | bytes 122888 | tf_op jit(solution)/shard_map/ppermute | solution.py:762
  52.1 2.1 %collective-permute-start.5 = (f32[20,4,128]{2,1,0:T(4,128)S(1)}, f32[20,4,128]{2,1,0:T(4,128)S(1)}, u32[]{:S(2)}, u32[]{:S(2)}) collective-permute-start(f32[20,4,128]{2,1,0:T(4,128)S(1)} %get-tuple-element.37), channel_id=1, source_target_pairs={{16,0},{32,16},{48,32},{64,48},{80,64},{96,80},{112,96},{17,1},{33... | collective-permute-start | bytes 122888 | tf_op jit(solution)/shard_map/ppermute | solution.py:763
  54.2 0.0 collective-permute-done.2.north_in
  54.2 0.0 collective-permute-done.3.south_in
  54.2 0.0 copy-start
  54.2 4.5 %arrange.1 = (f32[3,256,128]{2,1,0:T(8,128)S(1)}, f32[20,256,128]{2,1,0:T(8,128)S(1)}, f32[3,768,128]{2,1,0:T(8,128)S(1)}, f32[3,768,128]{2,1,0:T(8,128)S(1)}, f...) custom-call(f32[400,256,128]{2,1,0:T(8,128)} %get-tuple-element.20.s, ...), custom_call_target="tpu_custom_call" | custom-call | tf_op jit(solution)/shard_map/arrange/pallas_call | solution.py:421
  58.7 0.0 collective-permute-done.4.north
  58.7 0.0 collective-permute-done.5.south
  58.7 0.0 copy-done
  58.7 9.3 %diffuse.1 = f32[4,20,32,256]{3,2,1,0:T(8,128)} custom-call(f32[3,256,128]{2,1,0:T(8,128)S(1)} %get-tuple-element.25.mids, f32[20,256,128]{2,1,0:T(8,128)S(1)} %get-tuple-element.26.sides, f32[3,768,128]{2,1,0:T(8,128)S(1)} %get-tuple-element.27.responses, f32[3,768,128]{2,1,0:T(8,128)S(1)} %get-tuple-element.28.weights, ...), custom_call_target="tpu_custom_call" | custom-call | tf_op jit(solution)/shard_map/diffuse/pallas_call | solution.py:703
  (4 shorter events, 0.0 us)
Async XLA Ops:
  8.3 38.4 %all-to-all-start = ((f32[128,7,4,128]{3,2,1,0:T(4,128)}), f32[128,7,4,128]{3,2,1,0:T(4,128)S(1)}, u32[]{:S(2)}, u32[]{:S(2)}) async-start(f32[128,7,4,128]{3,2,1,0:T(4,128)} %remap.1), calls=%async_computation | async-start | bytes 3670016 | tf_op jit(solution)/shard_map/all_to_all | solution.py:744
  19.8 26.9 %copy-start.1 = (s32[32,256]{1,0:T(8,128)S(1)}, s32[32,256]{1,0:T(8,128)}, u32[]{:S(2)}) copy-start(s32[32,256]{1,0:T(8,128)} %mask.3) | copy-start | bytes 98308
  29.7 16.5 %collective-permute-start = (f32[4,32,128]{2,1,0:T(8,128)}, f32[4,32,128]{2,1,0:T(8,128)S(1)}, u32[]{:S(2)}, u32[]{:S(2)}) collective-permute-start(f32[4,32,128]{2,1,0:T(8,128)} %get-tuple-element.21), channel_id=1, source_target_pairs={{0,1},{1,2},{2,3},{3,4},{4,5},{5,6},{6,7},{7,8},{8,9},{9,10},{10,1... | collective-permute-start | bytes 196616 | tf_op jit(solution)/shard_map/ppermute | solution.py:754
  31.2 14.9 %collective-permute-start.1 = (f32[4,32,128]{2,1,0:T(8,128)}, f32[4,32,128]{2,1,0:T(8,128)S(1)}, u32[]{:S(2)}, u32[]{:S(2)}) collective-permute-start(f32[4,32,128]{2,1,0:T(8,128)} %get-tuple-element.22), channel_id=1, source_target_pairs={{1,0},{2,1},{3,2},{4,3},{5,4},{6,5},{7,6},{8,7},{9,8},{10,9},{11,1... | collective-permute-start | bytes 196616 | tf_op jit(solution)/shard_map/ppermute | solution.py:755
  35.4 18.8 %collective-permute-start.2 = (f32[121,4,256]{2,1,0:T(4,128)}, f32[121,4,256]{2,1,0:T(4,128)S(1)}, u32[]{:S(2)}, u32[]{:S(2)}) collective-permute-start(f32[121,4,256]{2,1,0:T(4,128)} %get-tuple-element.23), channel_id=1, source_target_pairs={{0,16},{16,32},{32,48},{48,64},{64,80},{80,96},{96,112},{1,17},{17... | collective-permute-start | bytes 1486856 | tf_op jit(solution)/shard_map/ppermute | solution.py:756
  39.0 15.2 %collective-permute-start.3 = (f32[121,4,256]{2,1,0:T(4,128)}, f32[121,4,256]{2,1,0:T(4,128)S(1)}, u32[]{:S(2)}, u32[]{:S(2)}) collective-permute-start(f32[121,4,256]{2,1,0:T(4,128)} %get-tuple-element.24), channel_id=1, source_target_pairs={{16,0},{32,16},{48,32},{64,48},{80,64},{96,80},{112,96},{17,1},{33... | collective-permute-start | bytes 1486856 | tf_op jit(solution)/shard_map/ppermute | solution.py:757
  48.1 10.6 %collective-permute-start.4 = (f32[20,4,128]{2,1,0:T(4,128)S(1)}, f32[20,4,128]{2,1,0:T(4,128)S(1)}, u32[]{:S(2)}, u32[]{:S(2)}) collective-permute-start(f32[20,4,128]{2,1,0:T(4,128)S(1)} %get-tuple-element.36), channel_id=1, source_target_pairs={{0,16},{16,32},{32,48},{48,64},{64,80},{80,96},{96,112},{1,17},{17... | collective-permute-start | bytes 122888 | tf_op jit(solution)/shard_map/ppermute | solution.py:762
  52.1 6.6 %collective-permute-start.5 = (f32[20,4,128]{2,1,0:T(4,128)S(1)}, f32[20,4,128]{2,1,0:T(4,128)S(1)}, u32[]{:S(2)}, u32[]{:S(2)}) collective-permute-start(f32[20,4,128]{2,1,0:T(4,128)S(1)} %get-tuple-element.37), channel_id=1, source_target_pairs={{16,0},{32,16},{48,32},{64,48},{80,64},{96,80},{112,96},{17,1},{33... | collective-permute-start | bytes 122888 | tf_op jit(solution)/shard_map/ppermute | solution.py:763
  54.2 4.5 %copy-start = (f32[4,32,256]{2,1,0:T(8,128)S(1)}, f32[4,32,256]{2,1,0:T(8,128)}, u32[]{:S(2)}) copy-start(f32[4,32,256]{2,1,0:T(8,128)} %get-tuple-element.19.main) | copy-start | bytes 393220

commit v5 on v4

--- a/solution.py
+++ b/solution.py
@@ -343,6 +343,7 @@
     )
     copies = [pltpu.make_async_copy(a, b, sem.at[k]) for k, (a, b) in enumerate(pairs)]
     copies += moves(store, mids, sides, responses, weights, depth, moved, True)
+    copies = copies[:4] + copies[-1:] + copies[4:-1]
     for copy in copies:
         copy.start()
     rows = depth.shape[1]
@@ -389,7 +390,12 @@
     halo_depth[0] = spread_middle(mid, lane8, nt)
     halo_depth[1] = near
     halo_depth[2] = far
-    for copy in copies[4:25]:
+    copies[4].wait()
+    for level in range(nl):
+        for f in range(nt):
+            group, place = job_place(f, level, nl)
+            patch(f * nl + level, sides, group, 10 + group, pl.ds(place * rows, rows))
+    for copy in copies[5:26]:
         copy.wait()
     for level in range(nl):
         for q, ref in ((nt, responses), (nt + 1, weights)):
@@ -397,11 +403,6 @@
                 patch(q * nl + level, ref, 1, 2, pl.ds(place * rows, rows))
     patch((nt + 2) * nl, depth, 1, 2, slice(None))
     copies[26].wait()
-    for level in range(nl):
-        for f in range(nt):
-            group, place = job_place(f, level, nl)
-            patch(f * nl + level, sides, group, 10 + group, pl.ds(place * rows, rows))
-    copies[25].wait()
 
 
 def arrange(nt, nl, store, halo):

time: 68.5 us -> 68.1 us (level)
  no operation moved by 1% of the time
where the time goes in v5:
time: 68.1 us; the launch traced here: 67.8 us
  Pallas kernels  32.3 us (47%)
  starting transfers between devices  28.8 us (42%)
  waiting for transfers between devices  5.7 us (8%)
  between operations  0.94 us (1%)
    all_to_all x1, starting transfers between devices, body(): lax.all_to_all(payload, ('oy', 'ox'), split_axis=0, concat_axis=0, tiled=...  11.5 us
    pallas_call x1, Pallas kernels, mix(): pl.pallas_call(mix_kernel, out_shape=out, in_specs=[VMEM] * 5, out_specs=...  9.84 us
    pallas_call x1, Pallas kernels, diffuse(): pl.pallas_call(functools.partial(diffuse_kernel, nl), out_shape=shaped(nt...  9.33 us
    pallas_call x1, Pallas kernels, remap(): pl.pallas_call(functools.partial(remap_kernel, n_ox), out_shape=shaped(de...  7.64 us
    ppermute x1, waiting for transfers between devices, body(): from_west = lax.ppermute(east, 'ox', eastward)  5.23 us
    ppermute x1, starting transfers between devices, body(): from_east = lax.ppermute(west, 'ox', westward)  4.14 us
    pallas_call x1, Pallas kernels, arrange(): pl.pallas_call(functools.partial(arrange_kernel, nt, nl), out_shape=out,...  4.02 us
    ppermute x1, starting transfers between devices, body(): flux_north = lax.ppermute(to_south, 'oy', southward)  3.93 us
  transfers between devices with their start and end apart: 7, of which 2 were waited for; matrix products, arithmetic and copies ran while one was open for 0% of the time, Pallas kernels for 23%

profile of v5, /device:TPU:1, one launch (start us, length us, event | category | flops | bytes accessed | tf_op | source)
XLA Modules:
  0.0 67.8 jit_solution(15032823966234501636)
XLA Ops:
  0.6 7.6 %remap.1 = f32[128,7,4,128]{3,2,1,0:T(4,128)} custom-call(s32[384]{0:T(512)} %source.1, s32[1,384]{1,0:T(1,128)} %bitcast.3, s32[384]{0:T(512)} %block_row.1, bf16[64,4,128]{2,1,0:T(4,128)(2,1)} %flux.1, bf16[384,128,128]{2,1,0:T(8,128)(2,1)} %weights.1), custom_call_target="tpu_custom_call" | custom-call | tf_op jit(solution)/shard_map/remap/pallas_call | solution.py:129
  8.3 11.5 %all-to-all-start = ((f32[128,7,4,128]{3,2,1,0:T(4,128)}), f32[128,7,4,128]{3,2,1,0:T(4,128)S(1)}, u32[]{:S(2)}, u32[]{:S(2)}) async-start(f32[128,7,4,128]{3,2,1,0:T(4,128)} %remap.1), calls=%async_computation | async-start | bytes 3670016 | tf_op jit(solution)/shard_map/all_to_all | solution.py:745
  19.8 0.0 copy-start.1
  19.8 9.8 %mix.1 = (f32[400,256,128]{2,1,0:T(8,128)}, f32[4,32,128]{2,1,0:T(8,128)}, f32[4,32,128]{2,1,0:T(8,128)}, f32[121,4,256]{2,1,0:T(4,128)}, f32[121,4,256]{2,1,0:T(4,128)}) custom-call(f32[4,20,32,256]{3,2,1,0:T(8,128)} %tracers.1, f32[20,32,256]{2,1,0:T(8,128)} %diffusivity.1, f32[20,32,256]{2,1,0:T(8,128)} %viscosity.1, s32[32,256]{1,0:T(8,128)} %mask.3, ...), custom_call_target="tpu_custom_call" | custom-call | tf_op jit(solution)/shard_map/mix/pallas_call | solution.py:312
  29.7 1.6 %collective-permute-start = (f32[4,32,128]{2,1,0:T(8,128)}, f32[4,32,128]{2,1,0:T(8,128)S(1)}, u32[]{:S(2)}, u32[]{:S(2)}) collective-permute-start(f32[4,32,128]{2,1,0:T(8,128)} %get-tuple-element.21), channel_id=1, source_target_pairs={{0,1},{1,2},{2,3},{3,4},{4,5},{5,6},{6,7},{7,8},{8,9},{9,10},{10,1... | collective-permute-start | bytes 196616 | tf_op jit(solution)/shard_map/ppermute | solution.py:755
  31.2 4.1 %collective-permute-start.1 = (f32[4,32,128]{2,1,0:T(8,128)}, f32[4,32,128]{2,1,0:T(8,128)S(1)}, u32[]{:S(2)}, u32[]{:S(2)}) collective-permute-start(f32[4,32,128]{2,1,0:T(8,128)} %get-tuple-element.22), channel_id=1, source_target_pairs={{1,0},{2,1},{3,2},{4,3},{5,4},{6,5},{7,6},{8,7},{9,8},{10,9},{11,1... | collective-permute-start | bytes 196616 | tf_op jit(solution)/shard_map/ppermute | solution.py:756
  35.4 3.6 %collective-permute-start.2 = (f32[121,4,256]{2,1,0:T(4,128)}, f32[121,4,256]{2,1,0:T(4,128)S(1)}, u32[]{:S(2)}, u32[]{:S(2)}) collective-permute-start(f32[121,4,256]{2,1,0:T(4,128)} %get-tuple-element.23), channel_id=1, source_target_pairs={{0,16},{16,32},{32,48},{48,64},{64,80},{80,96},{96,112},{1,17},{17... | collective-permute-start | bytes 1486856 | tf_op jit(solution)/shard_map/ppermute | solution.py:757
  39.0 1.9 %collective-permute-start.3 = (f32[121,4,256]{2,1,0:T(4,128)}, f32[121,4,256]{2,1,0:T(4,128)S(1)}, u32[]{:S(2)}, u32[]{:S(2)}) collective-permute-start(f32[121,4,256]{2,1,0:T(4,128)} %get-tuple-element.24), channel_id=1, source_target_pairs={{16,0},{32,16},{48,32},{64,48},{80,64},{96,80},{112,96},{17,1},{33... | collective-permute-start | bytes 1486856 | tf_op jit(solution)/shard_map/ppermute | solution.py:758
  40.9 5.2 %collective-permute-done.west_in = f32[4,32,128]{2,1,0:T(8,128)S(1)} collective-permute-done((f32[4,32,128]{2,1,0:T(8,128)}, f32[4,32,128]{2,1,0:T(8,128)S(1)}, u32[]{:S(2)}, u32[]{:S(2)}) %collective-permute-start) | collective-permute-done | bytes 65568 | tf_op jit(solution)/shard_map/ppermute | solution.py:755
  46.2 0.0 collective-permute-done.1.east_in
  46.2 0.5 all-to-all-done
  46.7 0.0 copy-done.1
  46.7 1.5 %collect.1 = (f32[4,32,256]{2,1,0:T(8,128)}, f32[4,32,128]{2,1,0:T(8,128)S(1)}, f32[20,4,128]{2,1,0:T(4,128)S(1)}, f32[20,4,128]{2,1,0:T(4,128)S(1)}) custom-call(f32[3584,128]{1,0:T(8,128)S(1)} %bitcast.2, s32[32,256]{1,0:T(8,128)S(1)} %copy-done.1, f32[8,8,128]{2,1,0:T(8,128)S(1)} %pad_maximum_fusion.corners), custom_call_target="tpu_custom_call" | custom-call | tf_op jit(solution)/shard_map/collect/pallas_call | solution.py:502
  48.1 3.9 %collective-permute-start.4 = (f32[20,4,128]{2,1,0:T(4,128)S(1)}, f32[20,4,128]{2,1,0:T(4,128)S(1)}, u32[]{:S(2)}, u32[]{:S(2)}) collective-permute-start(f32[20,4,128]{2,1,0:T(4,128)S(1)} %get-tuple-element.36), channel_id=1, source_target_pairs={{0,16},{16,32},{32,48},{48,64},{64,80},{80,96},{96,112},{1,17},{17... | collective-permute-start | bytes 122888 | tf_op jit(solution)/shard_map/ppermute | solution.py:763
  52.1 2.1 %collective-permute-start.5 = (f32[20,4,128]{2,1,0:T(4,128)S(1)}, f32[20,4,128]{2,1,0:T(4,128)S(1)}, u32[]{:S(2)}, u32[]{:S(2)}) collective-permute-start(f32[20,4,128]{2,1,0:T(4,128)S(1)} %get-tuple-element.37), channel_id=1, source_target_pairs={{16,0},{32,16},{48,32},{64,48},{80,64},{96,80},{112,96},{17,1},{33... | collective-permute-start | bytes 122888 | tf_op jit(solution)/shard_map/ppermute | solution.py:764
  54.2 0.0 collective-permute-done.2.north_in
  54.2 0.0 collective-permute-done.3.south_in
  54.2 0.0 copy-start
  54.2 4.0 %arrange.1 = (f32[3,256,128]{2,1,0:T(8,128)S(1)}, f32[20,256,128]{2,1,0:T(8,128)S(1)}, f32[3,768,128]{2,1,0:T(8,128)S(1)}, f32[3,768,128]{2,1,0:T(8,128)S(1)}, f...) custom-call(f32[400,256,128]{2,1,0:T(8,128)} %get-tuple-element.20.s, ...), custom_call_target="tpu_custom_call" | custom-call | tf_op jit(solution)/shard_map/arrange/pallas_call | solution.py:422
  58.2 0.0 collective-permute-done.4.north
  58.3 0.0 collective-permute-done.5.south
  58.3 0.0 copy-done
  58.3 9.3 %diffuse.1 = f32[4,20,32,256]{3,2,1,0:T(8,128)} custom-call(f32[3,256,128]{2,1,0:T(8,128)S(1)} %get-tuple-element.25.mids, f32[20,256,128]{2,1,0:T(8,128)S(1)} %get-tuple-element.26.sides, f32[3,768,128]{2,1,0:T(8,128)S(1)} %get-tuple-element.27.responses, f32[3,768,128]{2,1,0:T(8,128)S(1)} %get-tuple-element.28.weights, ...), custom_call_target="tpu_custom_call" | custom-call | tf_op jit(solution)/shard_map/diffuse/pallas_call | solution.py:704
  (4 shorter events, 0.0 us)
Async XLA Ops:
  8.3 38.4 %all-to-all-start = ((f32[128,7,4,128]{3,2,1,0:T(4,128)}), f32[128,7,4,128]{3,2,1,0:T(4,128)S(1)}, u32[]{:S(2)}, u32[]{:S(2)}) async-start(f32[128,7,4,128]{3,2,1,0:T(4,128)} %remap.1), calls=%async_computation | async-start | bytes 3670016 | tf_op jit(solution)/shard_map/all_to_all | solution.py:745
  19.8 26.9 %copy-start.1 = (s32[32,256]{1,0:T(8,128)S(1)}, s32[32,256]{1,0:T(8,128)}, u32[]{:S(2)}) copy-start(s32[32,256]{1,0:T(8,128)} %mask.3) | copy-start | bytes 98308
  29.7 16.5 %collective-permute-start = (f32[4,32,128]{2,1,0:T(8,128)}, f32[4,32,128]{2,1,0:T(8,128)S(1)}, u32[]{:S(2)}, u32[]{:S(2)}) collective-permute-start(f32[4,32,128]{2,1,0:T(8,128)} %get-tuple-element.21), channel_id=1, source_target_pairs={{0,1},{1,2},{2,3},{3,4},{4,5},{5,6},{6,7},{7,8},{8,9},{9,10},{10,1... | collective-permute-start | bytes 196616 | tf_op jit(solution)/shard_map/ppermute | solution.py:755
  31.2 14.9 %collective-permute-start.1 = (f32[4,32,128]{2,1,0:T(8,128)}, f32[4,32,128]{2,1,0:T(8,128)S(1)}, u32[]{:S(2)}, u32[]{:S(2)}) collective-permute-start(f32[4,32,128]{2,1,0:T(8,128)} %get-tuple-element.22), channel_id=1, source_target_pairs={{1,0},{2,1},{3,2},{4,3},{5,4},{6,5},{7,6},{8,7},{9,8},{10,9},{11,1... | collective-permute-start | bytes 196616 | tf_op jit(solution)/shard_map/ppermute | solution.py:756
  35.4 18.8 %collective-permute-start.2 = (f32[121,4,256]{2,1,0:T(4,128)}, f32[121,4,256]{2,1,0:T(4,128)S(1)}, u32[]{:S(2)}, u32[]{:S(2)}) collective-permute-start(f32[121,4,256]{2,1,0:T(4,128)} %get-tuple-element.23), channel_id=1, source_target_pairs={{0,16},{16,32},{32,48},{48,64},{64,80},{80,96},{96,112},{1,17},{17... | collective-permute-start | bytes 1486856 | tf_op jit(solution)/shard_map/ppermute | solution.py:757
  39.0 15.2 %collective-permute-start.3 = (f32[121,4,256]{2,1,0:T(4,128)}, f32[121,4,256]{2,1,0:T(4,128)S(1)}, u32[]{:S(2)}, u32[]{:S(2)}) collective-permute-start(f32[121,4,256]{2,1,0:T(4,128)} %get-tuple-element.24), channel_id=1, source_target_pairs={{16,0},{32,16},{48,32},{64,48},{80,64},{96,80},{112,96},{17,1},{33... | collective-permute-start | bytes 1486856 | tf_op jit(solution)/shard_map/ppermute | solution.py:758
  48.1 10.1 %collective-permute-start.4 = (f32[20,4,128]{2,1,0:T(4,128)S(1)}, f32[20,4,128]{2,1,0:T(4,128)S(1)}, u32[]{:S(2)}, u32[]{:S(2)}) collective-permute-start(f32[20,4,128]{2,1,0:T(4,128)S(1)} %get-tuple-element.36), channel_id=1, source_target_pairs={{0,16},{16,32},{32,48},{48,64},{64,80},{80,96},{96,112},{1,17},{17... | collective-permute-start | bytes 122888 | tf_op jit(solution)/shard_map/ppermute | solution.py:763
  52.1 6.2 %collective-permute-start.5 = (f32[20,4,128]{2,1,0:T(4,128)S(1)}, f32[20,4,128]{2,1,0:T(4,128)S(1)}, u32[]{:S(2)}, u32[]{:S(2)}) collective-permute-start(f32[20,4,128]{2,1,0:T(4,128)S(1)} %get-tuple-element.37), channel_id=1, source_target_pairs={{16,0},{32,16},{48,32},{64,48},{80,64},{96,80},{112,96},{17,1},{33... | collective-permute-start | bytes 122888 | tf_op jit(solution)/shard_map/ppermute | solution.py:764
  54.2 4.1 %copy-start = (f32[4,32,256]{2,1,0:T(8,128)S(1)}, f32[4,32,256]{2,1,0:T(8,128)}, u32[]{:S(2)}) copy-start(f32[4,32,256]{2,1,0:T(8,128)} %get-tuple-element.19.main) | copy-start | bytes 393220
